TPU v7x, 32 devices: a whole 2x2x4 slice. The times are simulated.
32 devices in a mesh: seq: 16 (over z, y, x), wshard: 2 (over core).
Axes of the slice: x: 2, y: 2, z: 4, core: 2. Of those that a mesh axis runs over, the one named last changes fastest.
Arguments:
- inputs: bfloat16 [2, 4096, 1792], P('wshard', 'seq'), may hold values from -6 to 6
- starts: int32 [2, 16], P('wshard', 'seq'), may hold values from 0 to 1, as said below
- attn_gain: bfloat16 [1792], P(('seq', 'wshard')), may hold values from 0.5 to 1.5
- query_weight: bfloat16 [1792, 1792], P(('seq', 'wshard')), may hold values from -0.125 to 0.125
- key_weight: bfloat16 [1792, 1792], P(('seq', 'wshard')), may hold values from -0.125 to 0.125
- value_weight: bfloat16 [1792, 1792], P(('seq', 'wshard')), may hold values from -0.125 to 0.125
- out_weight: bfloat16 [1792, 1792], P(('seq', 'wshard')), may hold values from -1 to 1
- ffn_gain: bfloat16 [1792], P(('seq', 'wshard')), may hold values from 0.5 to 1.5
- gate_weight: bfloat16 [1792, 4864], P(('seq', 'wshard')), may hold values from -0.125 to 0.125
- up_weight: bfloat16 [1792, 4864], P(('seq', 'wshard')), may hold values from -0.125 to 0.125
- down_weight: bfloat16 [4864, 1792], P(('seq', 'wshard')), may hold values from -0.078125 to 0.078125
- cotangent: bfloat16 [2, 4096, 1792], P('wshard', 'seq'), may hold values from -6 to 6
Outputs:
- layer_out: bfloat16 [2, 4096, 1792], P('wshard', 'seq')
- input_grad: float32 [2, 4096, 1792], P('wshard', 'seq')
- attn_gain_grad: float32 [1792], P(('seq', 'wshard'))
- query_grad: float32 [1792, 1792], P(('seq', 'wshard'))
- key_grad: float32 [1792, 1792], P(('seq', 'wshard'))
- value_grad: float32 [1792, 1792], P(('seq', 'wshard'))
- output_grad: float32 [1792, 1792], P(('seq', 'wshard'))
- ffn_gain_grad: float32 [1792], P(('seq', 'wshard'))
- gate_grad: float32 [1792, 4864], P(('seq', 'wshard'))
- up_grad: float32 [1792, 4864], P(('seq', 'wshard'))
- down_grad: float32 [4864, 1792], P(('seq', 'wshard'))
Inputs may be any that keep to these rules, and one draw needn't show every extreme that they name: starts[w, 0] is 1 in every stream; other ones stand only at block numbers that are multiples of 4; in one stream, drawn from the seed, starts[w, 0] is the only 1, so one sequence covers all its blocks.
All inputs are finite; a program needn't handle non-finite values.
Results may differ from a plain program's by a relative error of at most 0.014.
Values may be sent and summed in bfloat16 or wider, within the bound.
No kernel may reach another device: no remote copies, remote signals or barrier semaphores. Data moves between devices by JAX's collectives and lax.ppermute only.
A program may use at most 576 MiB of HBM per device.

v0:
```python
import jax
import jax.numpy as jnp
from jax import lax
from jax.sharding import PartitionSpec as P

H = 16
HD = 112
WINDOW = 64


EPS = 1e-06
MASKED = -1e30


def passed_along(block, axis, distance):
    devices = range(lax.axis_size(axis))
    route = [(i - distance, i) for i in devices if i - distance in devices]
    return lax.ppermute(block, axis, route)


def normalize(values):
    factor = lax.rsqrt(jnp.mean(values * values, axis=-1, keepdims=True) + EPS)
    return (values * factor, factor)


def norm_back(grad_normed, normed_rows, factor):
    return factor * (
        grad_normed - normed_rows * jnp.mean(grad_normed * normed_rows, axis=-1, keepdims=True)
    )


def windows(before, current):
    joined = jnp.concatenate(
        [before, current, jnp.zeros((1, current.shape[1]), current.dtype)], axis=0
    )
    blocks = joined.reshape(-1, WINDOW, H, HD)
    return jnp.concatenate([blocks[:-1], blocks[1:]], axis=1)


def unwindow(grads, rows):
    first = grads[:, :WINDOW]
    second = grads[:, WINDOW:]
    zero_block = jnp.zeros_like(first[:1])
    merged = jnp.concatenate([first, zero_block], axis=0) + jnp.concatenate(
        [zero_block, second], axis=0
    )
    flat = merged.reshape(-1, H * HD)
    return (flat[: WINDOW - 1], flat[WINDOW - 1 : WINDOW - 1 + rows])


def dot_left(rows_mat, other):
    return lax.dot_general(
        rows_mat, other, (((0,), (0,)), ((), ())), preferred_element_type=jnp.float32
    )


def dot_right(left, weight):
    return lax.dot_general(
        left, weight, (((1,), (1,)), ((), ())), preferred_element_type=jnp.float32
    )


def gain_block(gain_local):
    piece = gain_local[:, None]
    return jnp.pad(piece, ((0, 0), (0, 127)))


def body(
    inputs,
    starts,
    attn_gain,
    query_weight,
    key_weight,
    value_weight,
    out_weight,
    ffn_gain,
    gate_weight,
    up_weight,
    down_weight,
    cotangent,
):
    stream = inputs[0].astype(jnp.float32)
    rows = stream.shape[0]
    count = rows // WINDOW
    rim = WINDOW - 1
    factor_attn = HD ** (-0.5)
    begins = starts[0, 0] == 1
    width = stream.shape[1]
    hidden_units = gate_weight.shape[1]
    full_query, full_key, full_value, full_out, gain_attn = (
        lax.all_gather(query_weight, ("seq", "wshard"), axis=0, tiled=True),
        lax.all_gather(key_weight, ("seq", "wshard"), axis=0, tiled=True),
        lax.all_gather(value_weight, ("seq", "wshard"), axis=0, tiled=True),
        lax.all_gather(out_weight, ("seq", "wshard"), axis=0, tiled=True),
        lax.all_gather(attn_gain, ("seq", "wshard"), axis=0, tiled=True),
    )
    normed1, rscale1 = normalize(stream)
    hidden1 = (normed1 * gain_attn).astype(jnp.bfloat16)
    query = jnp.dot(hidden1, full_query, preferred_element_type=jnp.float32).astype(jnp.bfloat16)
    keys = jnp.dot(hidden1, full_key, preferred_element_type=jnp.float32).astype(jnp.bfloat16)
    values = jnp.dot(hidden1, full_value, preferred_element_type=jnp.float32).astype(jnp.bfloat16)
    prev_keys, prev_values = passed_along((keys[rows - rim :], values[rows - rim :]), "seq", 1)
    key_blocks = windows(prev_keys, keys)
    value_blocks = windows(prev_values, values)
    query_blocks = query.reshape(count, WINDOW, H, HD)
    rowpos = jnp.arange(WINDOW)[:, None]
    colpos = jnp.arange(2 * WINDOW)[None, :]
    band = (colpos >= rowpos) & (colpos <= rowpos + rim)
    blockpos = jnp.arange(count)[:, None, None, None]
    keypos = jnp.arange(2 * WINDOW)[None, None, None, :]
    cut = (blockpos == 0) & (keypos < rim) & begins
    valid = band[None, None] & jnp.logical_not(cut)

    def scores_of():
        raw = jnp.einsum(
            "bqhd,bkhd->bhqk", query_blocks, key_blocks, preferred_element_type=jnp.float32
        )
        return jnp.where(valid, raw * factor_attn, MASKED)

    scores = scores_of()
    peak = jnp.max(scores, axis=-1, keepdims=True)
    powers = jnp.exp(scores - peak)
    totals = jnp.sum(powers, axis=-1, keepdims=True)
    shares = powers / totals
    logsum = peak + jnp.log(totals)
    mixed = (
        jnp.einsum(
            "bhqk,bkhd->bqhd",
            shares.astype(jnp.bfloat16),
            value_blocks,
            preferred_element_type=jnp.float32,
        )
        .reshape(rows, H * HD)
        .astype(jnp.bfloat16)
    )
    middle = stream + jnp.dot(mixed, full_out, preferred_element_type=jnp.float32)
    full_gate, full_up, full_down, gain_ffn = (
        lax.all_gather(gate_weight, ("seq", "wshard"), axis=0, tiled=True),
        lax.all_gather(up_weight, ("seq", "wshard"), axis=0, tiled=True),
        lax.all_gather(down_weight, ("seq", "wshard"), axis=0, tiled=True),
        lax.all_gather(ffn_gain, ("seq", "wshard"), axis=0, tiled=True),
    )
    normed2, rscale2 = normalize(middle)
    hidden2 = (normed2 * gain_ffn).astype(jnp.bfloat16)
    gate = jnp.dot(hidden2, full_gate, preferred_element_type=jnp.float32)
    upper = jnp.dot(hidden2, full_up, preferred_element_type=jnp.float32)
    sigma = jax.nn.sigmoid(gate)
    activ = gate * sigma
    inner = (activ * upper).astype(jnp.bfloat16)
    layer_out = (middle + jnp.dot(inner, full_down, preferred_element_type=jnp.float32)).astype(
        jnp.bfloat16
    )
    grad_top = cotangent[0]
    grad_inner = dot_right(grad_top, full_down)
    grad_upper = (grad_inner * activ).astype(jnp.bfloat16)
    grad_gate = (grad_inner * upper * sigma * (1.0 + gate * (1.0 - sigma))).astype(jnp.bfloat16)
    grad_hidden2 = dot_right(grad_gate, full_gate) + dot_right(grad_upper, full_up)
    ffn_gain_local = jnp.sum(grad_hidden2 * normed2, axis=0)
    grad_middle = grad_top.astype(jnp.float32) + norm_back(
        grad_hidden2 * gain_ffn, normed2, rscale2
    )
    picked = hidden2
    ffn_sums = lax.psum_scatter(
        jnp.concatenate(
            [dot_left(picked, grad_gate), dot_left(picked, grad_upper), gain_block(ffn_gain_local)],
            axis=1,
        ),
        ("seq", "wshard"),
        scatter_dimension=0,
        tiled=True,
    )
    down_grad = lax.psum_scatter(
        dot_left(inner, grad_top), ("seq", "wshard"), scatter_dimension=0, tiled=True
    )
    gate_grad = ffn_sums[:, :hidden_units]
    up_grad = ffn_sums[:, hidden_units : 2 * hidden_units]
    ffn_gain_grad = ffn_sums[:, 2 * hidden_units]
    grad_branch = grad_middle.astype(jnp.bfloat16)
    grad_mixed = dot_right(grad_branch, full_out).astype(jnp.bfloat16)
    grad_blocks = grad_mixed.reshape(count, WINDOW, H, HD)
    shares = jnp.exp(scores_of() - logsum)
    grad_shares = jnp.einsum(
        "bqhd,bkhd->bhqk", grad_blocks, value_blocks, preferred_element_type=jnp.float32
    )
    grad_vblocks = jnp.einsum(
        "bhqk,bqhd->bkhd",
        shares.astype(jnp.bfloat16),
        grad_blocks,
        preferred_element_type=jnp.float32,
    )
    grad_raw = (
        shares * (grad_shares - jnp.sum(shares * grad_shares, axis=-1, keepdims=True)) * factor_attn
    ).astype(jnp.bfloat16)
    grad_qblocks = jnp.einsum(
        "bhqk,bkhd->bqhd", grad_raw, key_blocks, preferred_element_type=jnp.float32
    )
    grad_kblocks = jnp.einsum(
        "bhqk,bqhd->bkhd", grad_raw, query_blocks, preferred_element_type=jnp.float32
    )
    key_rim, key_here = unwindow(grad_kblocks, rows)
    value_rim, value_here = unwindow(grad_vblocks, rows)
    back_keys, back_values = (
        passed_along(key_rim.astype(jnp.bfloat16), "seq", -1).astype(key_rim.dtype),
        passed_along(value_rim.astype(jnp.bfloat16), "seq", -1).astype(value_rim.dtype),
    )
    key_total = jnp.concatenate(
        [key_here[: rows - rim], key_here[rows - rim :] + back_keys], axis=0
    )
    value_total = jnp.concatenate(
        [value_here[: rows - rim], value_here[rows - rim :] + back_values], axis=0
    )
    grad_query = grad_qblocks.reshape(rows, H * HD).astype(jnp.bfloat16)
    grad_keys = key_total.astype(jnp.bfloat16)
    grad_values = value_total.astype(jnp.bfloat16)
    grad_hidden1 = (
        dot_right(grad_query, full_query)
        + dot_right(grad_keys, full_key)
        + dot_right(grad_values, full_value)
    )
    attn_gain_local = jnp.sum(grad_hidden1 * normed1, axis=0)
    input_grad = grad_middle + norm_back(grad_hidden1 * gain_attn, normed1, rscale1)
    picked = hidden1
    attn_sums = lax.psum_scatter(
        jnp.concatenate(
            [
                dot_left(picked, grad_query),
                dot_left(picked, grad_keys),
                dot_left(picked, grad_values),
                dot_left(mixed, grad_branch),
                gain_block(attn_gain_local),
            ],
            axis=1,
        ),
        ("seq", "wshard"),
        scatter_dimension=0,
        tiled=True,
    )
    query_grad = attn_sums[:, :width]
    key_grad = attn_sums[:, width : 2 * width]
    value_grad = attn_sums[:, 2 * width : 3 * width]
    output_grad = attn_sums[:, 3 * width : 4 * width]
    attn_gain_grad = attn_sums[:, 4 * width]
    return (
        layer_out[None],
        input_grad[None],
        attn_gain_grad,
        query_grad,
        key_grad,
        value_grad,
        output_grad,
        ffn_gain_grad,
        gate_grad,
        up_grad,
        down_grad,
    )


def solution(mesh):
    in_specs = (
        P("wshard", "seq", None),
        P("wshard", "seq"),
        P(("seq", "wshard")),
        P(("seq", "wshard"), None),
        P(("seq", "wshard"), None),
        P(("seq", "wshard"), None),
        P(("seq", "wshard"), None),
        P(("seq", "wshard")),
        P(("seq", "wshard"), None),
        P(("seq", "wshard"), None),
        P(("seq", "wshard"), None),
        P("wshard", "seq", None),
    )
    out_specs = (
        P("wshard", "seq", None),
        P("wshard", "seq", None),
        P(("seq", "wshard")),
        P(("seq", "wshard"), None),
        P(("seq", "wshard"), None),
        P(("seq", "wshard"), None),
        P(("seq", "wshard"), None),
        P(("seq", "wshard")),
        P(("seq", "wshard"), None),
        P(("seq", "wshard"), None),
        P(("seq", "wshard"), None),
    )
    return jax.shard_map(body, mesh=mesh, in_specs=in_specs, out_specs=out_specs, check_vma=False)
```

profile of v0, /device:TPU:26, one launch (start us, length us, event | category | flops | bytes accessed | tf_op | source)
XLA Modules:
  0.0 3034.3 jit_solution(7285066947707154276)
XLA Ops:
  13.1 40.4 %all-reduce.13 = (bf16[1792]{0:T(1024)(128)(2,1)S(1)}, bf16[1792]{0:T(1024)(128)(2,1)S(1)}) all-reduce(bf16[1792]{0:T(1024)(128)(2,1)S(1)} %dynamic-update-slice, bf16[1792]{0:T(1024)(128)(2,1)S(1)} %dynamic-update-slice.1), channel_id=1, replica_groups=mesh['seq'=16,'wshard'=2] {'seq','wshard'}, use_global_device_ids=true, to_apply=%add.8 | all-reduce | flops 3584 | bytes 14336
  54.0 26.4 all-gather.12.cloned.1.call-done
  80.4 4.7 convolution_convert_fusion.1
  85.8 3.4 collective-permute-start.1
  89.3 63.6 %all-gather.8.cloned.1.call-done = bf16[1792,1792]{1,0:T(8,128)(2,1)} async-done(((bf16[56,1792]{1,0:T(8,128)(2,1)}), bf16[1792,1792]{1,0:T(8,128)(2,1)}) %all-gather.8.cloned.1.call-update) | async-done | bytes 6422544 | tf_op jit(solution)/shard_map/all_gather | solution.py:93
  152.9 4.7 convolution_convert_fusion.3
  159.3 3.4 collective-permute-start
  162.7 62.8 %all-gather.10.cloned.1.call-done = bf16[1792,1792]{1,0:T(8,128)(2,1)} async-done(((bf16[56,1792]{1,0:T(8,128)(2,1)}), bf16[1792,1792]{1,0:T(8,128)(2,1)}) %all-gather.10.cloned.1.call-update) | async-done | bytes 6422544 | tf_op jit(solution)/shard_map/all_gather | solution.py:91
  225.5 4.7 convolution_convert_fusion.2
  234.1 3.3 slice.105
  239.4 3.0 pad_maximum_fusion.3
  255.7 4.2 fusion.86
  268.6 28.2 all-gather.14.cloned.1.call-done
  296.7 5.0 multiply_reduce_fusion.3
  304.2 111.4 %all-gather.18.cloned.1.call-done = bf16[1792,4864]{1,0:T(8,128)(2,1)} async-done(((bf16[56,4864]{1,0:T(8,128)(2,1)}), bf16[1792,4864]{1,0:T(8,128)(2,1)}) %all-gather.18.cloned.1.call-update) | async-done | bytes 17432592 | tf_op jit(solution)/shard_map/all_gather | solution.py:139
  415.6 13.2 fusion.88
  428.8 105.8 %all-gather.16.cloned.1.call-done = bf16[1792,4864]{1,0:T(8,128)(2,1)} async-done(((bf16[56,4864]{1,0:T(8,128)(2,1)}), bf16[1792,4864]{1,0:T(8,128)(2,1)}) %all-gather.16.cloned.1.call-update) | async-done | bytes 17432592 | tf_op jit(solution)/shard_map/all_gather | solution.py:138
  534.6 13.2 fusion.87
  547.8 105.9 %all-gather.20.cloned.1.call-done = bf16[4864,1792]{1,0:T(8,128)(2,1)} async-done(((bf16[152,1792]{1,0:T(8,128)(2,1)}), bf16[4864,1792]{1,0:T(8,128)(2,1)}) %all-gather.20.cloned.1.call-update) | async-done | bytes 17432592 | tf_op jit(solution)/shard_map/all_gather | solution.py:140
  653.7 14.5 multiply_convert_fusion
  668.2 12.7 fusion.89
  680.8 13.7 multiply_reduce_fusion.1
  698.5 5.6 convolution_convert_fusion
  704.2 4.0 reshape.187
  708.1 4.9 fusion.48
  713.1 27.3 fusion.32
  740.4 28.1 convolution_bitcast_fusion.1
  775.3 5.1 copy.63
  785.6 13.6 fusion.92
  799.3 13.7 fusion.91
  821.3 4.4 fusion.85
  828.6 5.5 copy.61
  834.1 3.8 reshape.188
  839.8 4.5 collective-permute-start.2
  844.3 6.6 convolution_dynamic-update-slice_fusion.3
  850.9 45.3 %select_maximum_fusion = f32[1792,9856]{1,0:T(8,128)} fusion(f32[1792,1]{1,0:T(8,128)S(1)} %copy-done.9, f32[1792,4864]{1,0:T(8,128)} %fusion.92, f32[1792,4864]{1,0:T(8,128)} %fusion.91), kind=kLoop, calls=%fused_computation.1 | loop fusion | flops 70647808 | bytes 140385280 | tf_op jit(solution)/shard_map/concatenate | solution.py:164
  896.2 4.8 fusion.90
  902.6 4.8 convolution_add_fusion.1
  907.4 3.2 fusion.20
  910.6 6.5 convolution_dynamic-update-slice_fusion.2
  917.2 6.5 convolution_dynamic-update-slice_fusion.1
  923.7 6.4 convolution_dynamic-update-slice_fusion
  931.3 19.0 fusion.54
  950.4 13.4 fusion.3
  965.5 1686.3 %all-reduce.16.cloned.1.call-done = (f32[1792,7296]{0,1:T(8,128)}, f32[1792,9856]{1,0:T(8,128)}) async-done(((f32[1792,7296]{0,1:T(8,128)}, f32[1792,9856]{1,0:T(8,128)}), (f32[1792,7296]{0,1:T(8,128)}, f32[1792,9856]{1,0:T(8,128)})) %all-reduce.16.cloned.1.call-update) | async-done | bytes 122945552
  2651.8 5.1 fusion.83
  2665.0 3.3 fusion.82
  2668.2 359.4 %reduce-scatter.3.cloned.1.call-done = f32[152,1792]{1,0:T(8,128)} async-done(((f32[4864,1792]{1,0:T(8,128)}), f32[152,1792]{1,0:T(8,128)}) %reduce-scatter.3.cloned.1.call-update) | async-done | bytes 1089552 | tf_op jit(solution)/shard_map/reduce_scatter | solution.py:172
  (124 shorter events, 79.8 us)
Async XLA Ops:
  7.2 5.4 copy-start.16
  7.2 5.7 copy-start.17
  7.2 46.3 %copy-start = (bf16[1,256,1792]{2,1,0:T(8,128)(2,1)S(1)}, bf16[1,256,1792]{2,1,0:T(8,128)(2,1)}, u32[]{:S(2)}) copy-start(bf16[1,256,1792]{2,1,0:T(8,128)(2,1)} %param.12) | copy-start | bytes 2752516
  7.2 73.2 %all-gather.12.cloned.1.call-start = ((), (), s32[]{:S(2)}) async-start(), calls=%async_computation.3 | async-start | bytes 6623232 | tf_op jit(solution)/shard_map/all_gather | solution.py:92
  7.9 145.0 %all-gather.8.cloned.1.call-start = ((), (), s32[]{:S(2)}) async-start(), calls=%async_computation.1 | async-start | bytes 6623232 | tf_op jit(solution)/shard_map/all_gather | solution.py:93
  8.7 216.8 %all-gather.10.cloned.1.call-start = ((), (), s32[]{:S(2)}) async-start(), calls=%async_computation.2 | async-start | bytes 6623232 | tf_op jit(solution)/shard_map/all_gather | solution.py:91
  9.4 287.3 %all-gather.14.cloned.1.call-start = ((), (), s32[]{:S(2)}) async-start(), calls=%async_computation.4 | async-start | bytes 6623232 | tf_op jit(solution)/shard_map/all_gather | solution.py:94
  10.0 405.6 %all-gather.18.cloned.1.call-start = ((), (), s32[]{:S(2)}) async-start(), calls=%async_computation.6 | async-start | bytes 17977344 | tf_op jit(solution)/shard_map/all_gather | solution.py:139
  10.6 524.0 %all-gather.16.cloned.1.call-start = ((), (), s32[]{:S(2)}) async-start(), calls=%async_computation.5 | async-start | bytes 17977344 | tf_op jit(solution)/shard_map/all_gather | solution.py:138
  11.2 642.5 %all-gather.20.cloned.1.call-start = ((), (), s32[]{:S(2)}) async-start(), calls=%async_computation.7 | async-start | bytes 17977344 | tf_op jit(solution)/shard_map/all_gather | solution.py:140
  11.9 2639.9 %all-reduce.16.cloned.1.call-start = ((), (), s32[]{:S(2)}) async-start(), calls=%async_computation.9 | async-start | bytes 245891072
  85.8 147.1 %collective-permute-start.1 = (bf16[63,1792]{1,0:T(8,128)(2,1)}, bf16[63,1792]{1,0:T(8,128)(2,1)S(1)}, u32[]{:S(2)}, u32[]{:S(2)}) collective-permute-start(bf16[63,1792]{1,0:T(8,128)(2,1)} %slice.127), channel_id=1, source_target_pairs={{0,2},{2,4},{4,6},{6,8},{8,10},{10,12},{12,14},{14,16},{16,18},{18... | collective-permute-start | bytes 677384 | tf_op jit(solution)/shard_map/ppermute | solution.py:18
  157.6 0.9 copy-start.14
  159.3 80.1 %collective-permute-start = (bf16[63,1792]{1,0:T(8,128)(2,1)}, bf16[63,1792]{1,0:T(8,128)(2,1)S(1)}, u32[]{:S(2)}, u32[]{:S(2)}) collective-permute-start(bf16[63,1792]{1,0:T(8,128)(2,1)} %slice.126), channel_id=1, source_target_pairs={{0,2},{2,4},{4,6},{6,8},{8,10},{10,12},{12,14},{14,16},{16,18},{18... | collective-permute-start | bytes 677384 | tf_op jit(solution)/shard_map/ppermute | solution.py:18
  255.7 5.5 copy-start.6
  259.9 1.5 copy-start.5
  301.8 1.2 copy-start.4
  697.3 1.3 copy-start.1
  783.4 1.9 copy-start.3
  783.4 2.3 copy-start.12
  785.6 13.6 copy-start.11
  799.3 13.7 copy-start.15
  818.8 82.4 %collective-permute-start.3 = (bf16[63,1792]{1,0:T(8,128)(2,1)}, bf16[63,1792]{1,0:T(8,128)(2,1)S(1)}, u32[]{:S(2)}, u32[]{:S(2)}) collective-permute-start(bf16[63,1792]{1,0:T(8,128)(2,1)} %slice.137), channel_id=1, source_target_pairs={{2,0},{4,2},{6,4},{8,6},{10,8},{12,10},{14,12},{16,14},{18,16},{20... | collective-permute-start | bytes 677384 | tf_op jit(solution)/shard_map/ppermute | solution.py:18
  837.9 6.4 copy-start.8
  839.8 11.1 copy-start.9
  839.8 61.5 %collective-permute-start.2 = (bf16[63,1792]{1,0:T(8,128)(2,1)S(1)}, bf16[63,1792]{1,0:T(8,128)(2,1)S(1)}, u32[]{:S(2)}, u32[]{:S(2)}) collective-permute-start(bf16[63,1792]{1,0:T(8,128)(2,1)S(1)} %slice.132), channel_id=1, source_target_pairs={{2,0},{4,2},{6,4},{8,6},{10,8},{12,10},{14,12},{16,14},{18,16},{20... | collective-permute-start | bytes 677384 | tf_op jit(solution)/shard_map/ppermute | solution.py:18
  896.2 11.1 slice-start
  901.3 6.1 slice-start.1
  902.5 4.8 copy-start.10
  917.2 6.5 copy-start.2
  917.2 6.5 copy-start.7
  931.1 2096.5 %reduce-scatter.3.cloned.1.call-start = ((), (), s32[]{:S(2)}) async-start(), calls=%async_computation.8 | async-start | bytes 35954688 | tf_op jit(solution)/shard_map/reduce_scatter | solution.py:172
  950.4 13.4 copy-start.13
Sparse Core Ops, SparseCore 0:
  10.9 69.4 all-gather.11
  83.3 69.5 all-gather.7
  155.8 69.6 all-gather.9
  228.2 68.5 all-gather.13
  299.4 116.1 all-gather.17
  418.3 116.1 all-gather.15
  537.4 116.2 all-gather.19
  931.2 1720.5 all-reduce.15
  2654.8 372.7 reduce-scatter.2
where the time goes:
time: 3040 us; the launch traced here: 3030 us
  waiting for transfers between devices  2550 us (84%)
  matrix products  261 us (9%)
  local copies, waits for them, and re-layouts  84.1 us (3%)
  other arithmetic  65.7 us (2%)
  blocking collectives  40.4 us (1%)
    unnamed x10, waiting for transfers between devices  1690 us
    reduce_scatter x1, waiting for transfers between devices, body(): lax.psum_scatter(dot_left(inner, grad_top), ('seq', 'wshard'), scatter_di...  359 us
    all_gather x1, waiting for transfers between devices, body(): lax.all_gather(up_weight, ('seq', 'wshard'), axis=0, tiled=True)  111 us
    all_gather x1, waiting for transfers between devices, body(): lax.all_gather(down_weight, ('seq', 'wshard'), axis=0, tiled=True)  106 us
    all_gather x1, waiting for transfers between devices, body(): lax.all_gather(gate_weight, ('seq', 'wshard'), axis=0, tiled=True)  106 us
    dot_general x7, matrix products, dot_left(): lax.dot_general(rows_mat, other, (((0,), (0,)), ((), ())), preferred_elem...  72.4 us
    all_gather x1, waiting for transfers between devices, body(): lax.all_gather(value_weight, ('seq', 'wshard'), axis=0, tiled=True)  63.6 us
    all_gather x1, waiting for transfers between devices, body(): lax.all_gather(query_weight, ('seq', 'wshard'), axis=0, tiled=True)  62.8 us
  transfers between devices with their start and end apart: 13, of which 9 were waited for; matrix products, arithmetic and copies ran while one was open for 7% of the time, Pallas kernels for 0%

commit v1 on v0

v1 whole, which is shorter than its diff:
```python
import functools

import jax
import jax.numpy as jnp
from jax import lax
from jax.experimental import pallas as pl
from jax.experimental.pallas import tpu as pltpu
from jax.sharding import Mesh, PartitionSpec as P

H = 16
HD = 112
HP = 128
WINDOW = 64
EPS = 1e-06
MASKED = -1e30
SUB = 128
SPAN = SUB + WINDOW

BF = jnp.bfloat16
F32 = jnp.float32
ALL = ("z", "y", "x", "c")
PLANE = ("y", "x", "c")
SWAP = [(0, 1), (1, 0)]
NT = (((1,), (1,)), ((), ()))
TN = (((0,), (0,)), ((), ()))


def swap(block, axis):
    return lax.ppermute(block, axis, SWAP)


def normalize(values):
    factor = lax.rsqrt(jnp.mean(values * values, axis=-1, keepdims=True) + EPS)
    return (values * factor, factor)


def norm_back(grad_normed, normed_rows, factor):
    return factor * (
        grad_normed - normed_rows * jnp.mean(grad_normed * normed_rows, axis=-1, keepdims=True)
    )


def dot(left, right, dims=(((1,), (0,)), ((), ()))):
    return lax.dot_general(left, right, dims, preferred_element_type=F32)


def plane_gather(own):
    half = own.shape[0] // 2
    from_x = swap(own, "x")
    from_y = swap(own, "y")
    first = swap(from_y[:half], "x")
    second = swap(from_x[half:], "y")
    mine = [own, from_x, from_y, jnp.concatenate([first, second], axis=0)]
    other = [swap(block, "c") for block in mine]
    return jnp.stack([block for pair in zip(mine, other) for block in pair])


def plane_sum(parts):
    half = parts[0][0].shape[0] // 2
    met = [parts[r][0].astype(F32) + swap(parts[r][1], "c").astype(F32) for r in (3, 2, 1, 0)]
    far, along_y, along_x, here = met
    far = far.astype(BF)
    first = swap(far[:half], "x")
    second = swap(far[half:], "y")
    along_y = jnp.concatenate([along_y[:half] + first.astype(F32), along_y[half:]], axis=0)
    along_x = jnp.concatenate([along_x[:half], along_x[half:] + second.astype(F32)], axis=0)
    got_x = swap(along_x.astype(BF), "x")
    got_y = swap(along_y.astype(BF), "y")
    return here + got_x.astype(F32) + got_y.astype(F32)


def ring_gather(block, count):
    route = [(i, (i + 1) % count) for i in range(count)]
    held = [block]
    for _ in range(count - 1):
        held.append(lax.ppermute(held[-1], "z", route))
    me = lax.axis_index("z")
    stacked = jnp.stack(held[::-1])
    return jnp.roll(stacked, me + 1, axis=0)


def shares_of(query, keys, cut, offset):
    raw = lax.dot_general(query, keys, NT, preferred_element_type=F32)
    row = lax.broadcasted_iota(jnp.int32, raw.shape, 0)
    col = lax.broadcasted_iota(jnp.int32, raw.shape, 1)
    valid = (col > row) & (col <= row + WINDOW)
    if offset == 0:
        valid = valid & (col >= cut)
    scores = jnp.where(valid, raw * (HD ** (-0.5)), MASKED)
    peak = jnp.max(scores, axis=-1, keepdims=True)
    powers = jnp.exp(scores - peak)
    return powers / jnp.sum(powers, axis=-1, keepdims=True)


def joined(prev_ref, halo_ref, cur_ref, at_first, lo):
    before = jnp.where(
        at_first, halo_ref[:, lo - 2 * HP : lo - HP], prev_ref[:, lo : lo + HP]
    )
    return jnp.concatenate([before, cur_ref[:, lo : lo + HP]], axis=0)


def attend_kernel(info_ref, cur_ref, prev_ref, halo_ref, flat_ref, kept_ref):
    stream, block = pl.program_id(0), pl.program_id(1)
    at_first = block == 0
    cut = jnp.where(at_first & (info_ref[2 + stream] == 1), WINDOW, 0)
    rows = cur_ref.shape[0]
    for h in range(2):
        keys = joined(prev_ref, halo_ref, cur_ref, at_first, (2 + h) * HP)
        values = joined(prev_ref, halo_ref, cur_ref, at_first, (4 + h) * HP)
        for at in range(0, rows, SUB):
            query = cur_ref[at : at + SUB, h * HP : (h + 1) * HP]
            shares = shares_of(query, keys[at : at + SPAN], cut, at)
            mixed = jnp.dot(
                shares.astype(BF), values[at : at + SPAN], preferred_element_type=F32
            ).astype(BF)
            flat_ref[at : at + SUB, h * HP : (h + 1) * HP] = mixed
            kept_ref[at : at + SUB, h * HP : (h + 1) * HP] = mixed


def attend(qkv, halo, info):
    rows, blocks = qkv.shape[1], qkv.shape[0] // 2
    mine = lambda s, b, info: (2 * (b ^ info[0]) + s, 0, 0)
    before = lambda s, b, info: (2 * (jnp.maximum(b - 1, 0) ^ info[0]) + s, rows // WINDOW - 1, 0)
    spec = pltpu.PrefetchScalarGridSpec(
        num_scalar_prefetch=1,
        grid=(2, blocks),
        in_specs=[
            pl.BlockSpec((None, rows, 6 * HP), mine),
            pl.BlockSpec((None, WINDOW, 6 * HP), before),
            pl.BlockSpec((None, WINDOW, 4 * HP), lambda s, b, info: (s, 0, 0)),
        ],
        out_specs=[
            pl.BlockSpec((None, rows, 2 * HP), lambda s, b, info: (2 * b + (s ^ info[1]), 0, 0)),
            pl.BlockSpec((None, rows, 2 * HP), mine),
        ],
    )
    shape = jax.ShapeDtypeStruct((2 * blocks, rows, 2 * HP), BF)
    return pl.pallas_call(
        attend_kernel,
        grid_spec=spec,
        out_shape=[shape, shape],
        compiler_params=pltpu.CompilerParams(vmem_limit_bytes=32 * 2**20),
    )(info, qkv, qkv, halo)


def attend_back_kernel(
    info_ref, cur_ref, prev_ref, halo_ref, top_ref, out_ref, tail_ref, lead_ref, keep, acc
):
    stream, step = pl.program_id(0), pl.program_id(1)
    blocks = pl.num_programs(1)
    at_first = step == blocks - 1
    cut = jnp.where(at_first & (info_ref[2 + stream] == 1), WINDOW, 0)
    rows = cur_ref.shape[0]

    @pl.when(step == 0)
    def _():
        keep[...] = jnp.zeros_like(keep)

    acc[...] = jnp.zeros_like(acc)
    for h in range(2):
        lo, hi = h * HP, (h + 1) * HP
        keys = joined(prev_ref, halo_ref, cur_ref, at_first, (2 + h) * HP)
        values = joined(prev_ref, halo_ref, cur_ref, at_first, (4 + h) * HP)
        for at in range(0, rows, SUB):
            query = cur_ref[at : at + SUB, lo:hi]
            top = top_ref[at : at + SUB, lo:hi]
            key = keys[at : at + SPAN]
            shares = shares_of(query, key, cut, at)
            grad_shares = lax.dot_general(
                top, values[at : at + SPAN], NT, preferred_element_type=F32
            )
            grad_raw = (
                shares
                * (grad_shares - jnp.sum(shares * grad_shares, axis=-1, keepdims=True))
                * (HD ** (-0.5))
            ).astype(BF)
            out_ref[at : at + SUB, lo:hi] = jnp.dot(
                grad_raw, key, preferred_element_type=F32
            ).astype(BF)
            acc[at : at + SPAN, lo:hi] += lax.dot_general(
                grad_raw, query, TN, preferred_element_type=F32
            )
            acc[at : at + SPAN, 2 * HP + lo : 2 * HP + hi] += lax.dot_general(
                shares.astype(BF), top, TN, preferred_element_type=F32
            )
    last = acc[rows : rows + WINDOW, :] + keep[...]
    out_ref[: rows - WINDOW, 2 * HP :] = acc[WINDOW:rows, :].astype(BF)
    out_ref[rows - WINDOW :, 2 * HP :] = last.astype(BF)
    keep[...] = acc[:WINDOW, :]

    @pl.when(step == 0)
    def _():
        tail_ref[...] = last

    @pl.when(at_first)
    def _():
        lead_ref[...] = acc[:WINDOW, :].astype(BF)


def attend_back(qkv, halo, top, info):
    rows, blocks = qkv.shape[1], qkv.shape[0] // 2
    at = lambda t: blocks - 1 - t
    mine = lambda s, t, info: (2 * (at(t) ^ info[0]) + s, 0, 0)
    before = lambda s, t, info: (
        2 * (jnp.maximum(at(t) - 1, 0) ^ info[0]) + s,
        rows // WINDOW - 1,
        0,
    )
    side = lambda s, t, info: (s, 0, 0)
    spec = pltpu.PrefetchScalarGridSpec(
        num_scalar_prefetch=1,
        grid=(2, blocks),
        in_specs=[
            pl.BlockSpec((None, rows, 6 * HP), mine),
            pl.BlockSpec((None, WINDOW, 6 * HP), before),
            pl.BlockSpec((None, WINDOW, 4 * HP), side),
            pl.BlockSpec(
                (None, rows, 2 * HP), lambda s, t, info: (2 * at(t) + (s ^ info[1]), 0, 0)
            ),
        ],
        out_specs=[
            pl.BlockSpec((None, rows, 6 * HP), mine),
            pl.BlockSpec((None, WINDOW, 4 * HP), side),
            pl.BlockSpec((None, WINDOW, 4 * HP), side),
        ],
        scratch_shapes=[
            pltpu.VMEM((WINDOW, 4 * HP), F32),
            pltpu.VMEM((rows + WINDOW, 4 * HP), F32),
        ],
    )
    return pl.pallas_call(
        attend_back_kernel,
        grid_spec=spec,
        out_shape=[
            jax.ShapeDtypeStruct(qkv.shape, BF),
            jax.ShapeDtypeStruct(halo.shape, F32),
            jax.ShapeDtypeStruct(halo.shape, BF),
        ],
        compiler_params=pltpu.CompilerParams(vmem_limit_bytes=32 * 2**20),
    )(info, qkv, qkv, halo, top)


def padded_heads(block):
    rows = block.shape[0]
    wide = jnp.pad(block.reshape(rows, H, HD), ((0, 0), (0, 0), (0, HP - HD)))
    return wide.reshape(rows, 8, 2 * HP)


def body(
    inputs,
    starts,
    attn_gain,
    query_weight,
    key_weight,
    value_weight,
    out_weight,
    ffn_gain,
    gate_weight,
    up_weight,
    down_weight,
    cotangent,
):
    rows, width = inputs.shape[1:]
    layers = lax.axis_size("z")
    devices = 8 * layers
    share = query_weight.shape[0]
    hidden_units = gate_weight.shape[1]
    units = hidden_units // 8
    part = down_weight.shape[0]
    me_z = lax.axis_index("z")
    me_block = 2 * lax.axis_index("y") + lax.axis_index("x")
    me_core = lax.axis_index("c")

    streams = plane_gather(inputs[0])
    sheet = jnp.concatenate(
        [
            padded_heads(query_weight),
            padded_heads(key_weight),
            padded_heads(value_weight),
            gate_weight.reshape(share, layers, 8, part).swapaxes(1, 2).reshape(share, 8, units),
            up_weight.reshape(share, layers, 8, part).swapaxes(1, 2).reshape(share, 8, units),
        ],
        axis=2,
    ).swapaxes(0, 1)
    sheet = lax.all_to_all(sheet, PLANE, 0, 0, tiled=True).reshape(8 * share, -1)
    small = jnp.concatenate(
        [attn_gain, ffn_gain, starts[0].astype(BF)], axis=0
    )
    small = jnp.pad(small, (0, 128 - small.shape[0]))
    small = lax.all_to_all(jnp.broadcast_to(small, (devices, 128)), ALL, 0, 0, tiled=True)
    gain_attn = small[:, :share].reshape(width)
    gain_ffn = small[:, share : 2 * share].reshape(width)
    opened = lax.dynamic_slice(small, (8 * me_z, 2 * share), (2, 1))[:, 0].astype(jnp.int32)
    opened = jnp.where(me_core == 0, opened, opened[::-1])
    info = jnp.concatenate([jnp.stack([me_block, me_core]).astype(jnp.int32), opened])

    full_out = lax.all_gather(out_weight, ALL, axis=0, tiled=True)
    down = lax.all_gather(down_weight, "z", axis=0, tiled=True)
    qkv_weight = ring_gather(sheet[:, : 6 * HP], layers).reshape(width, 6 * HP)
    gate_up = lax.all_gather(sheet[:, 6 * HP :], "z", axis=0, tiled=True)
    tops = plane_gather(cotangent[0]).reshape(8 * rows, width)

    stream = streams.reshape(8 * rows, width).astype(F32)
    hidden1 = (normalize(stream)[0] * gain_attn).astype(BF)
    qkv = dot(hidden1, qkv_weight).astype(BF).reshape(8, rows, 6 * HP)
    last = 2 * (3 ^ me_block)
    rim = lax.dynamic_slice(
        qkv, (last, rows - WINDOW, 2 * HP), (2, WINDOW, 4 * HP)
    )
    halo = lax.ppermute(rim, "z", [(i, i + 1) for i in range(layers - 1)])
    flat, kept = attend(qkv, halo, info)
    mixed = lax.all_to_all(flat, PLANE, 0, 0, tiled=True)
    mixed = mixed.reshape(8, rows, 2, HP)[..., :HD].transpose(1, 0, 2, 3).reshape(rows, H * HD)
    middle = inputs[0].astype(F32) + dot(mixed, full_out)

    normed2, rscale2 = normalize(middle)
    hidden2 = plane_gather((normed2 * gain_ffn).astype(BF)).reshape(8 * rows, width)
    gate = dot(hidden2, gate_up[:, :units])
    upper = dot(hidden2, gate_up[:, units:])
    sigma = jax.nn.sigmoid(gate)
    activ = gate * sigma
    inner = (activ * upper).astype(BF)
    grad_inner = dot(tops, down, NT)
    grad_upper = (grad_inner * activ).astype(BF)
    grad_gate = (grad_inner * upper * sigma * (1.0 + gate * (1.0 - sigma))).astype(BF)
    parts = []
    for r in range(4):
        at = slice(2 * r * rows, 2 * (r + 1) * rows)
        part_sum = dot(grad_gate[at], gate_up[:, :units], NT) + dot(
            grad_upper[at], gate_up[:, units:], NT
        )
        part_sum = part_sum.astype(BF)
        parts.append((part_sum[:rows], part_sum[rows:]))
    grad_hidden2 = plane_sum(parts)
    down_sum = lax.psum_scatter(
        dot(inner, tops, TN).astype(BF), "z", scatter_dimension=0, tiled=True
    )
    gate_up_sum = lax.psum_scatter(
        jnp.concatenate([dot(hidden2, grad_gate, TN), dot(hidden2, grad_upper, TN)], axis=1).astype(BF),
        "z",
        scatter_dimension=0,
        tiled=True,
    )
    parts = []
    for r in range(4):
        at = slice(2 * r * rows, 2 * (r + 1) * rows)
        part_sum = dot(inner[at], down).astype(BF)
        parts.append((part_sum[:rows], part_sum[rows:]))
    layer_out = (middle + plane_sum(parts)).astype(BF)

    ffn_gain_local = jnp.sum(grad_hidden2 * normed2, axis=0)
    grad_middle = cotangent[0].astype(F32) + norm_back(grad_hidden2 * gain_ffn, normed2, rscale2)
    grad_branch = grad_middle.astype(BF)

    grad_mixed = padded_heads(dot(grad_branch, full_out, NT).astype(BF)).swapaxes(0, 1)
    grad_mixed = lax.all_to_all(grad_mixed, PLANE, 0, 0, tiled=True)
    branches = plane_gather(grad_branch).reshape(8 * rows, width)
    grad_qkv, tail, lead = attend_back(qkv, halo, grad_mixed, info)
    back = lax.ppermute(lead, "z", [(i + 1, i) for i in range(layers - 1)])
    grad_qkv = lax.dynamic_update_slice(
        grad_qkv, (tail + back.astype(F32)).astype(BF), (last, rows - WINDOW, 2 * HP)
    ).reshape(8 * rows, 6 * HP)
    parts = []
    for r in range(4):
        at = slice(2 * r * rows, 2 * (r + 1) * rows)
        part_sum = dot(grad_qkv[at], qkv_weight, NT).astype(BF)
        parts.append((part_sum[:rows], part_sum[rows:]))
    grad_hidden1 = plane_sum(parts)
    attn_sums = jnp.concatenate(
        [dot(hidden1, grad_qkv, TN), dot(branches, kept.reshape(8 * rows, 2 * HP), TN)], axis=1
    ).astype(BF)
    attn_sums = lax.psum_scatter(attn_sums, "z", scatter_dimension=0, tiled=True)
    normed1, rscale1 = normalize(inputs[0].astype(F32))
    attn_gain_local = jnp.sum(grad_hidden1 * normed1, axis=0)
    input_grad = grad_middle + norm_back(grad_hidden1 * gain_attn, normed1, rscale1)

    gate_up_sum = lax.all_to_all(
        gate_up_sum.reshape(8, share, 2 * units), PLANE, 0, 0, tiled=True
    ).astype(F32)
    gate_up_sum = gate_up_sum.reshape(8, share, 2, layers, part).transpose(2, 1, 3, 0, 4)
    gate_grad, up_grad = gate_up_sum.reshape(2, share, hidden_units)
    qkv_sum = lax.all_to_all(
        attn_sums[:, : 6 * HP].reshape(8, share, 6 * HP), PLANE, 0, 0, tiled=True
    ).astype(F32)
    qkv_sum = qkv_sum.reshape(8, share, 3, 2, HP)[..., :HD].transpose(2, 1, 0, 3, 4)
    query_grad, key_grad, value_grad = qkv_sum.reshape(3, share, width)
    out_sum = attn_sums[:, 6 * HP :].reshape(-1, 2, HP)[..., :HD].reshape(-1, layers, share)
    pieces = []
    for j in range(layers):
        route = [
            (8 * z + p, layers * p + (z + j) % layers) for z in range(layers) for p in range(8)
        ]
        piece = lax.dynamic_index_in_dim(out_sum, (me_z + j) % layers, axis=1, keepdims=False)
        pieces.append(lax.ppermute(piece, ALL, route))
    rank = 8 * me_z + 2 * me_block + me_core
    turned = jnp.roll(jnp.stack(pieces[::-1]), rank % layers + 1, axis=0)
    output_grad = turned.reshape(width, share).T.astype(F32)
    gains = jnp.stack([attn_gain_local, ffn_gain_local]).reshape(2, devices, share).swapaxes(0, 1)
    gains = jnp.sum(lax.all_to_all(gains, ALL, 0, 0, tiled=True), axis=0)
    return (
        layer_out[None],
        input_grad[None],
        gains[0],
        query_grad,
        key_grad,
        value_grad,
        output_grad,
        gains[1],
        gate_grad,
        up_grad,
        down_sum.astype(F32),
    )


def solution(mesh):
    blocks = mesh.shape["seq"]
    fine = Mesh(mesh.devices.reshape(blocks // 4, 2, 2, 2), ALL)
    tokens = P("c", ("z", "y", "x"), None)
    weight = P(ALL, None)
    gain = P(ALL)
    in_specs = (
        tokens,
        P("c", ("z", "y", "x")),
        gain,
        weight,
        weight,
        weight,
        weight,
        gain,
        weight,
        weight,
        weight,
        tokens,
    )
    out_specs = (
        tokens,
        tokens,
        gain,
        weight,
        weight,
        weight,
        weight,
        gain,
        weight,
        weight,
        weight,
    )
    return jax.shard_map(body, mesh=fine, in_specs=in_specs, out_specs=out_specs, check_vma=False)
```

time: 3040 us -> 783 us (0.26)
  waiting for transfers between devices: 2550 us -> 308 us
  matrix products: 261 us -> 135 us
  starting transfers between devices: 14.3 us -> 84.5 us
  local copies, waits for them, and re-layouts: 84.1 us -> 130 us
  other arithmetic: 65.7 us -> 35.1 us
    unnamed x10 -> x6, waiting for transfers between devices: 1690 us -> 1.43 us
    all_gather x7 -> x3, waiting for transfers between devices: 504 us -> 0.01 us  [the longest x1 0.01 us: body(): full_out = lax.all_gather(out_weight, ALL, axis=0, tiled=True)]
    reduce_scatter x1 -> x3, waiting for transfers between devices: 359 us -> 6.07 us  [the longest x1 6.05 us: body(): lax.psum_scatter(attn_sums, 'z', scatter_dimension=0, tiled=True)]
    ppermute x4 -> x65, waiting for transfers between devices: 0.01 us -> 232 us  [the longest x56 120 us: swap(): return lax.ppermute(block, axis, SWAP)]
    dot_general x27, matrix products: 261 us -> 135 us  [dot(): return lax.dot_general(left, right, dims, preferred_element_type=F32)]
    all_to_all x0 -> x6, waiting for transfers between devices: none -> 68.3 us  [the longest x1 41.5 us: body(): lax.all_to_all(jnp.broadcast_to(small, (devices, 128)), ALL, 0, 0, tiled=...]
    unnamed x48 -> x128, local copies, waits for them, and re-layouts: 9.78 us -> 55.2 us
    concatenate x3 -> x10, other arithmetic: 49.5 us -> 9.06 us  [the longest x1 4.62 us: body(): jnp.concatenate([dot(hidden2, grad_gate, TN), dot(hidden2, grad_upper, TN...]
  transfers between devices with their start and end apart: 13 -> 77, of which waited for: 9 -> 30; matrix products, arithmetic and copies ran while one was open for 7% -> 34% of each run, Pallas kernels for 0% -> 4%
where the time goes in v1:
time: 783 us; the launch traced here: 769 us
  waiting for transfers between devices  308 us (39%)
  matrix products  135 us (17%)
  local copies, waits for them, and re-layouts  130 us (17%)
  starting transfers between devices  84.5 us (11%)
  other arithmetic  35.1 us (4%)
  blocking collectives  31.9 us (4%)
  Pallas kernels  28.3 us (4%)
  between operations  16.6 us (2%)
    dot_general x27, matrix products, dot(): return lax.dot_general(left, right, dims, preferred_element_type=F32)  135 us
    ppermute x56, waiting for transfers between devices, swap(): return lax.ppermute(block, axis, SWAP)  120 us
    ppermute x3, waiting for transfers between devices, ring_gather(): held.append(lax.ppermute(held[-1], 'z', route))  104 us
    unnamed x128, local copies, waits for them, and re-layouts  55.2 us
    all_to_all x1, waiting for transfers between devices, body(): lax.all_to_all(jnp.broadcast_to(small, (devices, 128)), ALL, 0, 0, tiled=...  41.5 us
    ppermute x56, starting transfers between devices, swap(): return lax.ppermute(block, axis, SWAP)  33.8 us
    all_to_all x1, blocking collectives, body(): lax.all_to_all(sheet, PLANE, 0, 0, tiled=True).reshape(8 * share, -1)  31.9 us
    pallas_call x1, Pallas kernels, attend_back(): pl.pallas_call(attend_back_kernel, grid_spec=spec, out_shape=[jax.ShapeDt...  17.7 us
  transfers between devices with their start and end apart: 77, of which 30 were waited for; matrix products, arithmetic and copies ran while one was open for 34% of the time, Pallas kernels for 4%

profile of v1, /device:TPU:26, one launch (start us, length us, event | category | flops | bytes accessed | tf_op | source)
XLA Modules:
  0.0 769.2 jit_solution(8329634433921184287)
XLA Ops:
  22.3 31.9 %all_to_all.39 = bf16[8,56,1984]{2,1,0:T(8,128)(2,1)S(1)} all-to-all(bf16[8,56,1984]{2,1,0:T(8,128)(2,1)S(1)} %copy.76), channel_id=1, replica_groups=mesh['z'=4,'y'=2,'x'=2,'c'=2] {'y','x','c'}, dimensions={0} | all-to-all | bytes 3555328 | tf_op jit(solution)/shard_map/all_to_all | solution.py:285
  60.8 5.3 all-to-all-start
  70.0 41.5 %all-to-all-done = bf16[32,1,128]{2,1,0:T(2,128)(2,1)S(1)} async-done(((bf16[32,1,128]{2,1,0:T(2,128)(2,1)}), bf16[32,1,128]{2,1,0:T(2,128)(2,1)S(1)}, u32[]{:S(2)}, u32[]{:S(2)}) %all-to-all-start) | async-done | bytes 8224 | tf_op jit(solution)/shard_map/all_to_all | solution.py:290
  129.6 8.2 %collective-permute-done.5 = bf16[128,1792]{1,0:T(8,128)(2,1)S(1)} collective-permute-done((bf16[128,1792]{1,0:T(8,128)(2,1)S(1)}, bf16[128,1792]{1,0:T(8,128)(2,1)S(1)}, u32[]{:S(2)}, u32[]{:S(2)}) %collective-permute-start.5) | collective-permute-done | bytes 458784 | tf_op jit(solution)/shard_map/ppermute | solution.py:29
  143.4 46.8 %collective-permute-done.8 = bf16[448,768]{1,0:T(8,128)(2,1)S(1)} collective-permute-done((bf16[448,768]{1,0:T(8,128)(2,1)S(1)}, bf16[448,768]{1,0:T(8,128)(2,1)S(1)}, u32[]{:S(2)}, u32[]{:S(2)}) %collective-permute-start.8) | collective-permute-done | bytes 688160 | tf_op jit(solution)/shard_map/ppermute | solution.py:76
  192.0 19.9 %collective-permute-done.9 = bf16[448,768]{1,0:T(8,128)(2,1)S(1)} collective-permute-done((bf16[448,768]{1,0:T(8,128)(2,1)S(1)}, bf16[448,768]{1,0:T(8,128)(2,1)S(1)}, u32[]{:S(2)}, u32[]{:S(2)}) %collective-permute-start.9) | collective-permute-done | bytes 688160 | tf_op jit(solution)/shard_map/ppermute | solution.py:76
  215.6 4.7 fusion.2
  220.3 37.5 %collective-permute-done.10 = bf16[448,768]{1,0:T(8,128)(2,1)} collective-permute-done((bf16[448,768]{1,0:T(8,128)(2,1)S(1)}, bf16[448,768]{1,0:T(8,128)(2,1)}, u32[]{:S(2)}, u32[]{:S(2)}) %collective-permute-start.10) | collective-permute-done | bytes 688160 | tf_op jit(solution)/shard_map/ppermute | solution.py:76
  263.6 6.0 convolution_convert_fusion
  276.5 10.6 %shard_map.203 = (bf16[8,256,256]{2,1,0:T(8,128)(2,1)S(1)}, bf16[8,256,256]{2,1,0:T(8,128)(2,1)S(1)}) custom-call(s32[4]{0:T(128)S(1)} %pad_add_fusion.info_ref, bf16[8,256,768]{2,1,0:T(8,128)(2,1)S(1)} %bitcast.196, bf16[8,256,768]{2,1,0:T(8,128)(2,1)S(1)} %bitcast.197, bf16[2,64,512]{2,1,0:T(8,128)(2,1)S(1)} %collective-permute-done.11.halo_ref), custom_call_target="tpu_custom_call" | custom-call | tf_op jit(solution)/shard_map/pallas_call | solution.py:138
  289.0 4.8 all-to-all-start.2
  298.2 9.7 %all-to-all-done.2 = bf16[8,256,256]{2,1,0:T(8,128)(2,1)} async-done(((bf16[8,256,256]{2,1,0:T(8,128)(2,1)}), bf16[8,256,256]{2,1,0:T(8,128)(2,1)}, u32[]{:S(2)}, u32[]{:S(2)}) %all-to-all-start.2) | async-done | bytes 1048608 | tf_op jit(solution)/shard_map/all_to_all | solution.py:312
  312.8 5.3 multiply_reduce_fusion.2
  326.0 15.8 %collective-permute-done.13 = bf16[256,1792]{1,0:T(8,128)(2,1)S(1)} collective-permute-done((bf16[256,1792]{1,0:T(8,128)(2,1)S(1)}, bf16[256,1792]{1,0:T(8,128)(2,1)S(1)}, u32[]{:S(2)}, u32[]{:S(2)}) %collective-permute-start.13) | collective-permute-done | bytes 917536 | tf_op jit(solution)/shard_map/ppermute | solution.py:29
  347.3 8.8 %collective-permute-done.17 = bf16[128,1792]{1,0:T(8,128)(2,1)S(1)} collective-permute-done((bf16[128,1792]{1,0:T(8,128)(2,1)S(1)}, bf16[128,1792]{1,0:T(8,128)(2,1)S(1)}, u32[]{:S(2)}, u32[]{:S(2)}) %collective-permute-start.17) | collective-permute-done | bytes 458784 | tf_op jit(solution)/shard_map/ppermute | solution.py:29
  361.3 11.1 %fusion.19 = f32[2048,608]{0,1:T(8,128)} fusion(bf16[2048,1792]{1,0:T(8,128)(2,1)} %bitcast.33, bf16[1792,1216]{1,0:T(8,128)(2,1)} %all-gather.6.cloned.1.call-done), kind=kOutput, calls=%fused_computation.67 | convolution fusion | flops 4462739456 | bytes 14614528 | tf_op jit(solution)/shard_map/dot_general | solution.py:44
  372.4 10.2 %fusion.29 = f32[2048,608]{0,1:T(8,128)} fusion(bf16[2048,1792]{1,0:T(8,128)(2,1)} %bitcast.33, bf16[1792,1216]{1,0:T(8,128)(2,1)S(1)} %copy-done.25), kind=kOutput, calls=%fused_computation.77 | convolution fusion | flops 4462739456 | bytes 14614528 | tf_op jit(solution)/shard_map/dot_general | solution.py:44
  382.6 12.9 %multiply_convert_fusion = (bf16[2048,608]{0,1:T(8,128)(2,1)}, bf16[2048,608]{0,1:T(8,128)(2,1)}, bf16[2048,608]{0,1:T(8,128)(2,1)S(1)}) fusion(f32[2048,608]{0,1:T(8,128)} %fusion.29, f32[2048,608]{0,1:T(8,128)} %fusion.19, bf16[2048,1792]{1,0:T(8,128)(2,1)} %bitcast.239, bf16[608,1792]{1,0:T(8,128)(2,1)} %all-gather.8.cloned.1.call-done), kind=kOutput, calls=%fused_computation.6 | convolution fusion | flops 4481417216 | bytes 26951680 | tf_op jit(solution)/shard_map/dot_general | solution.py:44
  397.0 8.9 %convolution_convert_fusion.3 = bf16[608,1792]{1,0:T(8,128)(2,1)} fusion(bf16[2048,608]{0,1:T(8,128)(2,1)S(1)} %get-tuple-element.32, bf16[2048,1792]{1,0:T(8,128)(2,1)} %bitcast.240), kind=kOutput, calls=%fused_computation.20 | convolution fusion | flops 4463828992 | bytes 12009472 | tf_op jit(solution)/shard_map/dot_general | solution.py:44
  416.0 9.4 %convolution_convert_fusion.1 = bf16[1792,608]{0,1:T(8,128)(2,1)} fusion(bf16[2048,608]{0,1:T(8,128)(2,1)S(1)} %copy-done.27, bf16[2048,1792]{1,0:T(8,128)(2,1)} %bitcast.33), kind=kOutput, calls=%fused_computation.18 | convolution fusion | flops 4463828992 | bytes 12009472 | tf_op jit(solution)/shard_map/dot_general | solution.py:44
  437.0 4.3 add_convert_fusion.1
  441.3 4.3 add_convert_fusion.2
  445.8 4.9 fusion.27
  450.8 4.3 add_convert_fusion.3
  460.4 10.1 %collective-permute-done.26 = bf16[128,1792]{1,0:T(8,128)(2,1)S(1)} collective-permute-done((bf16[128,1792]{1,0:T(8,128)(2,1)S(1)}, bf16[128,1792]{1,0:T(8,128)(2,1)S(1)}, u32[]{:S(2)}, u32[]{:S(2)}) %collective-permute-start.26) | collective-permute-done | bytes 458784 | tf_op jit(solution)/shard_map/ppermute | solution.py:29
  472.7 9.5 %collective-permute-done.42 = bf16[128,1792]{1,0:T(8,128)(2,1)S(1)} collective-permute-done((bf16[128,1792]{1,0:T(8,128)(2,1)S(1)}, bf16[128,1792]{1,0:T(8,128)(2,1)S(1)}, u32[]{:S(2)}, u32[]{:S(2)}) %collective-permute-start.42) | collective-permute-done | bytes 458784 | tf_op jit(solution)/shard_map/ppermute | solution.py:29
  486.1 9.1 %convolution_convert_fusion.2 = bf16[1792,608]{0,1:T(8,128)(2,1)} fusion(bf16[2048,608]{0,1:T(8,128)(2,1)S(1)} %copy-done.29, bf16[2048,1792]{1,0:T(8,128)(2,1)} %bitcast.33), kind=kOutput, calls=%fused_computation.19 | convolution fusion | flops 4463828992 | bytes 12009472 | tf_op jit(solution)/shard_map/dot_general | solution.py:44
  495.3 4.4 collective-permute-done.27
  499.7 5.9 collective-permute-done.24
  505.5 13.3 %collective-permute-done.43 = bf16[256,1792]{1,0:T(8,128)(2,1)S(1)} collective-permute-done((bf16[256,1792]{1,0:T(8,128)(2,1)S(1)}, bf16[256,1792]{1,0:T(8,128)(2,1)S(1)}, u32[]{:S(2)}, u32[]{:S(2)}) %collective-permute-start.43) | collective-permute-done | bytes 917536 | tf_op jit(solution)/shard_map/ppermute | solution.py:29
  529.7 4.0 convolution_convert_fusion.12
  540.4 5.6 all-to-all-start.3
  546.0 4.6 pad_maximum_fusion
  550.7 7.2 copy.95
  558.0 4.9 all-to-all-done.3.top_ref
  562.9 17.7 %shard_map.204 = (bf16[8,256,768]{2,1,0:T(8,128)(2,1)S(1)}, f32[2,64,512]{2,1,0:T(8,128)S(1)}, bf16[2,64,512]{2,1,0:T(8,128)(2,1)S(1)}) custom-call(s32[4]{0:T(128)S(1)} %pad_add_fusion.info_ref, bf16[8,256,768]{2,1,0:T(8,128)(2,1)S(1)} %bitcast.198, bf16[8,256,768]{2,1,0:T(8,128)(2,1)S(1)} %bitcast.199, ...), custom_call_target="tpu_custom_call" | custom-call | tf_op jit(solution)/shard_map/pallas_call | solution.py:231
  592.0 9.5 %bitcast_convert_fusion = bf16[1792,768]{0,1:T(8,128)(2,1)S(1)} fusion(bf16[8,256,1792]{2,1,0:T(8,128)(2,1)} %fusion.2, bf16[8,256,768]{2,1,0:T(8,128)(2,1)S(1)} %fusion.50), kind=kOutput, calls=%fused_computation.5 | convolution fusion | flops 5638520832 | bytes 13238272 | tf_op jit(solution)/shard_map/dot_general | solution.py:44
  614.7 6.2 copy.93
  632.6 11.0 %collective-permute-done.51 = bf16[128,1792]{1,0:T(8,128)(2,1)S(1)} collective-permute-done((bf16[128,1792]{1,0:T(8,128)(2,1)S(1)}, bf16[128,1792]{1,0:T(8,128)(2,1)S(1)}, u32[]{:S(2)}, u32[]{:S(2)}) %collective-permute-start.51) | collective-permute-done | bytes 458784 | tf_op jit(solution)/shard_map/ppermute | solution.py:29
  648.3 18.2 %collective-permute-done.52 = bf16[256,1792]{1,0:T(8,128)(2,1)} collective-permute-done((bf16[256,1792]{1,0:T(8,128)(2,1)}, bf16[256,1792]{1,0:T(8,128)(2,1)}, u32[]{:S(2)}, u32[]{:S(2)}) %collective-permute-start.52) | collective-permute-done | bytes 917536 | tf_op jit(solution)/shard_map/ppermute | solution.py:29
  672.5 4.9 all-to-all-start.4
  681.4 5.5 all-to-all-start.6
  686.9 4.1 fusion.12
  691.6 10.4 %all-to-all-done.6 = bf16[8,56,1216]{2,1,0:T(8,128)(2,1)} async-done(((bf16[8,56,1216]{2,1,0:T(8,128)(2,1)}), bf16[8,56,1216]{2,1,0:T(8,128)(2,1)}, u32[]{:S(2)}, u32[]{:S(2)}) %all-to-all-start.6) | async-done | bytes 1089568 | tf_op jit(solution)/shard_map/all_to_all | solution.py:377
  702.0 7.8 %reshape.274 = f32[8,56,2,4,152]{4,3,2,1,0:T(4,128)} reshape(bf16[8,56,1216]{2,1,0:T(8,128)(2,1)} %all-to-all-done.6) | data formatting | bytes 3268608 | tf_op jit(solution)/shard_map/transpose | solution.py:380
  709.8 6.0 reduce-scatter.10.cloned.1.call-done
  735.6 4.8 all-to-all-start.5
  749.7 4.8 collective-permute-done.62
  (414 shorter events, 235.4 us)
Async XLA Ops:
  7.2 305.6 %all-gather.4.cloned.1.call-start = ((), (), s32[]{:S(2)}) async-start(), calls=%async_computation.10 | async-start | bytes 6623232 | tf_op jit(solution)/shard_map/all_gather | solution.py:297
  7.9 353.3 %all-gather.6.cloned.1.call-start = ((), (), s32[]{:S(2)}) async-start(), calls=%async_computation.11 | async-start | bytes 5734400 | tf_op jit(solution)/shard_map/all_gather | solution.py:300
  55.3 56.9 %collective-permute-start.29 = (bf16[256,1792]{1,0:T(8,128)(2,1)}, bf16[256,1792]{1,0:T(8,128)(2,1)}, u32[]{:S(2)}, u32[]{:S(2)}) collective-permute-start(bf16[256,1792]{1,0:T(8,128)(2,1)} %bitcast.218), channel_id=1, source_target_pairs={{0,2},{2,0},{1,3},{3,1},{4,6},{6,4},{5,7},{7,5},{8,10},{10,8},{9,1... | collective-permute-start | bytes 2752520 | tf_op jit(solution)/shard_map/ppermute | solution.py:29
  57.2 61.9 %collective-permute-start.28 = (bf16[256,1792]{1,0:T(8,128)(2,1)}, bf16[256,1792]{1,0:T(8,128)(2,1)}, u32[]{:S(2)}, u32[]{:S(2)}) collective-permute-start(bf16[256,1792]{1,0:T(8,128)(2,1)} %bitcast.219), channel_id=1, source_target_pairs={{0,1},{1,0},{2,3},{3,2},{4,5},{5,4},{6,7},{7,6},{8,9},{9,8},{10,11... | collective-permute-start | bytes 2752520 | tf_op jit(solution)/shard_map/ppermute | solution.py:29
  57.2 56.3 %collective-permute-start.31 = (bf16[256,1792]{1,0:T(8,128)(2,1)}, bf16[256,1792]{1,0:T(8,128)(2,1)}, u32[]{:S(2)}, u32[]{:S(2)}) collective-permute-start(bf16[256,1792]{1,0:T(8,128)(2,1)} %bitcast.220), channel_id=1, source_target_pairs={{0,4},{4,0},{1,5},{5,1},{2,6},{6,2},{3,7},{7,3},{8,12},{12,8},{9,1... | collective-permute-start | bytes 2752520 | tf_op jit(solution)/shard_map/ppermute | solution.py:29
  57.8 57.6 %collective-permute-start.1 = (bf16[256,1792]{1,0:T(8,128)(2,1)S(1)}, bf16[256,1792]{1,0:T(8,128)(2,1)}, u32[]{:S(2)}, u32[]{:S(2)}) collective-permute-start(bf16[256,1792]{1,0:T(8,128)(2,1)S(1)} %bitcast.200), channel_id=1, source_target_pairs={{0,2},{2,0},{1,3},{3,1},{4,6},{6,4},{5,7},{7,5},{8,10},{10,8},{9,1... | collective-permute-start | bytes 2752520 | tf_op jit(solution)/shard_map/ppermute | solution.py:29
  58.3 58.6 %collective-permute-start.3 = (bf16[256,1792]{1,0:T(8,128)(2,1)S(1)}, bf16[256,1792]{1,0:T(8,128)(2,1)}, u32[]{:S(2)}, u32[]{:S(2)}) collective-permute-start(bf16[256,1792]{1,0:T(8,128)(2,1)S(1)} %bitcast.201), channel_id=1, source_target_pairs={{0,4},{4,0},{1,5},{5,1},{2,6},{6,2},{3,7},{7,3},{8,12},{12,8},{9,1... | collective-permute-start | bytes 2752520 | tf_op jit(solution)/shard_map/ppermute | solution.py:29
  60.8 50.7 %all-to-all-start = ((bf16[32,1,128]{2,1,0:T(2,128)(2,1)}), bf16[32,1,128]{2,1,0:T(2,128)(2,1)S(1)}, u32[]{:S(2)}, u32[]{:S(2)}) async-start(bf16[32,1,128]{2,1,0:T(2,128)(2,1)} %broadcast_in_dim.6), calls=%async_computation | async-start | bytes 32768 | tf_op jit(solution)/shard_map/all_to_all | solution.py:290
  66.1 316.5 %all-gather.8.cloned.1.call-start = ((), (), s32[]{:S(2)}) async-start(), calls=%async_computation.12 | async-start | bytes 2723840 | tf_op jit(solution)/shard_map/all_gather | solution.py:298
  113.5 24.4 %collective-permute-start.34 = (bf16[128,1792]{1,0:T(8,128)(2,1)S(1)}, bf16[128,1792]{1,0:T(8,128)(2,1)S(1)}, u32[]{:S(2)}, u32[]{:S(2)}) collective-permute-start(bf16[128,1792]{1,0:T(8,128)(2,1)S(1)} %slice.382), channel_id=1, source_target_pairs={{0,4},{4,0},{1,5},{5,1},{2,6},{6,2},{3,7},{7,3},{8,12},{12,8},{9,1... | collective-permute-start | bytes 1376264 | tf_op jit(solution)/shard_map/ppermute | solution.py:29
  116.9 22.4 %collective-permute-start.6 = (bf16[128,1792]{1,0:T(8,128)(2,1)S(1)}, bf16[128,1792]{1,0:T(8,128)(2,1)S(1)}, u32[]{:S(2)}, u32[]{:S(2)}) collective-permute-start(bf16[128,1792]{1,0:T(8,128)(2,1)S(1)} %slice.353), channel_id=1, source_target_pairs={{0,4},{4,0},{1,5},{5,1},{2,6},{6,2},{3,7},{7,3},{8,12},{12,8},{9,1... | collective-permute-start | bytes 1376264 | tf_op jit(solution)/shard_map/ppermute | solution.py:29
  125.4 145.6 %collective-permute-start.30 = (bf16[256,1792]{1,0:T(8,128)(2,1)}, bf16[256,1792]{1,0:T(8,128)(2,1)}, u32[]{:S(2)}, u32[]{:S(2)}) collective-permute-start(bf16[256,1792]{1,0:T(8,128)(2,1)} %collective-permute-done.29), channel_id=1, source_target_pairs={{0,1},{1,0},{2,3},{3,2},{4,5},{5,4},{6,7},{7,6},{8,9},{9,8},{10,11... | collective-permute-start | bytes 2752520 | tf_op jit(solution)/shard_map/ppermute | solution.py:29
  137.9 158.2 %collective-permute-start.32 = (bf16[256,1792]{1,0:T(8,128)(2,1)}, bf16[256,1792]{1,0:T(8,128)(2,1)}, u32[]{:S(2)}, u32[]{:S(2)}) collective-permute-start(bf16[256,1792]{1,0:T(8,128)(2,1)} %collective-permute-done.31), channel_id=1, source_target_pairs={{0,1},{1,0},{2,3},{3,2},{4,5},{5,4},{6,7},{7,6},{8,9},{9,8},{10,11... | collective-permute-start | bytes 2752520 | tf_op jit(solution)/shard_map/ppermute | solution.py:29
  139.3 184.5 %collective-permute-start.35 = (bf16[256,1792]{1,0:T(8,128)(2,1)}, bf16[256,1792]{1,0:T(8,128)(2,1)}, u32[]{:S(2)}, u32[]{:S(2)}) collective-permute-start(bf16[256,1792]{1,0:T(8,128)(2,1)} %constant_dynamic-update-slice_fusion.5), channel_id=1, source_target_pairs={{0,1},{1,0},{2,3},{3,2},{4,5},{5,4},{6,7},{7,6},{8,9},{9,8},{10,11... | collective-permute-start | bytes 2752520 | tf_op jit(solution)/shard_map/ppermute | solution.py:29
  139.4 51.0 %collective-permute-start.7 = (bf16[256,1792]{1,0:T(8,128)(2,1)S(1)}, bf16[256,1792]{1,0:T(8,128)(2,1)S(1)}, u32[]{:S(2)}, u32[]{:S(2)}) collective-permute-start(bf16[256,1792]{1,0:T(8,128)(2,1)S(1)} %constant_dynamic-update-slice_fusion), channel_id=1, source_target_pairs={{0,1},{1,0},{2,3},{3,2},{4,5},{5,4},{6,7},{7,6},{8,9},{9,8},{10,11... | collective-permute-start | bytes 2752520 | tf_op jit(solution)/shard_map/ppermute | solution.py:29
  143.0 47.1 %collective-permute-start.8 = (bf16[448,768]{1,0:T(8,128)(2,1)S(1)}, bf16[448,768]{1,0:T(8,128)(2,1)S(1)}, u32[]{:S(2)}, u32[]{:S(2)}) collective-permute-start(bf16[448,768]{1,0:T(8,128)(2,1)S(1)} %slice.355), channel_id=1, source_target_pairs={{0,8},{8,16},{16,24},{24,0},{1,9},{9,17},{17,25},{25,1},{2,10},{10... | collective-permute-start | bytes 2064392 | tf_op jit(solution)/shard_map/ppermute | solution.py:76
  190.2 21.8 %collective-permute-start.9 = (bf16[448,768]{1,0:T(8,128)(2,1)S(1)}, bf16[448,768]{1,0:T(8,128)(2,1)S(1)}, u32[]{:S(2)}, u32[]{:S(2)}) collective-permute-start(bf16[448,768]{1,0:T(8,128)(2,1)S(1)} %collective-permute-done.8), channel_id=1, source_target_pairs={{0,8},{8,16},{16,24},{24,0},{1,9},{9,17},{17,25},{25,1},{2,10},{10... | collective-permute-start | bytes 2064392 | tf_op jit(solution)/shard_map/ppermute | solution.py:76
  211.9 45.9 %collective-permute-start.10 = (bf16[448,768]{1,0:T(8,128)(2,1)S(1)}, bf16[448,768]{1,0:T(8,128)(2,1)}, u32[]{:S(2)}, u32[]{:S(2)}) collective-permute-start(bf16[448,768]{1,0:T(8,128)(2,1)S(1)} %collective-permute-done.9), channel_id=1, source_target_pairs={{0,8},{8,16},{16,24},{24,0},{1,9},{9,17},{17,25},{25,1},{2,10},{10... | collective-permute-start | bytes 2064392 | tf_op jit(solution)/shard_map/ppermute | solution.py:76
  293.9 383.6 %reduce-scatter.8.cloned.1.call-start = ((), (), s32[]{:S(2)}) async-start(), calls=%async_computation.13 | async-start | bytes 2723840 | tf_op jit(solution)/shard_map/reduce_scatter | solution.py:335
  319.5 22.3 %collective-permute-start.13 = (bf16[256,1792]{1,0:T(8,128)(2,1)S(1)}, bf16[256,1792]{1,0:T(8,128)(2,1)S(1)}, u32[]{:S(2)}, u32[]{:S(2)}) collective-permute-start(bf16[256,1792]{1,0:T(8,128)(2,1)S(1)} %get-tuple-element.29), channel_id=1, source_target_pairs={{0,2},{2,0},{1,3},{3,1},{4,6},{6,4},{5,7},{7,5},{8,10},{10,8},{9,1... | collective-permute-start | bytes 2752520 | tf_op jit(solution)/shard_map/ppermute | solution.py:29
  321.0 24.3 %collective-permute-start.12 = (bf16[256,1792]{1,0:T(8,128)(2,1)S(1)}, bf16[256,1792]{1,0:T(8,128)(2,1)S(1)}, u32[]{:S(2)}, u32[]{:S(2)}) collective-permute-start(bf16[256,1792]{1,0:T(8,128)(2,1)S(1)} %get-tuple-element.29), channel_id=1, source_target_pairs={{0,1},{1,0},{2,3},{3,2},{4,5},{5,4},{6,7},{7,6},{8,9},{9,8},{10,11... | collective-permute-start | bytes 2752520 | tf_op jit(solution)/shard_map/ppermute | solution.py:29
  321.0 22.8 %collective-permute-start.15 = (bf16[256,1792]{1,0:T(8,128)(2,1)S(1)}, bf16[256,1792]{1,0:T(8,128)(2,1)S(1)}, u32[]{:S(2)}, u32[]{:S(2)}) collective-permute-start(bf16[256,1792]{1,0:T(8,128)(2,1)S(1)} %get-tuple-element.29), channel_id=1, source_target_pairs={{0,4},{4,0},{1,5},{5,1},{2,6},{6,2},{3,7},{7,3},{8,12},{12,8},{9,1... | collective-permute-start | bytes 2752520 | tf_op jit(solution)/shard_map/ppermute | solution.py:29
  409.6 45.6 %collective-permute-start.25 = (bf16[256,1792]{1,0:T(8,128)(2,1)S(1)}, bf16[256,1792]{1,0:T(8,128)(2,1)S(1)}, u32[]{:S(2)}, u32[]{:S(2)}) collective-permute-start(bf16[256,1792]{1,0:T(8,128)(2,1)S(1)} %slice.377), channel_id=1, source_target_pairs={{0,1},{1,0},{2,3},{3,2},{4,5},{5,4},{6,7},{7,6},{8,9},{9,8},{10,11... | collective-permute-start | bytes 2752520 | tf_op jit(solution)/shard_map/ppermute | solution.py:29
  411.9 44.5 %collective-permute-start.22 = (bf16[256,1792]{1,0:T(8,128)(2,1)S(1)}, bf16[256,1792]{1,0:T(8,128)(2,1)S(1)}, u32[]{:S(2)}, u32[]{:S(2)}) collective-permute-start(bf16[256,1792]{1,0:T(8,128)(2,1)S(1)} %slice.373), channel_id=1, source_target_pairs={{0,1},{1,0},{2,3},{3,2},{4,5},{5,4},{6,7},{7,6},{8,9},{9,8},{10,11... | collective-permute-start | bytes 2752520 | tf_op jit(solution)/shard_map/ppermute | solution.py:29
  415.4 40.2 %collective-permute-start.21 = (bf16[256,1792]{1,0:T(8,128)(2,1)S(1)}, bf16[256,1792]{1,0:T(8,128)(2,1)S(1)}, u32[]{:S(2)}, u32[]{:S(2)}) collective-permute-start(bf16[256,1792]{1,0:T(8,128)(2,1)S(1)} %slice.368), channel_id=1, source_target_pairs={{0,1},{1,0},{2,3},{3,2},{4,5},{5,4},{6,7},{7,6},{8,9},{9,8},{10,11... | collective-permute-start | bytes 2752520 | tf_op jit(solution)/shard_map/ppermute | solution.py:29
  415.9 68.6 %collective-permute-start.20 = (bf16[256,1792]{1,0:T(8,128)(2,1)S(1)}, bf16[256,1792]{1,0:T(8,128)(2,1)S(1)}, u32[]{:S(2)}, u32[]{:S(2)}) collective-permute-start(bf16[256,1792]{1,0:T(8,128)(2,1)S(1)} %slice.365), channel_id=1, source_target_pairs={{0,1},{1,0},{2,3},{3,2},{4,5},{5,4},{6,7},{7,6},{8,9},{9,8},{10,11... | collective-permute-start | bytes 2752520 | tf_op jit(solution)/shard_map/ppermute | solution.py:29
  429.5 27.3 %collective-permute-start.41 = (bf16[256,1792]{1,0:T(8,128)(2,1)S(1)}, bf16[256,1792]{1,0:T(8,128)(2,1)S(1)}, u32[]{:S(2)}, u32[]{:S(2)}) collective-permute-start(bf16[256,1792]{1,0:T(8,128)(2,1)S(1)} %slice.401), channel_id=1, source_target_pairs={{0,1},{1,0},{2,3},{3,2},{4,5},{5,4},{6,7},{7,6},{8,9},{9,8},{10,11... | collective-permute-start | bytes 2752520 | tf_op jit(solution)/shard_map/ppermute | solution.py:29
  456.3 38.9 %collective-permute-start.36 = (bf16[256,1792]{1,0:T(8,128)(2,1)S(1)}, bf16[256,1792]{1,0:T(8,128)(2,1)S(1)}, u32[]{:S(2)}, u32[]{:S(2)}) collective-permute-start(bf16[256,1792]{1,0:T(8,128)(2,1)S(1)} %slice.386), channel_id=1, source_target_pairs={{0,1},{1,0},{2,3},{3,2},{4,5},{5,4},{6,7},{7,6},{8,9},{9,8},{10,11... | collective-permute-start | bytes 2752520 | tf_op jit(solution)/shard_map/ppermute | solution.py:29
  459.0 24.0 %collective-permute-start.39 = (bf16[128,1792]{1,0:T(8,128)(2,1)S(1)}, bf16[128,1792]{1,0:T(8,128)(2,1)S(1)}, u32[]{:S(2)}, u32[]{:S(2)}) collective-permute-start(bf16[128,1792]{1,0:T(8,128)(2,1)S(1)} %get-tuple-element.45), channel_id=1, source_target_pairs={{0,4},{4,0},{1,5},{5,1},{2,6},{6,2},{3,7},{7,3},{8,12},{12,8},{9,1... | collective-permute-start | bytes 1376264 | tf_op jit(solution)/shard_map/ppermute | solution.py:29
  471.2 28.5 %collective-permute-start.27 = (bf16[256,1792]{1,0:T(8,128)(2,1)S(1)}, bf16[256,1792]{1,0:T(8,128)(2,1)S(1)}, u32[]{:S(2)}, u32[]{:S(2)}) collective-permute-start(bf16[256,1792]{1,0:T(8,128)(2,1)S(1)} %pad_maximum_fusion.3), channel_id=1, source_target_pairs={{0,4},{4,0},{1,5},{5,1},{2,6},{6,2},{3,7},{7,3},{8,12},{12,8},{9,1... | collective-permute-start | bytes 2752520 | tf_op jit(solution)/shard_map/ppermute | solution.py:29
  482.3 23.3 %collective-permute-start.24 = (bf16[256,1792]{1,0:T(8,128)(2,1)S(1)}, bf16[256,1792]{1,0:T(8,128)(2,1)S(1)}, u32[]{:S(2)}, u32[]{:S(2)}) collective-permute-start(bf16[256,1792]{1,0:T(8,128)(2,1)S(1)} %pad_maximum_fusion.2), channel_id=1, source_target_pairs={{0,2},{2,0},{1,3},{3,1},{4,6},{6,4},{5,7},{7,5},{8,10},{10,8},{9,1... | collective-permute-start | bytes 2752520 | tf_op jit(solution)/shard_map/ppermute | solution.py:29
  483.1 35.8 %collective-permute-start.43 = (bf16[256,1792]{1,0:T(8,128)(2,1)S(1)}, bf16[256,1792]{1,0:T(8,128)(2,1)S(1)}, u32[]{:S(2)}, u32[]{:S(2)}) collective-permute-start(bf16[256,1792]{1,0:T(8,128)(2,1)S(1)} %pad_maximum_fusion.5), channel_id=1, source_target_pairs={{0,4},{4,0},{1,5},{5,1},{2,6},{6,2},{3,7},{7,3},{8,12},{12,8},{9,1... | collective-permute-start | bytes 2752520 | tf_op jit(solution)/shard_map/ppermute | solution.py:29
  484.5 38.1 %collective-permute-start.40 = (bf16[256,1792]{1,0:T(8,128)(2,1)S(1)}, bf16[256,1792]{1,0:T(8,128)(2,1)S(1)}, u32[]{:S(2)}, u32[]{:S(2)}) collective-permute-start(bf16[256,1792]{1,0:T(8,128)(2,1)S(1)} %pad_maximum_fusion.4), channel_id=1, source_target_pairs={{0,2},{2,0},{1,3},{3,1},{4,6},{6,4},{5,7},{7,5},{8,10},{10,8},{9,1... | collective-permute-start | bytes 2752520 | tf_op jit(solution)/shard_map/ppermute | solution.py:29
  528.0 53.9 %collective-permute-start.54 = (bf16[256,1792]{1,0:T(8,128)(2,1)}, bf16[256,1792]{1,0:T(8,128)(2,1)}, u32[]{:S(2)}, u32[]{:S(2)}) collective-permute-start(bf16[256,1792]{1,0:T(8,128)(2,1)} %get-tuple-element.26), channel_id=1, source_target_pairs={{0,2},{2,0},{1,3},{3,1},{4,6},{6,4},{5,7},{7,5},{8,10},{10,8},{9,1... | collective-permute-start | bytes 2752520 | tf_op jit(solution)/shard_map/ppermute | solution.py:29
  528.6 58.6 %collective-permute-start.53 = (bf16[256,1792]{1,0:T(8,128)(2,1)}, bf16[256,1792]{1,0:T(8,128)(2,1)}, u32[]{:S(2)}, u32[]{:S(2)}) collective-permute-start(bf16[256,1792]{1,0:T(8,128)(2,1)} %get-tuple-element.26), channel_id=1, source_target_pairs={{0,1},{1,0},{2,3},{3,2},{4,5},{5,4},{6,7},{7,6},{8,9},{9,8},{10,11... | collective-permute-start | bytes 2752520 | tf_op jit(solution)/shard_map/ppermute | solution.py:29
  528.6 55.9 %collective-permute-start.56 = (bf16[256,1792]{1,0:T(8,128)(2,1)}, bf16[256,1792]{1,0:T(8,128)(2,1)}, u32[]{:S(2)}, u32[]{:S(2)}) collective-permute-start(bf16[256,1792]{1,0:T(8,128)(2,1)} %get-tuple-element.26), channel_id=1, source_target_pairs={{0,4},{4,0},{1,5},{5,1},{2,6},{6,2},{3,7},{7,3},{8,12},{12,8},{9,1... | collective-permute-start | bytes 2752520 | tf_op jit(solution)/shard_map/ppermute | solution.py:29
  540.4 22.5 %all-to-all-start.3 = ((bf16[8,256,256]{2,1,0:T(8,128)(2,1)}), bf16[8,256,256]{2,1,0:T(8,128)(2,1)}, u32[]{:S(2)}, u32[]{:S(2)}) async-start(bf16[8,256,256]{2,1,0:T(8,128)(2,1)} %bitcast.215), calls=%async_computation.3 | async-start | bytes 2097152 | tf_op jit(solution)/shard_map/all_to_all | solution.py:356
  546.0 135.4 %reduce-scatter.12.cloned.1.call-start = ((), (), s32[]{:S(2)}) async-start(), calls=%async_computation.15 | async-start | bytes 5734400 | tf_op jit(solution)/shard_map/reduce_scatter | solution.py:338
  557.9 158.0 %reduce-scatter.10.cloned.1.call-start = ((), (), s32[]{:S(2)}) async-start(), calls=%async_computation.14 | async-start | bytes 4587520 | tf_op jit(solution)/shard_map/reduce_scatter | solution.py:372
  583.0 23.7 %collective-permute-start.59 = (bf16[128,1792]{1,0:T(8,128)(2,1)S(1)}, bf16[128,1792]{1,0:T(8,128)(2,1)S(1)}, u32[]{:S(2)}, u32[]{:S(2)}) collective-permute-start(bf16[128,1792]{1,0:T(8,128)(2,1)S(1)} %slice.424), channel_id=1, source_target_pairs={{0,4},{4,0},{1,5},{5,1},{2,6},{6,2},{3,7},{7,3},{8,12},{12,8},{9,1... | collective-permute-start | bytes 1376264 | tf_op jit(solution)/shard_map/ppermute | solution.py:29
  585.5 21.1 %collective-permute-start.58 = (bf16[128,1792]{1,0:T(8,128)(2,1)S(1)}, bf16[128,1792]{1,0:T(8,128)(2,1)S(1)}, u32[]{:S(2)}, u32[]{:S(2)}) collective-permute-start(bf16[128,1792]{1,0:T(8,128)(2,1)S(1)} %slice.423), channel_id=1, source_target_pairs={{0,2},{2,0},{1,3},{3,1},{4,6},{6,4},{5,7},{7,5},{8,10},{10,8},{9,1... | collective-permute-start | bytes 1376264 | tf_op jit(solution)/shard_map/ppermute | solution.py:29
  587.2 21.5 %collective-permute-start.57 = (bf16[256,1792]{1,0:T(8,128)(2,1)}, bf16[256,1792]{1,0:T(8,128)(2,1)S(1)}, u32[]{:S(2)}, u32[]{:S(2)}) collective-permute-start(bf16[256,1792]{1,0:T(8,128)(2,1)} %collective-permute-done.56), channel_id=1, source_target_pairs={{0,1},{1,0},{2,3},{3,2},{4,5},{5,4},{6,7},{7,6},{8,9},{9,8},{10,11... | collective-permute-start | bytes 2752520 | tf_op jit(solution)/shard_map/ppermute | solution.py:29
  606.6 23.4 %collective-permute-start.50 = (bf16[256,1792]{1,0:T(8,128)(2,1)}, bf16[256,1792]{1,0:T(8,128)(2,1)S(1)}, u32[]{:S(2)}, u32[]{:S(2)}) collective-permute-start(bf16[256,1792]{1,0:T(8,128)(2,1)} %slice.419), channel_id=1, source_target_pairs={{0,1},{1,0},{2,3},{3,2},{4,5},{5,4},{6,7},{7,6},{8,9},{9,8},{10,11... | collective-permute-start | bytes 2752520 | tf_op jit(solution)/shard_map/ppermute | solution.py:29
  625.9 22.4 %collective-permute-start.45 = (bf16[256,1792]{1,0:T(8,128)(2,1)}, bf16[256,1792]{1,0:T(8,128)(2,1)}, u32[]{:S(2)}, u32[]{:S(2)}) collective-permute-start(bf16[256,1792]{1,0:T(8,128)(2,1)} %slice.407), channel_id=1, source_target_pairs={{0,1},{1,0},{2,3},{3,2},{4,5},{5,4},{6,7},{7,6},{8,9},{9,8},{10,11... | collective-permute-start | bytes 2752520 | tf_op jit(solution)/shard_map/ppermute | solution.py:29
  644.7 21.8 %collective-permute-start.52 = (bf16[256,1792]{1,0:T(8,128)(2,1)}, bf16[256,1792]{1,0:T(8,128)(2,1)}, u32[]{:S(2)}, u32[]{:S(2)}) collective-permute-start(bf16[256,1792]{1,0:T(8,128)(2,1)} %pad_maximum_fusion.7), channel_id=1, source_target_pairs={{0,4},{4,0},{1,5},{5,1},{2,6},{6,2},{3,7},{7,3},{8,12},{12,8},{9,1... | collective-permute-start | bytes 2752520 | tf_op jit(solution)/shard_map/ppermute | solution.py:29
  647.4 21.6 %collective-permute-start.49 = (bf16[256,1792]{1,0:T(8,128)(2,1)}, bf16[256,1792]{1,0:T(8,128)(2,1)}, u32[]{:S(2)}, u32[]{:S(2)}) collective-permute-start(bf16[256,1792]{1,0:T(8,128)(2,1)} %pad_maximum_fusion.6), channel_id=1, source_target_pairs={{0,2},{2,0},{1,3},{3,1},{4,6},{6,4},{5,7},{7,5},{8,10},{10,8},{9,1... | collective-permute-start | bytes 2752520 | tf_op jit(solution)/shard_map/ppermute | solution.py:29
  717.0 32.7 %collective-permute-start.61 = (bf16[448,56]{0,1:T(8,128)(2,1)S(1)}, bf16[448,56]{0,1:T(8,128)(2,1)S(1)}, u32[]{:S(2)}, u32[]{:S(2)}) collective-permute-start(bf16[448,56]{0,1:T(8,128)(2,1)S(1)} %get-tuple-element.52), channel_id=1, source_target_pairs={{0,3},{1,7},{2,11},{3,15},{4,19},{5,23},{6,27},{7,31},{8,0},{9,4},... | collective-permute-start | bytes 150536 | tf_op jit(solution)/shard_map/ppermute | solution.py:394
  735.6 21.0 %all-to-all-start.5 = ((bf16[8,56,768]{2,1,0:T(8,128)(2,1)}), bf16[8,56,768]{2,1,0:T(8,128)(2,1)S(1)}, u32[]{:S(2)}, u32[]{:S(2)}) async-start(bf16[8,56,768]{2,1,0:T(8,128)(2,1)} %bitcast.64), calls=%async_computation.5 | async-start | bytes 1376256 | tf_op jit(solution)/shard_map/all_to_all | solution.py:382
  (69 other events, 921.3 us)
Sparse Core Ops, SparseCore 0:
  10.9 85.9 all-gather.3
  98.5 104.4 all-gather.5
  204.5 60.9 all-gather.7
  406.1 43.8 reduce-scatter.7
  558.0 85.4 reduce-scatter.11
  645.7 70.1 reduce-scatter.9

commit v2 on v1

--- a/solution.py
+++ b/solution.py
@@ -44,6 +44,10 @@
     return lax.dot_general(left, right, dims, preferred_element_type=F32)
 
 
+def after(value, *others):
+    return lax.optimization_barrier((value, *others))[0]
+
+
 def plane_gather(own):
     half = own.shape[0] // 2
     from_x = swap(own, "x")
@@ -52,7 +56,7 @@
     second = swap(from_x[half:], "y")
     mine = [own, from_x, from_y, jnp.concatenate([first, second], axis=0)]
     other = [swap(block, "c") for block in mine]
-    return jnp.stack([block for pair in zip(mine, other) for block in pair])
+    return [block for pair in zip(mine, other) for block in pair]
 
 
 def plane_sum(parts):
@@ -66,7 +70,21 @@
     along_x = jnp.concatenate([along_x[:half], along_x[half:] + second.astype(F32)], axis=0)
     got_x = swap(along_x.astype(BF), "x")
     got_y = swap(along_y.astype(BF), "y")
+    return here, got_x, got_y
+
+
+def total(terms):
+    here, got_x, got_y = terms
     return here + got_x.astype(F32) + got_y.astype(F32)
+
+
+def placed(pieces):
+    count = len(pieces)
+    me = lax.axis_index("z")
+    whole = jnp.zeros((count, *pieces[0].shape), pieces[0].dtype)
+    for k, piece in enumerate(pieces):
+        whole = lax.dynamic_update_index_in_dim(whole, piece, (me - k) % count, 0)
+    return whole.reshape(-1, *pieces[0].shape[1:])
 
 
 def ring_gather(block, count):
@@ -74,9 +92,262 @@
     held = [block]
     for _ in range(count - 1):
         held.append(lax.ppermute(held[-1], "z", route))
-    me = lax.axis_index("z")
-    stacked = jnp.stack(held[::-1])
-    return jnp.roll(stacked, me + 1, axis=0)
+    return held
+
+
+def direct_gather(block, count):
+    return [block] + [
+        lax.ppermute(block, "z", [(i, (i + k) % count) for i in range(count)])
+        for k in range(1, count)
+    ]
+
+
+def head_sheet_kernel(query_ref, key_ref, value_ref, out_ref):
+    rows = query_ref.shape[0]
+    blank = jnp.zeros((rows, HP - HD), BF)
+    for i, ref in enumerate((query_ref, key_ref, value_ref)):
+        for h in range(H):
+            head = jnp.concatenate([ref[:, h * HD : (h + 1) * HD], blank], axis=1)
+            lo = (2 * i + h % 2) * HP
+            out_ref[h // 2, :, lo : lo + HP] = head
+
+
+def head_sheet(query, key, value):
+    return pl.pallas_call(
+        head_sheet_kernel,
+        out_shape=jax.ShapeDtypeStruct((8, query.shape[0], 6 * HP), BF),
+        compiler_params=pltpu.CompilerParams(vmem_limit_bytes=32 * 2**20),
+    )(query, key, value)
+
+
+def unit_sheet_kernel(layers, part, gate_ref, up_ref, out_ref):
+    for w, ref in enumerate((gate_ref, up_ref)):
+        for p in range(8):
+            pieces = [
+                ref[:, (8 * z + p) * part : (8 * z + p + 1) * part] for z in range(layers)
+            ]
+            lo = w * layers * part
+            out_ref[p, :, lo : lo + layers * part] = jnp.concatenate(pieces, axis=1)
+
+
+def unit_sheet(gate, up, layers, part):
+    return pl.pallas_call(
+        functools.partial(unit_sheet_kernel, layers, part),
+        out_shape=jax.ShapeDtypeStruct((8, gate.shape[0], 2 * layers * part), BF),
+        compiler_params=pltpu.CompilerParams(vmem_limit_bytes=32 * 2**20),
+    )(gate, up)
+
+
+def head_owner_kernel(sheet_ref, query_ref, key_ref, value_ref):
+    for i, ref in enumerate((query_ref, key_ref, value_ref)):
+        for h in range(H):
+            lo = (2 * i + h % 2) * HP
+            ref[:, h * HD : (h + 1) * HD] = sheet_ref[h // 2, :, lo : lo + HD].astype(F32)
+
+
+def head_owner(sheet):
+    shape = jax.ShapeDtypeStruct((sheet.shape[1], H * HD), F32)
+    return pl.pallas_call(
+        head_owner_kernel,
+        out_shape=[shape, shape, shape],
+        compiler_params=pltpu.CompilerParams(vmem_limit_bytes=32 * 2**20),
+    )(sheet)
+
+
+def unit_owner_kernel(layers, part, sheet_ref, gate_ref, up_ref):
+    for w, ref in enumerate((gate_ref, up_ref)):
+        for z in range(layers):
+            lo = (w * layers + z) * part
+            pieces = [sheet_ref[p, :, lo : lo + part].astype(F32) for p in range(8)]
+            ref[:, 8 * z * part : 8 * (z + 1) * part] = jnp.concatenate(pieces, axis=1)
+
+
+def unit_owner(sheet, layers, part):
+    shape = jax.ShapeDtypeStruct((sheet.shape[1], 8 * layers * part), F32)
+    return pl.pallas_call(
+        functools.partial(unit_owner_kernel, layers, part),
+        out_shape=[shape, shape],
+        compiler_params=pltpu.CompilerParams(vmem_limit_bytes=32 * 2**20),
+    )(sheet)
+
+
+def project_kernel(mixed_ref, weight_ref, input_ref, gain_ref, middle_ref, hidden_ref):
+    step = pl.program_id(0)
+
+    @pl.when(step == 0)
+    def _():
+        middle_ref[...] = input_ref[...].astype(F32)
+
+    middle_ref[...] += jnp.dot(mixed_ref[...], weight_ref[...], preferred_element_type=F32)
+
+    @pl.when(step == pl.num_programs(0) - 1)
+    def _():
+        normed, _ = normalize(middle_ref[...])
+        hidden_ref[...] = (normed * gain_ref[...]).astype(BF)
+
+
+def project(mixed, weight, own, gain):
+    count, rows, depth = mixed.shape
+    width = own.shape[1]
+    whole = lambda p: (0, 0)
+    return pl.pallas_call(
+        project_kernel,
+        grid=(count,),
+        in_specs=[
+            pl.BlockSpec((None, rows, depth), lambda p: (p, 0, 0)),
+            pl.BlockSpec((depth, width), lambda p: (p, 0)),
+            pl.BlockSpec((rows, width), whole),
+            pl.BlockSpec((1, width), whole),
+        ],
+        out_specs=[pl.BlockSpec((rows, width), whole), pl.BlockSpec((rows, width), whole)],
+        out_shape=[
+            jax.ShapeDtypeStruct((rows, width), F32),
+            jax.ShapeDtypeStruct((rows, width), BF),
+        ],
+        compiler_params=pltpu.CompilerParams(vmem_limit_bytes=32 * 2**20),
+    )(mixed, weight, own, gain)
+
+
+def unproject_kernel(
+    here_ref, x_ref, y_ref, middle_ref, top_ref, gain_ref, weight_ref, out_ref, grad_ref, branch_ref, gain_grad_ref
+):
+    @pl.when(pl.program_id(0) == 0)
+    def _():
+        grad_hidden = here_ref[...] + x_ref[...].astype(F32) + y_ref[...].astype(F32)
+        normed, factor = normalize(middle_ref[...])
+        gain_grad_ref[...] = jnp.sum(grad_hidden * normed, axis=0, keepdims=True)
+        grad = top_ref[...].astype(F32) + norm_back(grad_hidden * gain_ref[...], normed, factor)
+        grad_ref[...] = grad
+        branch_ref[...] = grad.astype(BF)
+
+    out_ref[...] = lax.dot_general(
+        branch_ref[...], weight_ref[...], NT, preferred_element_type=F32
+    ).astype(BF)
+
+
+def unproject(terms, middle, top, gain, weight):
+    rows, width = middle.shape
+    depth = weight.shape[0] // 8
+    full = pl.BlockSpec((rows, width), lambda p: (0, 0))
+    line = pl.BlockSpec((1, width), lambda p: (0, 0))
+    return pl.pallas_call(
+        unproject_kernel,
+        grid=(8,),
+        in_specs=[full] * 5 + [line, pl.BlockSpec((depth, width), lambda p: (p, 0))],
+        out_specs=[pl.BlockSpec((None, rows, depth), lambda p: (p, 0, 0)), full, full, line],
+        out_shape=[
+            jax.ShapeDtypeStruct((8, rows, depth), BF),
+            jax.ShapeDtypeStruct((rows, width), F32),
+            jax.ShapeDtypeStruct((rows, width), BF),
+            jax.ShapeDtypeStruct((1, width), F32),
+        ],
+        compiler_params=pltpu.CompilerParams(vmem_limit_bytes=48 * 2**20),
+    )(*terms, middle, top, gain, weight)
+
+
+def ffn_kernel(count, kept, *refs):
+    blocks, refs = refs[:count], refs[count:]
+    top_ref, gate_up_ref, down_ref, refs = *refs[:3], refs[3 + kept :]
+    inner_ref, grads_ref, hidden_ref, back_ref, out_ref = refs
+    for j, ref in enumerate(blocks):
+
+        @pl.when(pl.program_id(0) == j)
+        def _():
+            hidden_ref[...] = ref[...]
+
+    units = down_ref.shape[0]
+    both = jnp.dot(hidden_ref[...], gate_up_ref[...], preferred_element_type=F32)
+    grad_inner = lax.dot_general(top_ref[...], down_ref[...], NT, preferred_element_type=F32)
+    gate, upper = both[:, :units], both[:, units:]
+    sigma = jax.nn.sigmoid(gate)
+    activ = gate * sigma
+    inner = (activ * upper).astype(BF)
+    inner_ref[...] = inner
+    grad_upper = grad_inner * activ
+    grad_gate = grad_inner * upper * sigma * (1.0 + gate * (1.0 - sigma))
+    grads = jnp.concatenate([grad_gate, grad_upper], axis=1).astype(BF)
+    grads_ref[...] = grads
+    back_ref[...] = lax.dot_general(
+        grads, gate_up_ref[...], NT, preferred_element_type=F32
+    ).astype(BF)
+    out_ref[...] = jnp.dot(inner, down_ref[...], preferred_element_type=F32).astype(BF)
+
+
+def ffn(blocks, tops, gate_up, down, first, carried=()):
+    count = len(blocks)
+    rows, width = blocks[0].shape
+    units = down.shape[0]
+    whole = lambda i: (0, 0)
+    tile = lambda columns: pl.BlockSpec((rows, columns), lambda i: (i + first, 0))
+    part = pl.BlockSpec((None, rows, width), lambda i: (i, 0, 0))
+    stacked = lambda columns: jax.ShapeDtypeStruct((8 * rows, columns), BF)
+    return pl.pallas_call(
+        functools.partial(ffn_kernel, count, len(carried)),
+        grid=(count,),
+        in_specs=[pl.BlockSpec((rows, width), whole)] * count
+        + [
+            tile(width),
+            pl.BlockSpec((width, 2 * units), whole),
+            pl.BlockSpec((units, width), whole),
+        ]
+        + [pl.BlockSpec(memory_space=pl.ANY)] * len(carried),
+        out_specs=[tile(units), tile(2 * units), tile(width), part, part],
+        out_shape=[
+            stacked(units),
+            stacked(2 * units),
+            stacked(width),
+            jax.ShapeDtypeStruct((count, rows, width), BF),
+            jax.ShapeDtypeStruct((count, rows, width), BF),
+        ],
+        input_output_aliases={count + 3 + i: i for i in range(len(carried))},
+        compiler_params=pltpu.CompilerParams(vmem_limit_bytes=56 * 2**20),
+    )(*blocks, tops, gate_up, down, *carried)
+
+
+def outer_kernel(*refs):
+    *blocks, right_ref, out_ref = refs
+    sums = [
+        lax.dot_general(ref[...], right_ref[i], TN, preferred_element_type=F32)
+        for i, ref in enumerate(blocks)
+    ]
+    out_ref[...] = functools.reduce(jnp.add, sums).astype(BF)
+
+
+def outer(blocks, right):
+    rows, width = blocks[0].shape
+    count, _, depth = right.shape
+    tile = 256
+    return pl.pallas_call(
+        outer_kernel,
+        grid=(width // tile,),
+        in_specs=[pl.BlockSpec((rows, tile), lambda i: (0, i))] * count
+        + [pl.BlockSpec((count, rows, depth), lambda i: (0, 0, 0))],
+        out_specs=pl.BlockSpec((tile, depth), lambda i: (i, 0)),
+        out_shape=jax.ShapeDtypeStruct((width, depth), BF),
+        compiler_params=pltpu.CompilerParams(vmem_limit_bytes=32 * 2**20),
+    )(*blocks, right)
+
+
+def mend_kernel(info_ref, tail_ref, back_ref, cur_ref, out_ref):
+    out_ref[:, : 2 * HP] = cur_ref[:, : 2 * HP]
+    out_ref[:, 2 * HP :] = (tail_ref[...] + back_ref[...].astype(F32)).astype(BF)
+
+
+def mend(info, tail, back, grad_qkv):
+    rows, blocks = grad_qkv.shape[1], grad_qkv.shape[0] // 2
+    side = pl.BlockSpec((None, WINDOW, 4 * HP), lambda s, info: (s, 0, 0))
+    edge = pl.BlockSpec(
+        (None, WINDOW, 6 * HP),
+        lambda s, info: (2 * ((blocks - 1) ^ info[0]) + s, rows // WINDOW - 1, 0),
+    )
+    return pl.pallas_call(
+        mend_kernel,
+        grid_spec=pltpu.PrefetchScalarGridSpec(
+            num_scalar_prefetch=1, grid=(2,), in_specs=[side, side, edge], out_specs=edge
+        ),
+        out_shape=jax.ShapeDtypeStruct(grad_qkv.shape, BF),
+        input_output_aliases={3: 0},
+    )(info, tail, back, grad_qkv)
 
 
 def shares_of(query, keys, cut, offset):
@@ -240,12 +511,6 @@
     )(info, qkv, qkv, halo, top)
 
 
-def padded_heads(block):
-    rows = block.shape[0]
-    wide = jnp.pad(block.reshape(rows, H, HD), ((0, 0), (0, 0), (0, HP - HD)))
-    return wide.reshape(rows, 8, 2 * HP)
-
-
 def body(
     inputs,
     starts,
@@ -271,120 +536,91 @@
     me_block = 2 * lax.axis_index("y") + lax.axis_index("x")
     me_core = lax.axis_index("c")
 
-    streams = plane_gather(inputs[0])
-    sheet = jnp.concatenate(
-        [
-            padded_heads(query_weight),
-            padded_heads(key_weight),
-            padded_heads(value_weight),
-            gate_weight.reshape(share, layers, 8, part).swapaxes(1, 2).reshape(share, 8, units),
-            up_weight.reshape(share, layers, 8, part).swapaxes(1, 2).reshape(share, 8, units),
-        ],
-        axis=2,
-    ).swapaxes(0, 1)
-    sheet = lax.all_to_all(sheet, PLANE, 0, 0, tiled=True).reshape(8 * share, -1)
-    small = jnp.concatenate(
-        [attn_gain, ffn_gain, starts[0].astype(BF)], axis=0
-    )
+    own = inputs[0]
+    top = cotangent[0]
+    streams = plane_gather(own)
+    heads = head_sheet(query_weight, key_weight, value_weight)
+    heads = lax.all_to_all(heads, PLANE, 0, 0, tiled=True).reshape(8 * share, 6 * HP)
+    qkv_pieces = ring_gather(heads, layers)
+    qkv_weight = placed(qkv_pieces)
+    small = jnp.concatenate([attn_gain, ffn_gain, starts[0].astype(BF)], axis=0)
     small = jnp.pad(small, (0, 128 - small.shape[0]))
-    small = lax.all_to_all(jnp.broadcast_to(small, (devices, 128)), ALL, 0, 0, tiled=True)
-    gain_attn = small[:, :share].reshape(width)
-    gain_ffn = small[:, share : 2 * share].reshape(width)
+    small = after(jnp.broadcast_to(small, (devices, 128)), heads)
+    small = lax.all_to_all(small, ALL, 0, 0, tiled=True)
+    gain_attn = small[:, :share].reshape(1, width).astype(F32)
+    gain_ffn = small[:, share : 2 * share].reshape(1, width).astype(F32)
     opened = lax.dynamic_slice(small, (8 * me_z, 2 * share), (2, 1))[:, 0].astype(jnp.int32)
     opened = jnp.where(me_core == 0, opened, opened[::-1])
     info = jnp.concatenate([jnp.stack([me_block, me_core]).astype(jnp.int32), opened])
+    sheet = after(unit_sheet(gate_weight, up_weight, layers, part), small)
+    sheet = lax.all_to_all(sheet, PLANE, 0, 0, tiled=True).reshape(8 * share, 2 * units)
 
     full_out = lax.all_gather(out_weight, ALL, axis=0, tiled=True)
-    down = lax.all_gather(down_weight, "z", axis=0, tiled=True)
-    qkv_weight = ring_gather(sheet[:, : 6 * HP], layers).reshape(width, 6 * HP)
-    gate_up = lax.all_gather(sheet[:, 6 * HP :], "z", axis=0, tiled=True)
-    tops = plane_gather(cotangent[0]).reshape(8 * rows, width)
-
-    stream = streams.reshape(8 * rows, width).astype(F32)
+    full_out = jnp.pad(full_out.reshape(H, HD, width), ((0, 0), (0, HP - HD), (0, 0)))
+    full_out = full_out.reshape(H * HP, width)
+    gate_up = lax.all_gather(sheet, "z", axis=0, tiled=True)
+    down = placed(direct_gather(after(down_weight, qkv_pieces[-1]), layers))
+    tops = plane_gather(after(top, streams[6]))
+    tops = jnp.concatenate(tops[:4] + tops[6:] + tops[4:6], axis=0)
+
+    stream = jnp.concatenate(streams, axis=0).astype(F32)
     hidden1 = (normalize(stream)[0] * gain_attn).astype(BF)
     qkv = dot(hidden1, qkv_weight).astype(BF).reshape(8, rows, 6 * HP)
     last = 2 * (3 ^ me_block)
-    rim = lax.dynamic_slice(
-        qkv, (last, rows - WINDOW, 2 * HP), (2, WINDOW, 4 * HP)
-    )
+    rim = lax.dynamic_slice(qkv, (last, rows - WINDOW, 2 * HP), (2, WINDOW, 4 * HP))
     halo = lax.ppermute(rim, "z", [(i, i + 1) for i in range(layers - 1)])
     flat, kept = attend(qkv, halo, info)
     mixed = lax.all_to_all(flat, PLANE, 0, 0, tiled=True)
-    mixed = mixed.reshape(8, rows, 2, HP)[..., :HD].transpose(1, 0, 2, 3).reshape(rows, H * HD)
-    middle = inputs[0].astype(F32) + dot(mixed, full_out)
-
-    normed2, rscale2 = normalize(middle)
-    hidden2 = plane_gather((normed2 * gain_ffn).astype(BF)).reshape(8 * rows, width)
-    gate = dot(hidden2, gate_up[:, :units])
-    upper = dot(hidden2, gate_up[:, units:])
-    sigma = jax.nn.sigmoid(gate)
-    activ = gate * sigma
-    inner = (activ * upper).astype(BF)
-    grad_inner = dot(tops, down, NT)
-    grad_upper = (grad_inner * activ).astype(BF)
-    grad_gate = (grad_inner * upper * sigma * (1.0 + gate * (1.0 - sigma))).astype(BF)
-    parts = []
-    for r in range(4):
-        at = slice(2 * r * rows, 2 * (r + 1) * rows)
-        part_sum = dot(grad_gate[at], gate_up[:, :units], NT) + dot(
-            grad_upper[at], gate_up[:, units:], NT
-        )
-        part_sum = part_sum.astype(BF)
-        parts.append((part_sum[:rows], part_sum[rows:]))
-    grad_hidden2 = plane_sum(parts)
+    middle, hidden2 = project(mixed, full_out, own, gain_ffn)
+
+    hidden2 = plane_gather(hidden2)
+    *carried, back_near, out_near = ffn(hidden2[:4], tops, gate_up, down, 0)
+    inner, grads, hidden2, back_far, out_far = ffn(
+        hidden2[6:] + hidden2[4:6], tops, gate_up, down, 4, carried
+    )
+    pairs = lambda near, far: [
+        (near[0], near[1]), (near[2], near[3]), (far[2], far[3]), (far[0], far[1])
+    ]
+    terms = plane_sum(pairs(back_near, back_far))
     down_sum = lax.psum_scatter(
         dot(inner, tops, TN).astype(BF), "z", scatter_dimension=0, tiled=True
     )
     gate_up_sum = lax.psum_scatter(
-        jnp.concatenate([dot(hidden2, grad_gate, TN), dot(hidden2, grad_upper, TN)], axis=1).astype(BF),
-        "z",
-        scatter_dimension=0,
-        tiled=True,
-    )
-    parts = []
-    for r in range(4):
-        at = slice(2 * r * rows, 2 * (r + 1) * rows)
-        part_sum = dot(inner[at], down).astype(BF)
-        parts.append((part_sum[:rows], part_sum[rows:]))
-    layer_out = (middle + plane_sum(parts)).astype(BF)
-
-    ffn_gain_local = jnp.sum(grad_hidden2 * normed2, axis=0)
-    grad_middle = cotangent[0].astype(F32) + norm_back(grad_hidden2 * gain_ffn, normed2, rscale2)
-    grad_branch = grad_middle.astype(BF)
-
-    grad_mixed = padded_heads(dot(grad_branch, full_out, NT).astype(BF)).swapaxes(0, 1)
+        dot(hidden2, grads, TN).astype(BF), "z", scatter_dimension=0, tiled=True
+    )
+
+    grad_mixed, grad_middle, grad_branch, ffn_gain_local = unproject(
+        terms, middle, top, gain_ffn, full_out
+    )
     grad_mixed = lax.all_to_all(grad_mixed, PLANE, 0, 0, tiled=True)
-    branches = plane_gather(grad_branch).reshape(8 * rows, width)
+    branches = plane_gather(after(grad_branch, grad_mixed))
+    out_near, out_far, _ = lax.optimization_barrier((out_near, out_far, branches[6]))
+    out_terms = plane_sum(pairs(out_near, out_far))
+    layer_out = (middle + total(out_terms)).astype(BF)
     grad_qkv, tail, lead = attend_back(qkv, halo, grad_mixed, info)
     back = lax.ppermute(lead, "z", [(i + 1, i) for i in range(layers - 1)])
-    grad_qkv = lax.dynamic_update_slice(
-        grad_qkv, (tail + back.astype(F32)).astype(BF), (last, rows - WINDOW, 2 * HP)
-    ).reshape(8 * rows, 6 * HP)
+    grad_qkv = mend(info, tail, back, grad_qkv).reshape(8 * rows, 6 * HP)
     parts = []
     for r in range(4):
         at = slice(2 * r * rows, 2 * (r + 1) * rows)
         part_sum = dot(grad_qkv[at], qkv_weight, NT).astype(BF)
         parts.append((part_sum[:rows], part_sum[rows:]))
-    grad_hidden1 = plane_sum(parts)
-    attn_sums = jnp.concatenate(
-        [dot(hidden1, grad_qkv, TN), dot(branches, kept.reshape(8 * rows, 2 * HP), TN)], axis=1
-    ).astype(BF)
-    attn_sums = lax.psum_scatter(attn_sums, "z", scatter_dimension=0, tiled=True)
-    normed1, rscale1 = normalize(inputs[0].astype(F32))
+    grad_hidden1 = total(plane_sum(parts))
+    out_sum = lax.psum_scatter(outer(branches, kept), "z", scatter_dimension=0, tiled=True)
+    qkv_sum = lax.psum_scatter(
+        dot(hidden1, grad_qkv, TN).astype(BF), "z", scatter_dimension=0, tiled=True
+    )
+    normed1, rscale1 = normalize(own.astype(F32))
     attn_gain_local = jnp.sum(grad_hidden1 * normed1, axis=0)
     input_grad = grad_middle + norm_back(grad_hidden1 * gain_attn, normed1, rscale1)
 
     gate_up_sum = lax.all_to_all(
         gate_up_sum.reshape(8, share, 2 * units), PLANE, 0, 0, tiled=True
-    ).astype(F32)
-    gate_up_sum = gate_up_sum.reshape(8, share, 2, layers, part).transpose(2, 1, 3, 0, 4)
-    gate_grad, up_grad = gate_up_sum.reshape(2, share, hidden_units)
-    qkv_sum = lax.all_to_all(
-        attn_sums[:, : 6 * HP].reshape(8, share, 6 * HP), PLANE, 0, 0, tiled=True
-    ).astype(F32)
-    qkv_sum = qkv_sum.reshape(8, share, 3, 2, HP)[..., :HD].transpose(2, 1, 0, 3, 4)
-    query_grad, key_grad, value_grad = qkv_sum.reshape(3, share, width)
-    out_sum = attn_sums[:, 6 * HP :].reshape(-1, 2, HP)[..., :HD].reshape(-1, layers, share)
+    )
+    gate_grad, up_grad = unit_owner(gate_up_sum, layers, part)
+    qkv_sum = lax.all_to_all(qkv_sum.reshape(8, share, 6 * HP), PLANE, 0, 0, tiled=True)
+    query_grad, key_grad, value_grad = head_owner(qkv_sum)
+    out_sum = out_sum.reshape(-1, 2, HP)[..., :HD].reshape(-1, layers, share)
     pieces = []
     for j in range(layers):
         route = [
@@ -395,7 +631,7 @@
     rank = 8 * me_z + 2 * me_block + me_core
     turned = jnp.roll(jnp.stack(pieces[::-1]), rank % layers + 1, axis=0)
     output_grad = turned.reshape(width, share).T.astype(F32)
-    gains = jnp.stack([attn_gain_local, ffn_gain_local]).reshape(2, devices, share).swapaxes(0, 1)
+    gains = jnp.stack([attn_gain_local, ffn_gain_local[0]]).reshape(2, devices, share).swapaxes(0, 1)
     gains = jnp.sum(lax.all_to_all(gains, ALL, 0, 0, tiled=True), axis=0)
     return (
         layer_out[None],

time: 783 us -> 709 us (0.905)
  matrix products: 135 us -> 52.9 us
  Pallas kernels: 28.3 us -> 107 us
  waiting for transfers between devices: 308 us -> 253 us
  starting transfers between devices: 84.5 us -> 120 us
  local copies, waits for them, and re-layouts: 130 us -> 97.8 us
  blocking collectives: 31.9 us -> 17.8 us
    ppermute x3, waiting for transfers between devices: 104 us -> 10.8 us  [ring_gather(): held.append(lax.ppermute(held[-1], 'z', route))]
    dot_general x27 -> x8, matrix products: 135 us -> 52.9 us  [dot(): return lax.dot_general(left, right, dims, preferred_element_type=F32)]
    pallas_call x0 -> x10, Pallas kernels: none -> 80.1 us  [the longest x2 44.5 us: ffn(): pl.pallas_call(functools.partial(ffn_kernel, count, len(carried)), grid=(...]
    ppermute x0 -> x3, waiting for transfers between devices: none -> 23.3 us  [direct_gather(): lax.ppermute(block, 'z', [(i, (i + k) % count) for i in range(count)])]
    another operation x18 -> x2, local copies, waits for them, and re-layouts: 22.6 us -> 0.17 us  [body(): jnp.stack([attn_gain_local, ffn_gain_local[0]]).reshape(2, devices, share)]
    all_to_all x3 -> x4, waiting for transfers between devices: 46.5 us -> 31.4 us  [the longest x1 16.1 us: body(): lax.all_to_all(heads, PLANE, 0, 0, tiled=True).reshape(8 * share, 6 * HP)]
    reshape x15 -> x1, local copies, waits for them, and re-layouts: 15.9 us -> 1.07 us  [body(): out_sum = out_sum.reshape(-1, 2, HP)[..., :HD].reshape(-1, layers, share)]
    all_to_all x1, blocking collectives: 31.9 us -> 17.8 us  [body(): grad_mixed = lax.all_to_all(grad_mixed, PLANE, 0, 0, tiled=True)]
  transfers between devices with their start and end apart: 77 -> 81, of which waited for: 30 -> 31; matrix products, arithmetic and copies ran while one was open for 34% -> 23% of each run, Pallas kernels for 4% -> 12%
where the time goes in v2:
time: 709 us; the launch traced here: 696 us
  waiting for transfers between devices  253 us (36%)
  starting transfers between devices  120 us (17%)
  Pallas kernels  107 us (15%)
  local copies, waits for them, and re-layouts  97.8 us (14%)
  matrix products  52.9 us (7%)
  other arithmetic  31.5 us (4%)
  blocking collectives  17.8 us (3%)
  between operations  16.3 us (2%)
    ppermute x56, waiting for transfers between devices, swap(): return lax.ppermute(block, axis, SWAP)  130 us
    dot_general x8, matrix products, dot(): return lax.dot_general(left, right, dims, preferred_element_type=F32)  52.9 us
    unnamed x117, local copies, waits for them, and re-layouts  44.8 us
    pallas_call x2, Pallas kernels, ffn(): pl.pallas_call(functools.partial(ffn_kernel, count, len(carried)), grid=(...  44.5 us
    ppermute x56, starting transfers between devices, swap(): return lax.ppermute(block, axis, SWAP)  38.1 us
    ppermute x3, waiting for transfers between devices, direct_gather(): lax.ppermute(block, 'z', [(i, (i + k) % count) for i in range(count)])  23.3 us
    all_to_all x1, blocking collectives, body(): grad_mixed = lax.all_to_all(grad_mixed, PLANE, 0, 0, tiled=True)  17.8 us
    ppermute x4, waiting for transfers between devices, body(): pieces.append(lax.ppermute(piece, ALL, route))  17.1 us
  transfers between devices with their start and end apart: 81, of which 31 were waited for; matrix products, arithmetic and copies ran while one was open for 23% of the time, Pallas kernels for 12%

profile of v2, /device:TPU:26, one launch (start us, length us, event | category | flops | bytes accessed | tf_op | source)
XLA Modules:
  0.0 696.3 jit_solution(6337181053188481031)
XLA Ops:
  14.1 5.1 all-to-all-start
  23.2 16.1 %all-to-all-done = bf16[8,56,768]{2,1,0:T(8,128)(2,1)S(1)} async-done(((bf16[8,56,768]{2,1,0:T(8,128)(2,1)}), bf16[8,56,768]{2,1,0:T(8,128)(2,1)S(1)}, u32[]{:S(2)}, u32[]{:S(2)}) %all-to-all-start) | async-done | bytes 688160 | tf_op jit(solution)/shard_map/all_to_all | solution.py:543
  40.1 6.5 all-to-all-start.1
  49.3 15.3 %all-to-all-done.1 = bf16[32,1,128]{2,1,0:T(2,128)(2,1)S(1)} async-done(((bf16[32,1,128]{2,1,0:T(2,128)(2,1)}), bf16[32,1,128]{2,1,0:T(2,128)(2,1)S(1)}, u32[]{:S(2)}, u32[]{:S(2)}) %all-to-all-start.1) | async-done | bytes 8224 | tf_op jit(solution)/shard_map/all_to_all | solution.py:549
  65.2 5.0 all-to-all-start.3
  87.4 16.0 %collective-permute-done.5 = bf16[128,1792]{1,0:T(8,128)(2,1)S(1)} collective-permute-done((bf16[128,1792]{1,0:T(8,128)(2,1)S(1)}, bf16[128,1792]{1,0:T(8,128)(2,1)S(1)}, u32[]{:S(2)}, u32[]{:S(2)}) %collective-permute-start.5) | collective-permute-done | bytes 458784 | tf_op jit(solution)/shard_map/ppermute | solution.py:29
  115.3 10.8 %collective-permute-done.10 = bf16[448,768]{1,0:T(8,128)(2,1)} collective-permute-done((bf16[448,768]{1,0:T(8,128)(2,1)}, bf16[448,768]{1,0:T(8,128)(2,1)}, u32[]{:S(2)}, u32[]{:S(2)}) %collective-permute-start.10) | collective-permute-done | bytes 688160 | tf_op jit(solution)/shard_map/ppermute | solution.py:94
  129.6 4.8 fusion
  134.9 7.9 %convolution_convert_fusion.2 = bf16[2048,768]{1,0:T(8,128)(2,1)S(1)} fusion(bf16[1792,768]{1,0:T(8,128)(2,1)} %bitcast.10, bf16[2048,1792]{1,0:T(8,128)(2,1)S(1)} %copy-done.19, f32[1792]{0:T(1024)S(1)} %reshape.151, f32[2048]{0:T(1024)S(1)} %add_rsqrt_fusion), kind=kOutput, calls=%fused_computation.7 | convolution fusion | flops 5653397504 | bytes 13253632 | tf_op jit(solution)/shard_map/dot_general | solution.py:44
  147.6 5.3 collective-permute-start.24
  157.4 13.5 %collective-permute-done.11.halo_ref = bf16[2,64,512]{2,1,0:T(8,128)(2,1)S(1)} collective-permute-done((bf16[2,64,512]{2,1,0:T(8,128)(2,1)S(1)}, bf16[2,64,512]{2,1,0:T(8,128)(2,1)S(1)}, u32[]{:S(2)}, u32[]{:S(2)}) %collective-permute-start.11) | collective-permute-done | bytes 131104 | tf_op jit(solution)/shard_map/ppermute | solution.py:571
  173.5 10.6 %shard_map.204 = (bf16[8,256,256]{2,1,0:T(8,128)(2,1)S(1)}, bf16[8,256,256]{2,1,0:T(8,128)(2,1)S(1)}) custom-call(s32[4]{0:T(128)S(1)} %pad_add_fusion.info_ref, bf16[8,256,768]{2,1,0:T(8,128)(2,1)S(1)} %bitcast.138, bf16[8,256,768]{2,1,0:T(8,128)(2,1)S(1)} %bitcast.139, bf16[2,64,512]{2,1,0:T(8,128)(2,1)S(1)} %collective-permute-done.11.halo_ref), custom_call_target="tpu_custom_call" | custom-call | tf_op jit(solution)/shard_map/pallas_call | solution.py:409
  186.0 4.2 all-to-all-start.2
  198.5 6.6 pad.9
  209.4 7.2 %shard_map.205 = (f32[256,1792]{1,0:T(8,128)S(1)}, bf16[256,1792]{1,0:T(8,128)(2,1)}) custom-call(bf16[8,256,256]{2,1,0:T(8,128)(2,1)} %all-to-all-done.2.mixed_ref, bf16[2048,1792]{1,0:T(8,128)(2,1)S(1)} %bitcast.136, bf16[256,1792]{1,0:T(8,128)(2,1)S(1)} %bitcast.145, f32[1,1792]{1,0:T(1,128)S(1)} %reshape.152.gain_ref), custom_call_target="tpu_custom_call" | custom-call | tf_op jit(solution)/shard_map/pallas_call | solution.py:193
  216.5 23.3 %collective-permute-done.24 = bf16[152,1792]{1,0:T(8,128)(2,1)} collective-permute-done((bf16[152,1792]{1,0:T(8,128)(2,1)}, bf16[152,1792]{1,0:T(8,128)(2,1)}, u32[]{:S(2)}, u32[]{:S(2)}) %collective-permute-start.24) | collective-permute-done | bytes 544800 | tf_op jit(solution)/shard_map/ppermute | solution.py:100
  248.5 12.6 %collective-permute-done.26.refs_2_ = bf16[256,1792]{1,0:T(8,128)(2,1)} collective-permute-done((bf16[256,1792]{1,0:T(8,128)(2,1)}, bf16[256,1792]{1,0:T(8,128)(2,1)}, u32[]{:S(2)}, u32[]{:S(2)}) %collective-permute-start.26) | collective-permute-done | bytes 917536 | tf_op jit(solution)/shard_map/ppermute | solution.py:29
  271.2 5.3 collective-permute-done.27
  286.1 22.1 %shard_map.207 = (bf16[2048,608]{1,0:T(8,128)(2,1)}, bf16[2048,1216]{1,0:T(8,128)(2,1)}, bf16[2048,1792]{1,0:T(8,128)(2,1)}, bf16[4,256,1792]{2,1,0:T(8,128)(2,1)}, bf16[4,256,1792]{2,1,0:T(8,128)(2,1)}) custom-call(bf16[256,1792]{1,0:T(8,128)(2,1)} %get-tuple-element.47.refs_0_, bf16[256,1792]{1,0:T(8,128)(2,1)} %collective-permute-done.12.refs_1_, ...), custom_call_target="tpu_custom_call" | custom-call | tf_op jit(solution)/shard_map/pallas_call | solution.py:284
  308.3 22.3 %shard_map.208 = (bf16[2048,608]{1,0:T(8,128)(2,1)}, bf16[2048,1216]{1,0:T(8,128)(2,1)}, bf16[2048,1792]{1,0:T(8,128)(2,1)}, bf16[4,256,1792]{2,1,0:T(8,128)(2,1)}, bf16[4,256,1792]{2,1,0:T(8,128)(2,1)}) custom-call(bf16[256,1792]{1,0:T(8,128)(2,1)} %constant_dynamic-update-slice_fusion.20.refs_0_, ...), custom_call_target="tpu_custom_call", output_to_operand_aliasing={{0}: (7, {}), {1}: (8, {}), {2}: (9, {})} | custom-call | tf_op jit(solution)/shard_map/pallas_call | solution.py:284
  342.0 7.3 %collective-permute-done.34 = bf16[128,1792]{1,0:T(8,128)(2,1)S(1)} collective-permute-done((bf16[128,1792]{1,0:T(8,128)(2,1)S(1)}, bf16[128,1792]{1,0:T(8,128)(2,1)S(1)}, u32[]{:S(2)}, u32[]{:S(2)}) %collective-permute-start.34) | collective-permute-done | bytes 458784 | tf_op jit(solution)/shard_map/ppermute | solution.py:29
  355.2 6.1 convolution_convert_fusion.3
  361.3 11.6 %collective-permute-done.35.x_ref = bf16[256,1792]{1,0:T(8,128)(2,1)} collective-permute-done((bf16[256,1792]{1,0:T(8,128)(2,1)}, bf16[256,1792]{1,0:T(8,128)(2,1)}, u32[]{:S(2)}, u32[]{:S(2)}) %collective-permute-start.35) | collective-permute-done | bytes 917536 | tf_op jit(solution)/shard_map/ppermute | solution.py:29
  376.1 11.9 %shard_map.209 = (bf16[8,256,256]{2,1,0:T(8,128)(2,1)S(1)}, f32[256,1792]{1,0:T(8,128)}, bf16[256,1792]{1,0:T(8,128)(2,1)}, f32[1,1792]{1,0:T(1,128)S(1)}) custom-call(f32[256,1792]{1,0:T(8,128)} %get-tuple-element.90.here_ref, bf16[256,1792]{1,0:T(8,128)(2,1)} %collective-permute-done.35.x_ref, bf16[256,1792]{1,0:T(8,128)(2,1)} %collective-permute-done.38.y_ref, ...), custom_call_target="tpu_custom_call" | custom-call | tf_op jit(solution)/shard_map/pallas_call | solution.py:233
  388.0 17.8 %all_to_all.47.top_ref = bf16[8,256,256]{2,1,0:T(8,128)(2,1)S(1)} all-to-all(bf16[8,256,256]{2,1,0:T(8,128)(2,1)S(1)} %get-tuple-element.59), channel_id=1, replica_groups=mesh['z'=4,'y'=2,'x'=2,'c'=2] {'y','x','c'}, dimensions={0} | all-to-all | bytes 2097152 | tf_op jit(solution)/shard_map/all_to_all | solution.py:595
  407.8 20.6 %collective-permute-done.39.refs_4_ = bf16[256,1792]{1,0:T(8,128)(2,1)} collective-permute-done((bf16[256,1792]{1,0:T(8,128)(2,1)}, bf16[256,1792]{1,0:T(8,128)(2,1)}, u32[]{:S(2)}, u32[]{:S(2)}) %collective-permute-start.39) | collective-permute-done | bytes 917536 | tf_op jit(solution)/shard_map/ppermute | solution.py:29
  432.3 8.8 %collective-permute-done.40 = bf16[128,1792]{1,0:T(8,128)(2,1)S(1)} collective-permute-done((bf16[128,1792]{1,0:T(8,128)(2,1)S(1)}, bf16[128,1792]{1,0:T(8,128)(2,1)S(1)}, u32[]{:S(2)}, u32[]{:S(2)}) %collective-permute-start.40) | collective-permute-done | bytes 458784 | tf_op jit(solution)/shard_map/ppermute | solution.py:29
  443.1 16.7 %shard_map.210 = (bf16[8,256,768]{2,1,0:T(8,128)(2,1)S(1)}, f32[2,64,512]{2,1,0:T(8,128)S(1)}, bf16[2,64,512]{2,1,0:T(8,128)(2,1)S(1)}) custom-call(s32[4]{0:T(128)S(1)} %pad_add_fusion.info_ref, bf16[8,256,768]{2,1,0:T(8,128)(2,1)S(1)} %bitcast.140, bf16[8,256,768]{2,1,0:T(8,128)(2,1)S(1)} %bitcast.141, ...), custom_call_target="tpu_custom_call" | custom-call | tf_op jit(solution)/shard_map/pallas_call | solution.py:502
  462.1 8.2 %collective-permute-start.51 = (bf16[2,64,512]{2,1,0:T(8,128)(2,1)S(1)}, bf16[2,64,512]{2,1,0:T(8,128)(2,1)S(1)}, u32[]{:S(2)}, u32[]{:S(2)}) collective-permute-start(bf16[2,64,512]{2,1,0:T(8,128)(2,1)S(1)} %get-tuple-element.65), channel_id=1, source_target_pairs={{8,0},{16,8},{24,16},{9,1},{17,9},{25,17},{10,2},{18,10},{26,18},{... | collective-permute-start | bytes 393224 | tf_op jit(solution)/shard_map/ppermute | solution.py:601
  478.1 7.3 %shard_map.213 = bf16[1792,256]{1,0:T(8,128)(2,1)S(1)} custom-call(bf16[256,1792]{1,0:T(8,128)(2,1)} %get-tuple-element.60.refs_0_, bf16[256,1792]{1,0:T(8,128)(2,1)} %collective-permute-done.60.refs_1_, bf16[256,1792]{1,0:T(8,128)(2,1)} %collective-permute-done.41.refs_2_, bf16[256,1792]{1,0:T(8,128)(2,1)} %collective-permute-done.61.refs_3_, ...), custom_call_target="tpu_custom_call" | custom-call | tf_op jit(solution)/shard_map/pallas_call | solution.py:320
  486.4 9.8 %convolution_convert_fusion.1 = bf16[1792,768]{1,0:T(8,128)(2,1)} fusion(bf16[2048,768]{1,0:T(8,128)(2,1)S(1)} %bitcast.146, bf16[2048,1792]{1,0:T(8,128)(2,1)} %constant_dynamic-update-slice_fusion.2, f32[1792]{0:T(1024)S(1)} %reshape.151, f32[2048]{0:T(1024)S(1)} %add_rsqrt_fusion), kind=kOutput, calls=%fused_computation.6 | convolution fusion | flops 5653200896 | bytes 13253632 | tf_op jit(solution)/shard_map/dot_general | solution.py:44
  497.7 15.3 %convolution_convert_fusion = bf16[1792,1216]{1,0:T(8,128)(2,1)} fusion(bf16[2048,1792]{1,0:T(8,128)(2,1)} %get-tuple-element.72, bf16[2048,1216]{1,0:T(8,128)(2,1)} %get-tuple-element.73), kind=kOutput, calls=%fused_computation.5 | convolution fusion | flops 8927657984 | bytes 16678912 | tf_op jit(solution)/shard_map/dot_general | solution.py:44
  518.8 3.6 convolution_convert_fusion.5
  526.8 3.4 convolution_convert_fusion.7
  542.3 4.0 collective-permute-done.58
  556.3 16.6 %collective-permute-done.59 = bf16[256,1792]{1,0:T(8,128)(2,1)S(1)} collective-permute-done((bf16[256,1792]{1,0:T(8,128)(2,1)S(1)}, bf16[256,1792]{1,0:T(8,128)(2,1)S(1)}, u32[]{:S(2)}, u32[]{:S(2)}) %collective-permute-start.59) | collective-permute-done | bytes 917536 | tf_op jit(solution)/shard_map/ppermute | solution.py:29
  576.7 6.9 all-to-all-start.5
  590.3 3.4 fusion.12
  595.4 3.5 collective-permute-start.64
  598.9 10.6 %collective-permute-done.50 = bf16[256,1792]{1,0:T(8,128)(2,1)} collective-permute-done((bf16[256,1792]{1,0:T(8,128)(2,1)}, bf16[256,1792]{1,0:T(8,128)(2,1)}, u32[]{:S(2)}, u32[]{:S(2)}) %collective-permute-start.50) | collective-permute-done | bytes 917536 | tf_op jit(solution)/shard_map/ppermute | solution.py:29
  612.2 3.4 fusion.21
  615.7 4.3 collective-permute-start.66
  622.3 7.8 %all-to-all-start.6 = ((bf16[8,56,768]{2,1,0:T(8,128)(2,1)}), bf16[8,56,768]{2,1,0:T(8,128)(2,1)S(1)}, u32[]{:S(2)}, u32[]{:S(2)}) async-start(bf16[8,56,768]{2,1,0:T(8,128)(2,1)} %bitcast.160), calls=%async_computation.7 | async-start | bytes 1376256 | tf_op jit(solution)/shard_map/all_to_all | solution.py:621
  630.1 4.7 collective-permute-done.66
  634.9 12.3 %collective-permute-done.67 = bf16[448,56]{0,1:T(8,128)(2,1)S(1)} collective-permute-done((bf16[448,56]{0,1:T(8,128)(2,1)S(1)}, bf16[448,56]{0,1:T(8,128)(2,1)S(1)}, u32[]{:S(2)}, u32[]{:S(2)}) %collective-permute-start.67) | collective-permute-done | bytes 50208 | tf_op jit(solution)/shard_map/ppermute | solution.py:630
  647.2 10.8 %reduce-scatter.9.cloned.1.call-done = bf16[448,1216]{1,0:T(8,128)(2,1)} async-done(((bf16[1792,1216]{1,0:T(8,128)(2,1)}), bf16[448,1216]{1,0:T(8,128)(2,1)}) %reduce-scatter.9.cloned.1.call-update) | async-done | bytes 1089552 | tf_op jit(solution)/shard_map/reduce_scatter | solution.py:588
  658.0 13.8 %all-to-all-start.7 = ((bf16[8,56,1216]{2,1,0:T(8,128)(2,1)}), bf16[8,56,1216]{2,1,0:T(8,128)(2,1)S(1)}, u32[]{:S(2)}, u32[]{:S(2)}) async-start(bf16[8,56,1216]{2,1,0:T(8,128)(2,1)} %bitcast.153), calls=%async_computation.10 | async-start | bytes 2293760 | tf_op jit(solution)/shard_map/all_to_all | solution.py:617
  674.6 12.2 %all-to-all-done.7.sheet_ref = bf16[8,56,1216]{2,1,0:T(8,128)(2,1)S(1)} async-done(((bf16[8,56,1216]{2,1,0:T(8,128)(2,1)}), bf16[8,56,1216]{2,1,0:T(8,128)(2,1)S(1)}, u32[]{:S(2)}, u32[]{:S(2)}) %all-to-all-start.7) | async-done | bytes 1089568 | tf_op jit(solution)/shard_map/all_to_all | solution.py:617
  (354 shorter events, 196.8 us)
Async XLA Ops:
  7.2 191.3 %all-gather.3.cloned.1.call-start = ((), (), s32[]{:S(2)}) async-start(), calls=%async_computation.12 | async-start | bytes 6623232 | tf_op jit(solution)/shard_map/all_gather | solution.py:558
  7.9 56.6 %collective-permute-start.1 = (bf16[256,1792]{1,0:T(8,128)(2,1)}, bf16[256,1792]{1,0:T(8,128)(2,1)}, u32[]{:S(2)}, u32[]{:S(2)}) collective-permute-start(bf16[256,1792]{1,0:T(8,128)(2,1)} %bitcast.142), channel_id=1, source_target_pairs={{0,2},{2,0},{1,3},{3,1},{4,6},{6,4},{5,7},{7,5},{8,10},{10,8},{9,1... | collective-permute-start | bytes 2752520 | tf_op jit(solution)/shard_map/ppermute | solution.py:29
  8.5 61.7 %collective-permute-start.3 = (bf16[256,1792]{1,0:T(8,128)(2,1)}, bf16[256,1792]{1,0:T(8,128)(2,1)}, u32[]{:S(2)}, u32[]{:S(2)}) collective-permute-start(bf16[256,1792]{1,0:T(8,128)(2,1)} %bitcast.143), channel_id=1, source_target_pairs={{0,4},{4,0},{1,5},{5,1},{2,6},{6,2},{3,7},{7,3},{8,12},{12,8},{9,1... | collective-permute-start | bytes 2752520 | tf_op jit(solution)/shard_map/ppermute | solution.py:29
  10.1 64.5 %collective-permute-start = (bf16[256,1792]{1,0:T(8,128)(2,1)}, bf16[256,1792]{1,0:T(8,128)(2,1)}, u32[]{:S(2)}, u32[]{:S(2)}) collective-permute-start(bf16[256,1792]{1,0:T(8,128)(2,1)} %bitcast.144), channel_id=1, source_target_pairs={{0,1},{1,0},{2,3},{3,2},{4,5},{5,4},{6,7},{7,6},{8,9},{9,8},{10,11... | collective-permute-start | bytes 2752520 | tf_op jit(solution)/shard_map/ppermute | solution.py:29
  14.1 25.3 %all-to-all-start = ((bf16[8,56,768]{2,1,0:T(8,128)(2,1)}), bf16[8,56,768]{2,1,0:T(8,128)(2,1)S(1)}, u32[]{:S(2)}, u32[]{:S(2)}) async-start(bf16[8,56,768]{2,1,0:T(8,128)(2,1)} %shard_map.203), calls=%async_computation | async-start | bytes 1376256 | tf_op jit(solution)/shard_map/all_to_all | solution.py:543
  39.4 39.6 %collective-permute-start.8 = (bf16[448,768]{1,0:T(8,128)(2,1)S(1)}, bf16[448,768]{1,0:T(8,128)(2,1)S(1)}, u32[]{:S(2)}, u32[]{:S(2)}) collective-permute-start(bf16[448,768]{1,0:T(8,128)(2,1)S(1)} %bitcast.151), channel_id=1, source_target_pairs={{0,8},{8,16},{16,24},{24,0},{1,9},{9,17},{17,25},{25,1},{2,10},{10... | collective-permute-start | bytes 2064392 | tf_op jit(solution)/shard_map/ppermute | solution.py:94
  40.1 24.5 %all-to-all-start.1 = ((bf16[32,1,128]{2,1,0:T(2,128)(2,1)}), bf16[32,1,128]{2,1,0:T(2,128)(2,1)S(1)}, u32[]{:S(2)}, u32[]{:S(2)}) async-start(bf16[32,1,128]{2,1,0:T(2,128)(2,1)} %copy.38), calls=%async_computation.1 | async-start | bytes 32768 | tf_op jit(solution)/shard_map/all_to_all | solution.py:549
  65.2 42.4 %all-to-all-start.3 = ((bf16[8,56,1216]{2,1,0:T(8,128)(2,1)}), bf16[8,56,1216]{2,1,0:T(8,128)(2,1)S(1)}, u32[]{:S(2)}, u32[]{:S(2)}) async-start(bf16[8,56,1216]{2,1,0:T(8,128)(2,1)} %shard_map.206), calls=%async_computation.3 | async-start | bytes 2293760 | tf_op jit(solution)/shard_map/all_to_all | solution.py:556
  70.2 216.0 %all-gather.5.cloned.1.call-start = ((), (), s32[]{:S(2)}) async-start(), calls=%async_computation.13 | async-start | bytes 5734400 | tf_op jit(solution)/shard_map/all_gather | solution.py:561
  71.3 32.1 %collective-permute-start.5 = (bf16[128,1792]{1,0:T(8,128)(2,1)S(1)}, bf16[128,1792]{1,0:T(8,128)(2,1)S(1)}, u32[]{:S(2)}, u32[]{:S(2)}) collective-permute-start(bf16[128,1792]{1,0:T(8,128)(2,1)S(1)} %slice.258), channel_id=1, source_target_pairs={{0,2},{2,0},{1,3},{3,1},{4,6},{6,4},{5,7},{7,5},{8,10},{10,8},{9,1... | collective-permute-start | bytes 1376264 | tf_op jit(solution)/shard_map/ppermute | solution.py:29
  72.6 31.8 %collective-permute-start.6 = (bf16[128,1792]{1,0:T(8,128)(2,1)S(1)}, bf16[128,1792]{1,0:T(8,128)(2,1)S(1)}, u32[]{:S(2)}, u32[]{:S(2)}) collective-permute-start(bf16[128,1792]{1,0:T(8,128)(2,1)S(1)} %slice.259), channel_id=1, source_target_pairs={{0,4},{4,0},{1,5},{5,1},{2,6},{6,2},{3,7},{7,3},{8,12},{12,8},{9,1... | collective-permute-start | bytes 1376264 | tf_op jit(solution)/shard_map/ppermute | solution.py:29
  78.9 26.6 %collective-permute-start.9 = (bf16[448,768]{1,0:T(8,128)(2,1)S(1)}, bf16[448,768]{1,0:T(8,128)(2,1)}, u32[]{:S(2)}, u32[]{:S(2)}) collective-permute-start(bf16[448,768]{1,0:T(8,128)(2,1)S(1)} %collective-permute-done.8), channel_id=1, source_target_pairs={{0,8},{8,16},{16,24},{24,0},{1,9},{9,17},{17,25},{25,1},{2,10},{10... | collective-permute-start | bytes 2064392 | tf_op jit(solution)/shard_map/ppermute | solution.py:94
  105.4 23.2 %collective-permute-start.7 = (bf16[256,1792]{1,0:T(8,128)(2,1)}, bf16[256,1792]{1,0:T(8,128)(2,1)S(1)}, u32[]{:S(2)}, u32[]{:S(2)}) collective-permute-start(bf16[256,1792]{1,0:T(8,128)(2,1)} %get-tuple-element.103), channel_id=1, source_target_pairs={{0,1},{1,0},{2,3},{3,2},{4,5},{5,4},{6,7},{7,6},{8,9},{9,8},{10,11... | collective-permute-start | bytes 2752520 | tf_op jit(solution)/shard_map/ppermute | solution.py:29
  108.6 82.2 %collective-permute-start.15 = (bf16[256,1792]{1,0:T(8,128)(2,1)}, bf16[256,1792]{1,0:T(8,128)(2,1)}, u32[]{:S(2)}, u32[]{:S(2)}) collective-permute-start(bf16[256,1792]{1,0:T(8,128)(2,1)} %bitcast.14.top_ref), channel_id=1, source_target_pairs={{0,1},{1,0},{2,3},{3,2},{4,5},{5,4},{6,7},{7,6},{8,9},{9,8},{10,11... | collective-permute-start | bytes 2752520 | tf_op jit(solution)/shard_map/ppermute | solution.py:29
  108.7 45.0 %collective-permute-start.16 = (bf16[256,1792]{1,0:T(8,128)(2,1)}, bf16[256,1792]{1,0:T(8,128)(2,1)}, u32[]{:S(2)}, u32[]{:S(2)}) collective-permute-start(bf16[256,1792]{1,0:T(8,128)(2,1)} %bitcast.14.top_ref), channel_id=1, source_target_pairs={{0,2},{2,0},{1,3},{3,1},{4,6},{6,4},{5,7},{7,5},{8,10},{10,8},{9,1... | collective-permute-start | bytes 2752520 | tf_op jit(solution)/shard_map/ppermute | solution.py:29
  109.6 37.9 %collective-permute-start.18 = (bf16[256,1792]{1,0:T(8,128)(2,1)}, bf16[256,1792]{1,0:T(8,128)(2,1)S(1)}, u32[]{:S(2)}, u32[]{:S(2)}) collective-permute-start(bf16[256,1792]{1,0:T(8,128)(2,1)} %bitcast.14.top_ref), channel_id=1, source_target_pairs={{0,4},{4,0},{1,5},{5,1},{2,6},{6,2},{3,7},{7,3},{8,12},{12,8},{9,1... | collective-permute-start | bytes 2752520 | tf_op jit(solution)/shard_map/ppermute | solution.py:29
  126.2 70.4 %collective-permute-start.23 = (bf16[152,1792]{1,0:T(8,128)(2,1)}, bf16[152,1792]{1,0:T(8,128)(2,1)}, u32[]{:S(2)}, u32[]{:S(2)}) collective-permute-start(bf16[152,1792]{1,0:T(8,128)(2,1)} %param.22), channel_id=1, source_target_pairs={{0,8},{8,16},{16,24},{24,0},{1,9},{9,17},{17,25},{25,1},{2,10},{10... | collective-permute-start | bytes 1634312 | tf_op jit(solution)/shard_map/ppermute | solution.py:100
  142.8 28.1 %collective-permute-start.11 = (bf16[2,64,512]{2,1,0:T(8,128)(2,1)S(1)}, bf16[2,64,512]{2,1,0:T(8,128)(2,1)S(1)}, u32[]{:S(2)}, u32[]{:S(2)}) collective-permute-start(bf16[2,64,512]{2,1,0:T(8,128)(2,1)S(1)} %constant_dynamic-slice_fusion.1), channel_id=1, source_target_pairs={{0,8},{8,16},{16,24},{1,9},{9,17},{17,25},{2,10},{10,18},{18,26},{... | collective-permute-start | bytes 393224 | tf_op jit(solution)/shard_map/ppermute | solution.py:571
  147.6 92.2 %collective-permute-start.24 = (bf16[152,1792]{1,0:T(8,128)(2,1)}, bf16[152,1792]{1,0:T(8,128)(2,1)}, u32[]{:S(2)}, u32[]{:S(2)}) collective-permute-start(bf16[152,1792]{1,0:T(8,128)(2,1)} %param.22), channel_id=1, source_target_pairs={{0,16},{8,24},{16,0},{24,8},{1,17},{9,25},{17,1},{25,9},{2,18},{10... | collective-permute-start | bytes 1634312 | tf_op jit(solution)/shard_map/ppermute | solution.py:100
  153.6 92.8 %collective-permute-start.25 = (bf16[152,1792]{1,0:T(8,128)(2,1)}, bf16[152,1792]{1,0:T(8,128)(2,1)}, u32[]{:S(2)}, u32[]{:S(2)}) collective-permute-start(bf16[152,1792]{1,0:T(8,128)(2,1)} %param.22), channel_id=1, source_target_pairs={{0,24},{8,0},{16,8},{24,16},{1,25},{9,1},{17,9},{25,17},{2,26},{10... | collective-permute-start | bytes 1634312 | tf_op jit(solution)/shard_map/ppermute | solution.py:100
  170.9 72.8 %collective-permute-start.19 = (bf16[128,1792]{1,0:T(8,128)(2,1)}, bf16[128,1792]{1,0:T(8,128)(2,1)}, u32[]{:S(2)}, u32[]{:S(2)}) collective-permute-start(bf16[128,1792]{1,0:T(8,128)(2,1)} %slice.262), channel_id=1, source_target_pairs={{0,2},{2,0},{1,3},{3,1},{4,6},{6,4},{5,7},{7,5},{8,10},{10,8},{9,1... | collective-permute-start | bytes 1376264 | tf_op jit(solution)/shard_map/ppermute | solution.py:29
  190.3 346.5 %reduce-scatter.11.cloned.1.call-start = ((), (), s32[]{:S(2)}) async-start(), calls=%async_computation.17 | async-start | bytes 2723840 | tf_op jit(solution)/shard_map/reduce_scatter | solution.py:585
  190.8 52.9 %collective-permute-start.20 = (bf16[128,1792]{1,0:T(8,128)(2,1)}, bf16[128,1792]{1,0:T(8,128)(2,1)}, u32[]{:S(2)}, u32[]{:S(2)}) collective-permute-start(bf16[128,1792]{1,0:T(8,128)(2,1)} %slice.263), channel_id=1, source_target_pairs={{0,4},{4,0},{1,5},{5,1},{2,6},{6,2},{3,7},{7,3},{8,12},{12,8},{9,1... | collective-permute-start | bytes 1376264 | tf_op jit(solution)/shard_map/ppermute | solution.py:29
  196.6 67.8 %collective-permute-start.17 = (bf16[256,1792]{1,0:T(8,128)(2,1)}, bf16[256,1792]{1,0:T(8,128)(2,1)}, u32[]{:S(2)}, u32[]{:S(2)}) collective-permute-start(bf16[256,1792]{1,0:T(8,128)(2,1)} %collective-permute-done.16), channel_id=1, source_target_pairs={{0,1},{1,0},{2,3},{3,2},{4,5},{5,4},{6,7},{7,6},{8,9},{9,8},{10,11... | collective-permute-start | bytes 2752520 | tf_op jit(solution)/shard_map/ppermute | solution.py:29
  243.7 41.4 %collective-permute-start.22 = (bf16[256,1792]{1,0:T(8,128)(2,1)S(1)}, bf16[256,1792]{1,0:T(8,128)(2,1)S(1)}, u32[]{:S(2)}, u32[]{:S(2)}) collective-permute-start(bf16[256,1792]{1,0:T(8,128)(2,1)S(1)} %copy-done.37), channel_id=1, source_target_pairs={{0,1},{1,0},{2,3},{3,2},{4,5},{5,4},{6,7},{7,6},{8,9},{9,8},{10,11... | collective-permute-start | bytes 2752520 | tf_op jit(solution)/shard_map/ppermute | solution.py:29
  243.7 23.5 %collective-permute-start.13 = (bf16[256,1792]{1,0:T(8,128)(2,1)}, bf16[256,1792]{1,0:T(8,128)(2,1)}, u32[]{:S(2)}, u32[]{:S(2)}) collective-permute-start(bf16[256,1792]{1,0:T(8,128)(2,1)} %get-tuple-element.47.refs_0_), channel_id=1, source_target_pairs={{0,2},{2,0},{1,3},{3,1},{4,6},{6,4},{5,7},{7,5},{8,10},{10,8},{9,1... | collective-permute-start | bytes 2752520 | tf_op jit(solution)/shard_map/ppermute | solution.py:29
  246.4 34.4 %collective-permute-start.21 = (bf16[256,1792]{1,0:T(8,128)(2,1)S(1)}, bf16[256,1792]{1,0:T(8,128)(2,1)S(1)}, u32[]{:S(2)}, u32[]{:S(2)}) collective-permute-start(bf16[256,1792]{1,0:T(8,128)(2,1)S(1)} %pad_maximum_fusion), channel_id=1, source_target_pairs={{0,1},{1,0},{2,3},{3,2},{4,5},{5,4},{6,7},{7,6},{8,9},{9,8},{10,11... | collective-permute-start | bytes 2752520 | tf_op jit(solution)/shard_map/ppermute | solution.py:29
  280.0 28.3 %collective-permute-start.30 = (bf16[256,1792]{1,0:T(8,128)(2,1)}, bf16[256,1792]{1,0:T(8,128)(2,1)}, u32[]{:S(2)}, u32[]{:S(2)}) collective-permute-start(bf16[256,1792]{1,0:T(8,128)(2,1)} %collective-permute-done.26.refs_2_), channel_id=1, source_target_pairs={{0,1},{1,0},{2,3},{3,2},{4,5},{5,4},{6,7},{7,6},{8,9},{9,8},{10,11... | collective-permute-start | bytes 2752520 | tf_op jit(solution)/shard_map/ppermute | solution.py:29
  280.8 27.5 %collective-permute-start.29 = (bf16[256,1792]{1,0:T(8,128)(2,1)}, bf16[256,1792]{1,0:T(8,128)(2,1)}, u32[]{:S(2)}, u32[]{:S(2)}) collective-permute-start(bf16[256,1792]{1,0:T(8,128)(2,1)} %constant_dynamic-update-slice_fusion.20.refs_0_), channel_id=1, source_target_pairs={{0,1},{1,0},{2,3},{3,2},{4,5},{5,4},{6,7},{7,6},{8,9},{9,8},{10,11... | collective-permute-start | bytes 2752520 | tf_op jit(solution)/shard_map/ppermute | solution.py:29
  361.3 233.0 %reduce-scatter.7.cloned.1.call-start = ((), (), s32[]{:S(2)}) async-start(), calls=%async_computation.15 | async-start | bytes 1146880 | tf_op jit(solution)/shard_map/reduce_scatter | solution.py:609
  406.4 23.9 %collective-permute-start.41 = (bf16[256,1792]{1,0:T(8,128)(2,1)}, bf16[256,1792]{1,0:T(8,128)(2,1)}, u32[]{:S(2)}, u32[]{:S(2)}) collective-permute-start(bf16[256,1792]{1,0:T(8,128)(2,1)} %get-tuple-element.60.refs_0_), channel_id=1, source_target_pairs={{0,2},{2,0},{1,3},{3,1},{4,6},{6,4},{5,7},{7,5},{8,10},{10,8},{9,1... | collective-permute-start | bytes 2752520 | tf_op jit(solution)/shard_map/ppermute | solution.py:29
  431.8 45.1 %collective-permute-start.60 = (bf16[256,1792]{1,0:T(8,128)(2,1)}, bf16[256,1792]{1,0:T(8,128)(2,1)}, u32[]{:S(2)}, u32[]{:S(2)}) collective-permute-start(bf16[256,1792]{1,0:T(8,128)(2,1)} %get-tuple-element.60.refs_0_), channel_id=1, source_target_pairs={{0,1},{1,0},{2,3},{3,2},{4,5},{5,4},{6,7},{7,6},{8,9},{9,8},{10,11... | collective-permute-start | bytes 2752520 | tf_op jit(solution)/shard_map/ppermute | solution.py:29
  431.8 45.1 %collective-permute-start.61 = (bf16[256,1792]{1,0:T(8,128)(2,1)}, bf16[256,1792]{1,0:T(8,128)(2,1)}, u32[]{:S(2)}, u32[]{:S(2)}) collective-permute-start(bf16[256,1792]{1,0:T(8,128)(2,1)} %collective-permute-done.41.refs_2_), channel_id=1, source_target_pairs={{0,1},{1,0},{2,3},{3,2},{4,5},{5,4},{6,7},{7,6},{8,9},{9,8},{10,11... | collective-permute-start | bytes 2752520 | tf_op jit(solution)/shard_map/ppermute | solution.py:29
  432.3 44.6 %collective-permute-start.62 = (bf16[256,1792]{1,0:T(8,128)(2,1)}, bf16[256,1792]{1,0:T(8,128)(2,1)}, u32[]{:S(2)}, u32[]{:S(2)}) collective-permute-start(bf16[256,1792]{1,0:T(8,128)(2,1)} %collective-permute-done.39.refs_4_), channel_id=1, source_target_pairs={{0,1},{1,0},{2,3},{3,2},{4,5},{5,4},{6,7},{7,6},{8,9},{9,8},{10,11... | collective-permute-start | bytes 2752520 | tf_op jit(solution)/shard_map/ppermute | solution.py:29
  443.1 33.8 %collective-permute-start.63 = (bf16[256,1792]{1,0:T(8,128)(2,1)}, bf16[256,1792]{1,0:T(8,128)(2,1)}, u32[]{:S(2)}, u32[]{:S(2)}) collective-permute-start(bf16[256,1792]{1,0:T(8,128)(2,1)} %constant_dynamic-update-slice_fusion.22.refs_6_), channel_id=1, source_target_pairs={{0,1},{1,0},{2,3},{3,2},{4,5},{5,4},{6,7},{7,6},{8,9},{9,8},{10,11... | collective-permute-start | bytes 2752520 | tf_op jit(solution)/shard_map/ppermute | solution.py:29
  486.4 135.9 %reduce-scatter.5.cloned.1.call-start = ((), (), s32[]{:S(2)}) async-start(), calls=%async_computation.14 | async-start | bytes 3440640 | tf_op jit(solution)/shard_map/reduce_scatter | solution.py:610
  496.3 161.8 %reduce-scatter.9.cloned.1.call-start = ((), (), s32[]{:S(2)}) async-start(), calls=%async_computation.16 | async-start | bytes 5734400 | tf_op jit(solution)/shard_map/reduce_scatter | solution.py:588
  531.3 23.5 %collective-permute-start.52 = (bf16[256,1792]{1,0:T(8,128)(2,1)}, bf16[256,1792]{1,0:T(8,128)(2,1)}, u32[]{:S(2)}, u32[]{:S(2)}) collective-permute-start(bf16[256,1792]{1,0:T(8,128)(2,1)} %slice.282), channel_id=1, source_target_pairs={{0,1},{1,0},{2,3},{3,2},{4,5},{5,4},{6,7},{7,6},{8,9},{9,8},{10,11... | collective-permute-start | bytes 2752520 | tf_op jit(solution)/shard_map/ppermute | solution.py:29
  547.6 51.3 %collective-permute-start.43 = (bf16[256,1792]{1,0:T(8,128)(2,1)}, bf16[256,1792]{1,0:T(8,128)(2,1)}, u32[]{:S(2)}, u32[]{:S(2)}) collective-permute-start(bf16[256,1792]{1,0:T(8,128)(2,1)} %get-tuple-element.79), channel_id=1, source_target_pairs={{0,1},{1,0},{2,3},{3,2},{4,5},{5,4},{6,7},{7,6},{8,9},{9,8},{10,11... | collective-permute-start | bytes 2752520 | tf_op jit(solution)/shard_map/ppermute | solution.py:29
  549.6 23.3 %collective-permute-start.59 = (bf16[256,1792]{1,0:T(8,128)(2,1)S(1)}, bf16[256,1792]{1,0:T(8,128)(2,1)S(1)}, u32[]{:S(2)}, u32[]{:S(2)}) collective-permute-start(bf16[256,1792]{1,0:T(8,128)(2,1)S(1)} %pad_maximum_fusion.6), channel_id=1, source_target_pairs={{0,4},{4,0},{1,5},{5,1},{2,6},{6,2},{3,7},{7,3},{8,12},{12,8},{9,1... | collective-permute-start | bytes 2752520 | tf_op jit(solution)/shard_map/ppermute | solution.py:29
  550.2 23.3 %collective-permute-start.56 = (bf16[256,1792]{1,0:T(8,128)(2,1)S(1)}, bf16[256,1792]{1,0:T(8,128)(2,1)S(1)}, u32[]{:S(2)}, u32[]{:S(2)}) collective-permute-start(bf16[256,1792]{1,0:T(8,128)(2,1)S(1)} %pad_maximum_fusion.5), channel_id=1, source_target_pairs={{0,2},{2,0},{1,3},{3,1},{4,6},{6,4},{5,7},{7,5},{8,10},{10,8},{9,1... | collective-permute-start | bytes 2752520 | tf_op jit(solution)/shard_map/ppermute | solution.py:29
  553.5 30.2 %collective-permute-start.49 = (bf16[128,1792]{1,0:T(8,128)(2,1)}, bf16[128,1792]{1,0:T(8,128)(2,1)}, u32[]{:S(2)}, u32[]{:S(2)}) collective-permute-start(bf16[128,1792]{1,0:T(8,128)(2,1)} %get-tuple-element.100), channel_id=1, source_target_pairs={{0,2},{2,0},{1,3},{3,1},{4,6},{6,4},{5,7},{7,5},{8,10},{10,8},{9,1... | collective-permute-start | bytes 1376264 | tf_op jit(solution)/shard_map/ppermute | solution.py:29
  554.8 32.8 %collective-permute-start.46 = (bf16[128,1792]{1,0:T(8,128)(2,1)}, bf16[128,1792]{1,0:T(8,128)(2,1)}, u32[]{:S(2)}, u32[]{:S(2)}) collective-permute-start(bf16[128,1792]{1,0:T(8,128)(2,1)} %get-tuple-element.99), channel_id=1, source_target_pairs={{0,4},{4,0},{1,5},{5,1},{2,6},{6,2},{3,7},{7,3},{8,12},{12,8},{9,1... | collective-permute-start | bytes 1376264 | tf_op jit(solution)/shard_map/ppermute | solution.py:29
  586.1 23.4 %collective-permute-start.50 = (bf16[256,1792]{1,0:T(8,128)(2,1)}, bf16[256,1792]{1,0:T(8,128)(2,1)}, u32[]{:S(2)}, u32[]{:S(2)}) collective-permute-start(bf16[256,1792]{1,0:T(8,128)(2,1)} %pad_maximum_fusion.4), channel_id=1, source_target_pairs={{0,4},{4,0},{1,5},{5,1},{2,6},{6,2},{3,7},{7,3},{8,12},{12,8},{9,1... | collective-permute-start | bytes 2752520 | tf_op jit(solution)/shard_map/ppermute | solution.py:29
  595.4 26.8 %collective-permute-start.64 = (bf16[448,56]{0,1:T(8,128)(2,1)S(1)}, bf16[448,56]{0,1:T(8,128)(2,1)S(1)}, u32[]{:S(2)}, u32[]{:S(2)}) collective-permute-start(bf16[448,56]{0,1:T(8,128)(2,1)S(1)} %get-tuple-element.110), channel_id=1, source_target_pairs={{0,3},{1,7},{2,11},{3,15},{4,19},{5,23},{6,27},{7,31},{8,0},{9,4},... | collective-permute-start | bytes 150536 | tf_op jit(solution)/shard_map/ppermute | solution.py:630
  619.9 27.3 %collective-permute-start.67 = (bf16[448,56]{0,1:T(8,128)(2,1)S(1)}, bf16[448,56]{0,1:T(8,128)(2,1)S(1)}, u32[]{:S(2)}, u32[]{:S(2)}) collective-permute-start(bf16[448,56]{0,1:T(8,128)(2,1)S(1)} %get-tuple-element.107), channel_id=1, source_target_pairs={{0,0},{1,4},{2,8},{3,12},{4,16},{5,20},{6,24},{7,28},{8,1},{9,5},{... | collective-permute-start | bytes 150536 | tf_op jit(solution)/shard_map/ppermute | solution.py:630
  622.3 35.7 %all-to-all-start.6 = ((bf16[8,56,768]{2,1,0:T(8,128)(2,1)}), bf16[8,56,768]{2,1,0:T(8,128)(2,1)S(1)}, u32[]{:S(2)}, u32[]{:S(2)}) async-start(bf16[8,56,768]{2,1,0:T(8,128)(2,1)} %bitcast.160), calls=%async_computation.7 | async-start | bytes 1376256 | tf_op jit(solution)/shard_map/all_to_all | solution.py:621
  658.0 28.7 %all-to-all-start.7 = ((bf16[8,56,1216]{2,1,0:T(8,128)(2,1)}), bf16[8,56,1216]{2,1,0:T(8,128)(2,1)S(1)}, u32[]{:S(2)}, u32[]{:S(2)}) async-start(bf16[8,56,1216]{2,1,0:T(8,128)(2,1)} %bitcast.153), calls=%async_computation.10 | async-start | bytes 2293760 | tf_op jit(solution)/shard_map/all_to_all | solution.py:617
  (79 other events, 1159.4 us)
Sparse Core Ops, SparseCore 0:
  10.9 97.5 all-gather.2
  110.6 136.3 all-gather.4
  361.4 49.9 reduce-scatter.10
  486.5 24.3 reduce-scatter.6
  513.1 53.7 reduce-scatter.4
  569.1 88.9 reduce-scatter.8

commit v3 on v2

v3 whole, which is shorter than its diff:
```python
import functools

import jax
import jax.numpy as jnp
from jax import lax
from jax.experimental import pallas as pl
from jax.experimental.pallas import tpu as pltpu
from jax.sharding import Mesh, PartitionSpec as P

H = 16
HD = 112
HP = 128
WINDOW = 64
EPS = 1e-06
MASKED = -1e30
SUB = 128
SPAN = 256

BF = jnp.bfloat16
F32 = jnp.float32
ALL = ("z", "y", "x", "c")
PLANE = ("y", "x", "c")
SWAP = [(0, 1), (1, 0)]
NT = (((1,), (1,)), ((), ()))
TN = (((0,), (0,)), ((), ()))
NN = (((1,), (0,)), ((), ()))


def cost(us):
    return pl.CostEstimate(flops=int(us * 1.1e9), bytes_accessed=int(us * 3.5e6), transcendentals=0)


def swap(block, axis):
    return lax.ppermute(block, axis, SWAP)


def normalize(values):
    factor = lax.rsqrt(jnp.mean(values * values, axis=-1, keepdims=True) + EPS)
    return (values * factor, factor)


def norm_back(grad_normed, normed_rows, factor):
    return factor * (
        grad_normed - normed_rows * jnp.mean(grad_normed * normed_rows, axis=-1, keepdims=True)
    )


def dot(left, right, dims=NN):
    return lax.dot_general(left, right, dims, preferred_element_type=F32)


ANY = pl.BlockSpec(memory_space=pl.ANY)


VMEM = pl.BlockSpec(memory_space=pltpu.VMEM)
SMEM = pl.BlockSpec(memory_space=pltpu.SMEM)


def held_kernel(source_ref, *refs):
    refs[-1][...] = source_ref[...]


def held(value, *others):
    return pl.pallas_call(
        held_kernel,
        in_specs=[VMEM] + [ANY] * len(others),
        out_specs=VMEM,
        out_shape=jax.ShapeDtypeStruct(value.shape, value.dtype),
        cost_estimate=cost(2),
        compiler_params=pltpu.CompilerParams(vmem_limit_bytes=32 * 2**20),
    )(value, *others)


def stack_kernel(count, *refs):
    for k in range(count):
        refs[-1][k] = refs[k][...]


def stack(pieces, *others):
    count = len(pieces)
    return pl.pallas_call(
        functools.partial(stack_kernel, count),
        in_specs=[VMEM] * count + [ANY] * len(others),
        out_specs=VMEM,
        out_shape=jax.ShapeDtypeStruct((count, *pieces[0].shape), pieces[0].dtype),
        cost_estimate=cost(2),
        compiler_params=pltpu.CompilerParams(vmem_limit_bytes=32 * 2**20),
    )(*pieces, *others)


def neighbours(own):
    return swap(own, "x"), swap(own, "y")


def join_kernel(first_ref, second_ref, *refs):
    half = first_ref.shape[0]
    refs[-1][:half] = first_ref[...]
    refs[-1][half:] = second_ref[...]


def join(first, second, *others):
    shape = (2 * first.shape[0], *first.shape[1:])
    return pl.pallas_call(
        join_kernel,
        in_specs=[VMEM] * 2 + [ANY] * len(others),
        out_specs=VMEM,
        out_shape=jax.ShapeDtypeStruct(shape, first.dtype),
        cost_estimate=cost(2),
        compiler_params=pltpu.CompilerParams(vmem_limit_bytes=32 * 2**20),
    )(first, second, *others)


def halves_kernel(x_ref, y_ref, *refs):
    half = x_ref.shape[0] // 2
    refs[-2][...] = y_ref[:half]
    refs[-1][...] = x_ref[half:]


def halves(from_x, from_y, *others):
    shape = jax.ShapeDtypeStruct((from_x.shape[0] // 2, *from_x.shape[1:]), from_x.dtype)
    return pl.pallas_call(
        halves_kernel,
        in_specs=[VMEM] * 2 + [ANY] * len(others),
        out_specs=[VMEM] * 2,
        out_shape=[shape, shape],
        cost_estimate=cost(2),
        compiler_params=pltpu.CompilerParams(vmem_limit_bytes=32 * 2**20),
    )(from_x, from_y, *others)


def diagonal(from_x, from_y, *others):
    first, second = halves(from_x, from_y, *others)
    return swap(first, "x"), swap(second, "y")


def both_cores(blocks):
    return [block for mine in blocks for block in (mine, swap(mine, "c"))]


def add_kernel(mine_ref, other_ref, *refs):
    refs[-1][...] = (mine_ref[...].astype(F32) + other_ref[...].astype(F32)).astype(BF)


def add(mine, other, *others):
    return pl.pallas_call(
        add_kernel,
        in_specs=[VMEM] * 2 + [ANY] * len(others),
        out_specs=VMEM,
        out_shape=jax.ShapeDtypeStruct(mine.shape, BF),
        cost_estimate=cost(2),
        compiler_params=pltpu.CompilerParams(vmem_limit_bytes=32 * 2**20),
    )(mine, other, *others)


def plane_sum(parts, *others):
    half = parts[0][0].shape[0] // 2
    other = {r: swap(parts[r][1], "c") for r in (3, 2, 1, 0)}
    far = add(parts[3][0], other[3], *others)
    first = swap(far[:half], "x")
    second = swap(far[half:], "y")
    along_y, along_x, here = (parts[r][0].astype(F32) + other[r].astype(F32) for r in (2, 1, 0))
    along_y = jnp.concatenate([along_y[:half] + first.astype(F32), along_y[half:]], axis=0).astype(BF)
    along_x = jnp.concatenate([along_x[:half], along_x[half:] + second.astype(F32)], axis=0).astype(BF)
    return (here, swap(along_x, "x"), swap(along_y, "y")), (along_x, along_y), far


def total(terms):
    here, got_x, got_y = terms
    return here + got_x.astype(F32) + got_y.astype(F32)


def direct_gather(block, count):
    return [block] + [
        lax.ppermute(block, "z", [(i, (i + k) % count) for i in range(count)])
        for k in range(1, count)
    ]


def padded(share):
    return share * HP // HD


def head_sheet_kernel(starts_ref, query_ref, key_ref, value_ref, gains_ref, out_ref):
    rows = query_ref.shape[0]
    spare = padded(rows) - rows
    same = lax.broadcasted_iota(jnp.int32, (rows, rows), 0) == lax.broadcasted_iota(
        jnp.int32, (rows, rows), 1
    )
    extra = [
        jnp.sum(
            jnp.where(same, jnp.broadcast_to(gains_ref[i : i + 1, :], (rows, rows)), 0.0),
            axis=1,
            keepdims=True,
        )
        for i in range(2)
    ]
    extra = extra + [jnp.full((rows, 1), starts_ref[0, 0], jnp.int32).astype(F32)]
    extra = jnp.concatenate(extra + [jnp.zeros((rows, HP - HD - 3), F32)], axis=1).astype(BF)
    for i, ref in enumerate((query_ref, key_ref, value_ref)):
        for h in range(H):
            pieces = []
            for a in range(HD // rows):
                pieces.append(ref[:, h * HD + a * rows : h * HD + (a + 1) * rows])
                if i == 0 and h % 2 == 0:
                    pieces.append(extra[:, a * spare : (a + 1) * spare])
                else:
                    pieces.append(jnp.zeros((rows, spare), BF))
            lo = (2 * i + h % 2) * HP
            out_ref[h // 2, :, lo : lo + HP] = jnp.concatenate(pieces, axis=1)


def head_sheet(query, key, value, gains, starts):
    whole = pl.BlockSpec(memory_space=pltpu.VMEM)
    return pl.pallas_call(
        head_sheet_kernel,
        in_specs=[pl.BlockSpec(memory_space=pltpu.SMEM)] + [whole] * 4,
        out_specs=whole,
        out_shape=jax.ShapeDtypeStruct((8, query.shape[0], 6 * HP), BF),
        cost_estimate=cost(2),
        compiler_params=pltpu.CompilerParams(vmem_limit_bytes=32 * 2**20),
    )(starts, query, key, value, gains)


def extra_column(j, share):
    spare = padded(share) - share
    return j // spare * padded(share) + share + j % spare


def attn_sheet_kernel(heads_ref, out_weight_ref, *refs):
    sheet_ref = refs[-1]
    count, rows, columns = heads_ref.shape
    size, tile = padded(rows), sheet_ref.shape[1] - columns
    heads = [heads_ref[p].astype(F32) for p in range(count)]
    sheet_ref[:, :columns] = jnp.concatenate(heads, axis=0).astype(BF)
    blank = jnp.zeros((size - rows, tile), F32)
    blocks = []
    for i in range(out_weight_ref.shape[1] // tile):
        blocks += [out_weight_ref[:, i * tile : (i + 1) * tile].astype(F32), blank]
    sheet_ref[:, columns:] = jnp.concatenate(blocks, axis=0).astype(BF)


def attn_sheet(heads, out_weight, *others):
    count, rows, columns = heads.shape
    return pl.pallas_call(
        attn_sheet_kernel,
        in_specs=[VMEM] * 2 + [ANY] * len(others),
        out_shape=jax.ShapeDtypeStruct((count * rows, columns + 256), BF),
        cost_estimate=cost(2),
        compiler_params=pltpu.CompilerParams(vmem_limit_bytes=32 * 2**20),
    )(heads, out_weight, *others)


def out_sheet_kernel(info_ref, *refs):
    *blocks, out_ref = refs
    layers, size, width = out_ref.shape
    tile = blocks[0].shape[1]
    count = width // tile
    for r, block in enumerate(blocks):

        @pl.when(pl.program_id(0) == r)
        def _():
            for z in range(layers):
                for i in range(count):
                    at = (z * count + i) * size
                    out_ref[z, :, i * tile : (i + 1) * tile] = block[at : at + size, :]


def out_sheet(blocks, info, layers):
    depth, tile = blocks[0].shape
    size, width = 2 * HP // layers, depth * tile * 8 // (16 * HP)
    place = lambda r, info: (0, 2 * ((r // 2) ^ info[0]) + ((r % 2) ^ info[1]), 0, 0)
    out = pl.pallas_call(
        out_sheet_kernel,
        grid_spec=pltpu.PrefetchScalarGridSpec(
            num_scalar_prefetch=1,
            grid=(8,),
            in_specs=[pl.BlockSpec((depth, tile), lambda r, info: (0, 0))] * 8,
            out_specs=pl.BlockSpec((layers, None, size, width), place),
        ),
        out_shape=pltpu.HBM((layers, 8, size, width), BF),
        cost_estimate=cost(6),
        compiler_params=pltpu.CompilerParams(vmem_limit_bytes=32 * 2**20),
    )(info, *blocks)
    return out.reshape(-1, width)


def unit_sheet_kernel(layers, part, gate_ref, up_ref, *refs):
    out_ref = refs[-1]
    units = out_ref.shape[2] // 2
    blank = jnp.zeros((gate_ref.shape[0], units // layers - part), BF)
    for w, ref in enumerate((gate_ref, up_ref)):
        for p in range(8):
            pieces = []
            for z in range(layers):
                pieces.append(ref[:, (8 * z + p) * part : (8 * z + p + 1) * part])
                pieces.append(blank)
            out_ref[p, :, w * units : (w + 1) * units] = jnp.concatenate(pieces, axis=1)


def unit_sheet(gate, up, layers, part, units, *others):
    return pl.pallas_call(
        functools.partial(unit_sheet_kernel, layers, part),
        in_specs=[pl.BlockSpec(memory_space=pltpu.VMEM)] * 2 + [ANY] * len(others),
        out_shape=jax.ShapeDtypeStruct((8, gate.shape[0], 2 * units), BF),
        cost_estimate=cost(2),
        compiler_params=pltpu.CompilerParams(vmem_limit_bytes=32 * 2**20),
    )(gate, up, *others)


def gain_row(products, gain):
    rows = products.shape[0]
    same = lax.broadcasted_iota(jnp.int32, (rows, rows), 0) == lax.broadcasted_iota(
        jnp.int32, (rows, rows), 1
    )
    row = jnp.sum(jnp.where(same, jnp.broadcast_to(products, (rows, rows)), 0.0), axis=0, keepdims=True)
    return row / gain


def head_owner_kernel(sheet_ref, *refs):
    weights, gain_ref, (*grads, gain_grad_ref) = refs[:3], refs[3], refs[4:]
    rows = weights[0].shape[0]
    products = jnp.zeros((rows, 1), F32)
    for i, ref in enumerate(grads):
        pieces = []
        for h in range(H):
            lo = (h % 2) * HP
            pieces += [
                sheet_ref[h // 2, i, :, lo + a * padded(rows) : lo + a * padded(rows) + rows]
                for a in range(HD // rows)
            ]
        grad = jnp.concatenate(pieces, axis=1).astype(F32)
        ref[...] = grad
        products += jnp.sum(grad * weights[i][...].astype(F32), axis=1, keepdims=True)
    gain_grad_ref[...] = gain_row(products, gain_ref[...])


def head_owner(sheet, weights, gain):
    share, width = weights[0].shape
    shape = jax.ShapeDtypeStruct((share, width), F32)
    return pl.pallas_call(
        head_owner_kernel,
        out_shape=[shape, shape, shape, jax.ShapeDtypeStruct((1, share), F32)],
        cost_estimate=cost(3),
        compiler_params=pltpu.CompilerParams(vmem_limit_bytes=32 * 2**20),
    )(sheet, *weights, gain)


def unit_owner_kernel(layers, part, sheet_ref, *refs):
    weights, gain_ref, (*grads, gain_grad_ref) = refs[:2], refs[2], refs[3:]
    _, columns, rows, tile = sheet_ref.shape
    units = columns * tile // 2
    owned = [
        jnp.concatenate([sheet_ref[p, b] for b in range(columns)], axis=1).astype(F32)
        for p in range(8)
    ]
    products = jnp.zeros((rows, 1), F32)
    for w, ref in enumerate(grads):
        for z in range(layers):
            lo = w * units + z * (units // layers)
            at = slice(8 * z * part, 8 * (z + 1) * part)
            grad = jnp.concatenate([value[:, lo : lo + part] for value in owned], axis=1)
            ref[:, at] = grad
            products += jnp.sum(grad * weights[w][:, at].astype(F32), axis=1, keepdims=True)
    gain_grad_ref[...] = gain_row(products, gain_ref[...])


def unit_owner(sheet, weights, gain, layers, part):
    share, columns = weights[0].shape
    shape = jax.ShapeDtypeStruct((share, columns), F32)
    return pl.pallas_call(
        functools.partial(unit_owner_kernel, layers, part),
        out_shape=[shape, shape, jax.ShapeDtypeStruct((1, share), F32)],
        cost_estimate=cost(3),
        compiler_params=pltpu.CompilerParams(vmem_limit_bytes=32 * 2**20),
    )(sheet, *weights, gain)


def enter_kernel(share, stream_ref, factor_ref, weight_ref, *refs):
    hidden_ref, qkv_ref, gains_ref = refs[-3:]

    @pl.when(pl.program_id(0) == 0)
    def _():
        row = lax.broadcasted_iota(jnp.int32, (8, HP), 0)
        col = lax.broadcasted_iota(jnp.int32, (8, HP), 1)
        pick = (row == 0) & (col == extra_column(0, share))
        pick = pick | ((row == 1) & (col == extra_column(1, share)))
        pick = pick.astype(F32).astype(BF)
        gains_ref[...] = dot(pick, weight_ref[:, :HP], NT)

    normed = stream_ref[...].astype(F32) * factor_ref[...]
    hidden = (normed * gains_ref[0:1, :]).astype(BF)
    hidden_ref[...] = hidden
    qkv_ref[...] = dot(hidden, weight_ref[...]).astype(BF)


def enter(stream, factor, weight, rows, share, *others):
    tokens, width = stream.shape
    whole = lambda i: (0, 0)
    tile = lambda columns: pl.BlockSpec((rows, columns), lambda i: (i, 0))
    return pl.pallas_call(
        functools.partial(enter_kernel, share),
        grid=(tokens // rows,),
        in_specs=[tile(width), tile(1), pl.BlockSpec((width, 6 * HP), whole)] + [ANY] * len(others),
        out_specs=[tile(width), tile(6 * HP), pl.BlockSpec((8, width), whole)],
        out_shape=[
            pltpu.HBM((tokens, width), BF),
            pltpu.HBM((tokens, 6 * HP), BF),
            jax.ShapeDtypeStruct((8, width), F32),
        ],
        cost_estimate=cost(12),
        compiler_params=pltpu.CompilerParams(vmem_limit_bytes=32 * 2**20),
    )(stream, factor, weight, *others)


def project_kernel(mixed_ref, weight_ref, input_ref, gain_ref, *refs):
    middle_ref, hidden_ref = refs[-2:]
    step = pl.program_id(0)

    @pl.when(step == 0)
    def _():
        middle_ref[...] = input_ref[...].astype(F32)

    middle_ref[...] += jnp.dot(mixed_ref[...], weight_ref[...], preferred_element_type=F32)

    @pl.when(step == pl.num_programs(0) - 1)
    def _():
        normed, _ = normalize(middle_ref[...])
        hidden_ref[...] = (normed * gain_ref[...]).astype(BF)


def project(mixed, weight, own, gain, *others):
    count, rows, depth = mixed.shape
    width = own.shape[1]
    whole = lambda p: (0, 0)
    return pl.pallas_call(
        project_kernel,
        grid=(count,),
        in_specs=[
            pl.BlockSpec((None, rows, depth), lambda p: (p, 0, 0)),
            pl.BlockSpec((depth, width), lambda p: (p, 0)),
            pl.BlockSpec((rows, width), whole),
            pl.BlockSpec((1, width), whole),
        ]
        + [ANY] * len(others),
        out_specs=[pl.BlockSpec((rows, width), whole), pl.BlockSpec((rows, width), whole)],
        out_shape=[
            jax.ShapeDtypeStruct((rows, width), F32),
            jax.ShapeDtypeStruct((rows, width), BF),
        ],
        cost_estimate=cost(7),
        compiler_params=pltpu.CompilerParams(vmem_limit_bytes=32 * 2**20),
    )(mixed, weight, own, gain, *others)


def unproject_kernel(
    here_ref, x_ref, y_ref, middle_ref, top_ref, gain_ref, weight_ref, *refs
):
    out_ref, grad_ref, branch_ref = refs[-3:]

    @pl.when(pl.program_id(0) == 0)
    def _():
        grad_hidden = here_ref[...] + x_ref[...].astype(F32) + y_ref[...].astype(F32)
        normed, factor = normalize(middle_ref[...])
        grad = top_ref[...].astype(F32) + norm_back(grad_hidden * gain_ref[...], normed, factor)
        grad_ref[...] = grad
        branch_ref[...] = grad.astype(BF)

    out_ref[...] = lax.dot_general(
        branch_ref[...], weight_ref[...], NT, preferred_element_type=F32
    ).astype(BF)


def unproject(terms, middle, top, gain, weight, *others):
    rows, width = middle.shape
    depth = weight.shape[0] // 8
    full = pl.BlockSpec((rows, width), lambda p: (0, 0))
    line = pl.BlockSpec((1, width), lambda p: (0, 0))
    return pl.pallas_call(
        unproject_kernel,
        grid=(8,),
        in_specs=[full] * 5
        + [line, pl.BlockSpec((depth, width), lambda p: (p, 0))]
        + [ANY] * len(others),
        out_specs=[pl.BlockSpec((None, rows, depth), lambda p: (p, 0, 0)), full, full],
        out_shape=[
            jax.ShapeDtypeStruct((8, rows, depth), BF),
            jax.ShapeDtypeStruct((rows, width), F32),
            jax.ShapeDtypeStruct((rows, width), BF),
        ],
        cost_estimate=cost(12),
        compiler_params=pltpu.CompilerParams(vmem_limit_bytes=48 * 2**20),
    )(*terms, middle, top, gain, weight, *others)


def ffn_kernel(count, kept, *refs):
    blocks, tops, refs = refs[:count], refs[count : 2 * count], refs[2 * count :]
    gate_up_ref, down_ref, refs = refs[0], refs[1], refs[2 + kept :]
    inner_ref, grads_ref, hidden_ref, top_ref = refs[:4]
    backs, (held_hidden, held_top, held_back, sems) = refs[4 : 4 + count], refs[4 + count :]
    rows = blocks[0].shape[0]
    step = pl.program_id(0)
    bring = [
        [
            pltpu.make_async_copy(source, place.at[j], sems.at[k, j])
            for j, source in enumerate(sources)
        ]
        for k, (sources, place) in enumerate(((blocks, held_hidden), (tops, held_top)))
    ]
    send = [
        pltpu.make_async_copy(
            held_back.at[j // 2, pl.ds(j % 2 * rows, rows)], backs[j], sems.at[2, j]
        )
        for j in range(count)
    ]

    @pl.when(step == 0)
    def _():
        for j in range(count):
            bring[0][j].start()
            bring[1][j].start()

    for j in range(0, count, 2):

        @pl.when(step == j // 2)
        def _():
            for k in range(2):
                bring[k][j].wait()
                bring[k][j + 1].wait()

    for half in range(2):
        at = slice(half * rows, (half + 1) * rows)
        hidden_ref[at, :] = held_hidden[2 * step + half]
        top_ref[at, :] = held_top[2 * step + half]
    units = down_ref.shape[0]
    both = dot(hidden_ref[...], gate_up_ref[...])
    grad_inner = dot(top_ref[...], down_ref[...], NT)
    gate, upper = both[:, :units], both[:, units:]
    sigma = jax.nn.sigmoid(gate)
    activ = gate * sigma
    inner_ref[...] = (activ * upper).astype(BF)
    grads_ref[:, units:] = (grad_inner * activ).astype(BF)
    grad_gate = grad_inner * upper * sigma * (1.0 + gate * (1.0 - sigma))
    grads_ref[:, :units] = grad_gate.astype(BF)
    held_back[step] = dot(grads_ref[...], gate_up_ref[...], NT).astype(BF)
    for j in range(0, count, 2):

        @pl.when(step == j // 2)
        def _():
            send[j].start()
            send[j + 1].start()

    @pl.when(step == count // 2 - 1)
    def _():
        for copy in send:
            copy.wait()


def ffn(blocks, tops, gate_up, down, first, carried=(), others=()):
    count = len(blocks)
    rows, width = blocks[0].shape
    units = down.shape[0]
    whole = lambda i: (0, 0)
    tile = lambda columns: pl.BlockSpec((2 * rows, columns), lambda i: (i + first, 0))
    once = lambda shape: pl.BlockSpec(shape, whole, pipeline_mode=pl.Buffered(1))
    stacked = lambda columns: jax.ShapeDtypeStruct((8 * rows, columns), BF)
    out = pl.pallas_call(
        functools.partial(ffn_kernel, count, len(carried) + len(others)),
        grid=(count // 2,),
        in_specs=[ANY] * (2 * count)
        + [once((width, 2 * units)), once((units, width))]
        + [ANY] * (len(carried) + len(others)),
        out_specs=[tile(units), tile(2 * units), tile(width), tile(width)] + [ANY] * count,
        out_shape=[stacked(units), stacked(2 * units), stacked(width), stacked(width)]
        + [jax.ShapeDtypeStruct((rows, width), BF)] * count,
        scratch_shapes=[
            pltpu.VMEM((count, rows, width), BF),
            pltpu.VMEM((count, rows, width), BF),
            pltpu.VMEM((count // 2, 2 * rows, width), BF),
            pltpu.SemaphoreType.DMA((3, count)),
        ],
        input_output_aliases={2 * count + 2 + i: i for i in range(len(carried))},
        cost_estimate=cost(4 * count + 2),
        compiler_params=pltpu.CompilerParams(vmem_limit_bytes=60 * 2**20),
    )(*blocks, *tops, gate_up, down, *carried, *others)
    return out[:4], out[4:]


def split_kernel(order, dims, left_ref, right_ref, *refs):
    rows = left_ref.shape[0] // 2
    both = dot(left_ref[...], right_ref[...], dims)
    outs = refs[-2 * len(order) :]
    both = both.astype(BF)
    for i in range(len(order)):

        @pl.when(pl.program_id(0) == i)
        def _():
            outs[2 * i][...] = both[:rows]
            outs[2 * i + 1][...] = both[rows:]


def split(left, right, dims, order, rows, others=()):
    width = right.shape[1 - dims[0][1][0]]

    def place(i):
        at = order[0]
        for n, r in enumerate(order):
            at = jnp.where(i == n, r, at)
        return at, 0

    used = (width, left.shape[1]) if dims == NT else (left.shape[1], width)
    out = pl.pallas_call(
        functools.partial(split_kernel, order, dims),
        grid=(len(order),),
        in_specs=[
            pl.BlockSpec((2 * rows, left.shape[1]), place),
            pl.BlockSpec(used, lambda i: (0, 0)),
        ]
        + [ANY] * len(others),
        out_specs=[pl.BlockSpec((rows, width), lambda i: (0, 0))] * (2 * len(order)),
        out_shape=[jax.ShapeDtypeStruct((rows, width), BF)] * (2 * len(order)),
        cost_estimate=cost(3 * len(order) + 2),
        compiler_params=pltpu.CompilerParams(vmem_limit_bytes=56 * 2**20),
    )(left, right, *others)
    return [tuple(out[2 * order.index(r) :][:2]) for r in range(len(order))]


def down_sums_kernel(inner_ref, top_ref, *refs):
    out_ref = refs[-1]
    count, size, _ = out_ref.shape
    found = dot(inner_ref[...], top_ref[...], TN).astype(BF)
    for z in range(count):
        out_ref[z] = found[z * size : (z + 1) * size]


def unit_sums_kernel(hidden_ref, grads_ref, *refs):
    out_ref = refs[-1]
    count, size, tile = out_ref.shape
    columns = grads_ref.shape[1] // tile
    depth = size // columns
    found = dot(hidden_ref[...], grads_ref[...], TN).astype(BF)
    for z in range(count):
        for b in range(columns):
            out_ref[z, b * depth : (b + 1) * depth, :] = found[
                z * depth : (z + 1) * depth, b * tile : (b + 1) * tile
            ]


def unit_sums(hidden, grads, layers, below, *others):
    tokens, width = hidden.shape
    tile = 256
    above = grads.shape[1] // tile * width // layers
    return pl.pallas_call(
        unit_sums_kernel,
        grid=(2,),
        in_specs=[
            pl.BlockSpec((tokens, width // 2), lambda i: (0, i)),
            pl.BlockSpec(grads.shape, lambda i: (0, 0)),
        ]
        + [ANY] * len(others),
        out_specs=pl.BlockSpec((layers // 2, above, tile), lambda i: (i, 0, 0)),
        out_shape=jax.ShapeDtypeStruct((layers, above + below, tile), BF),
        cost_estimate=cost(14),
        compiler_params=pltpu.CompilerParams(vmem_limit_bytes=56 * 2**20),
    )(hidden, grads, *others)


def down_sums(inner, tops, carried, *others):
    tokens, units = inner.shape
    width = tops.shape[1]
    layers, length, tile = carried.shape
    size = units // layers
    above = length - width // tile * size
    return pl.pallas_call(
        down_sums_kernel,
        grid=(width // tile,),
        in_specs=[
            pl.BlockSpec((tokens, units), lambda i: (0, 0)),
            pl.BlockSpec((tokens, tile), lambda i: (0, i)),
        ]
        + [ANY] * (1 + len(others)),
        out_specs=pl.BlockSpec((layers, size, tile), lambda i: (0, above // size + i, 0)),
        out_shape=jax.ShapeDtypeStruct(carried.shape, BF),
        input_output_aliases={2: 0},
        cost_estimate=cost(10),
        compiler_params=pltpu.CompilerParams(vmem_limit_bytes=56 * 2**20),
    )(inner, tops, carried, *others)


def part_sheet_kernel(sum_ref, *refs):
    heads_ref, out_ref = refs[-2:]
    owners, blocks, share, _ = heads_ref.shape
    depth = owners * share
    for b in range(blocks):
        block = sum_ref[b * depth : (b + 1) * depth].astype(F32)
        for p in range(owners):
            heads_ref[p, b] = block[p * share : (p + 1) * share].astype(BF)
    out_ref[...] = sum_ref[blocks * depth :]


def part_sheet(total_sum, share, *others):
    rows, tile = total_sum.shape
    blocks = 6 * HP // tile
    return pl.pallas_call(
        part_sheet_kernel,
        in_specs=[VMEM] + [ANY] * len(others),
        out_specs=[VMEM, VMEM],
        out_shape=[
            jax.ShapeDtypeStruct((8, blocks, share, tile), BF),
            jax.ShapeDtypeStruct((rows - blocks * 8 * share, tile), BF),
        ],
        cost_estimate=cost(2),
        compiler_params=pltpu.CompilerParams(vmem_limit_bytes=32 * 2**20),
    )(total_sum, *others)


def out_owner_kernel(piece_ref, out_ref):
    share, width = out_ref.shape
    size, tile = padded(share), piece_ref.shape[1]
    for i in range(width // tile):
        block = piece_ref[i * size : (i + 1) * size].astype(F32)
        out_ref[:, i * tile : (i + 1) * tile] = block[:share]


def out_owner(piece, share, width):
    return pl.pallas_call(
        out_owner_kernel,
        out_shape=jax.ShapeDtypeStruct((share, width), F32),
        cost_estimate=cost(2),
        compiler_params=pltpu.CompilerParams(vmem_limit_bytes=32 * 2**20),
    )(piece)


def out_sums_kernel(count, *refs):
    blocks, kept_ref, out_ref = refs[:count], refs[count], refs[-1]
    layers, size, _ = out_ref.shape
    found = [dot(kept_ref[i], ref[...], TN) for i, ref in enumerate(blocks)]
    found = functools.reduce(jnp.add, found).astype(BF)
    for z in range(layers):
        out_ref[z] = found[z * size : (z + 1) * size]


def head_sums_kernel(hidden_ref, grads_ref, rim_ref, lead_ref, *refs):
    out_ref = refs[-1]
    count, size, tile = out_ref.shape
    columns = grads_ref.shape[1] // tile
    depth = size // columns
    found = dot(hidden_ref[...], grads_ref[...], TN)
    more = dot(rim_ref[...], lead_ref[...], TN)
    skip = found.shape[1] - more.shape[1]
    found = jnp.concatenate([found[:, :skip], found[:, skip:] + more], axis=1).astype(BF)
    for z in range(count):
        for b in range(columns):
            out_ref[z, b * depth : (b + 1) * depth, :] = found[
                z * depth : (z + 1) * depth, b * tile : (b + 1) * tile
            ]


def head_sums(hidden, grad, rim, lead, layers, rows, *others):
    tokens, width = hidden.shape
    tile = 256
    above = grad.shape[1] // tile * width // layers
    whole = lambda i: (0, 0)
    return pl.pallas_call(
        head_sums_kernel,
        grid=(2,),
        in_specs=[
            pl.BlockSpec((tokens, width // 2), lambda i: (0, i)),
            pl.BlockSpec(grad.shape, whole),
            pl.BlockSpec((rim.shape[0], width // 2), lambda i: (0, i)),
            pl.BlockSpec(lead.shape, whole),
        ]
        + [ANY] * len(others),
        out_specs=pl.BlockSpec((layers // 2, above, tile), lambda i: (i, 0, 0)),
        out_shape=jax.ShapeDtypeStruct((layers, above + rows, tile), BF),
        cost_estimate=cost(11),
        compiler_params=pltpu.CompilerParams(vmem_limit_bytes=56 * 2**20),
    )(hidden, grad, rim, lead, *others)


def out_sums(blocks, kept, carried, *others):
    rows, width = blocks[0].shape
    count, _, depth = kept.shape
    layers, length, tile = carried.shape
    size = depth // layers
    above = length - width // tile * size
    return pl.pallas_call(
        functools.partial(out_sums_kernel, count),
        grid=(width // tile,),
        in_specs=[pl.BlockSpec((rows, tile), lambda i: (0, i))] * count
        + [pl.BlockSpec((count, rows, depth), lambda i: (0, 0, 0))]
        + [ANY] * (1 + len(others)),
        out_specs=pl.BlockSpec((layers, size, tile), lambda i: (0, above // size + i, 0)),
        out_shape=jax.ShapeDtypeStruct(carried.shape, BF),
        input_output_aliases={count + 1: 0},
        cost_estimate=cost(6),
        compiler_params=pltpu.CompilerParams(vmem_limit_bytes=32 * 2**20),
    )(*blocks, kept, carried, *others)


def leave_kernel(here_ref, x_ref, y_ref, own_ref, grad_ref, gain_ref, *refs):
    grad_hidden = here_ref[...] + x_ref[...].astype(F32) + y_ref[...].astype(F32)
    normed, factor = normalize(own_ref[...].astype(F32))
    refs[-1][...] = grad_ref[...] + norm_back(grad_hidden * gain_ref[...], normed, factor)


def leave(terms, own, grad_middle, gain, *others):
    return pl.pallas_call(
        leave_kernel,
        in_specs=[VMEM] * 6 + [ANY] * len(others),
        out_specs=VMEM,
        out_shape=jax.ShapeDtypeStruct(own.shape, F32),
        cost_estimate=cost(6),
        compiler_params=pltpu.CompilerParams(vmem_limit_bytes=32 * 2**20),
    )(*terms, own, grad_middle, gain, *others)


def mend_kernel(info_ref, tail_ref, back_ref, cur_ref, *refs):
    out_ref = refs[-1]
    out_ref[:, : 2 * HP] = cur_ref[:, : 2 * HP]
    out_ref[:, 2 * HP :] = (tail_ref[...] + back_ref[...].astype(F32)).astype(BF)


def mend(info, tail, back, grad_qkv, *others):
    rows, blocks = grad_qkv.shape[1], grad_qkv.shape[0] // 2
    side = pl.BlockSpec((None, WINDOW, 4 * HP), lambda s, info: (s, 0, 0))
    edge = pl.BlockSpec(
        (None, WINDOW, 6 * HP),
        lambda s, info: (2 * ((blocks - 1) ^ info[0]) + s, rows // WINDOW - 1, 0),
    )
    return pl.pallas_call(
        mend_kernel,
        grid_spec=pltpu.PrefetchScalarGridSpec(
            num_scalar_prefetch=1,
            grid=(2,),
            in_specs=[side, side, edge] + [ANY] * len(others),
            out_specs=edge,
        ),
        out_shape=jax.ShapeDtypeStruct(grad_qkv.shape, BF),
        cost_estimate=cost(2),
        input_output_aliases={3: 0},
    )(info, tail, back, grad_qkv, *others)


def first_key(at, rows):
    return min(at, rows + WINDOW - SPAN)


def shares_of(raws, cut, rows):
    row = lax.broadcasted_iota(jnp.int32, (SUB, SPAN), 0)
    col = lax.broadcasted_iota(jnp.int32, (SUB, SPAN), 1)
    seen = {}
    for at in range(0, rows, SUB):
        shift = at - first_key(at, rows)
        valid = (col > row + shift) & (col <= row + (shift + WINDOW))
        seen[at] = valid & (col >= cut) if at == 0 else valid
    scores = [jnp.where(seen[at], raw, MASKED) for at, raw in raws]
    peaks = [jnp.max(score, axis=-1, keepdims=True) for score in scores]
    powers = [jnp.exp((s - p) * (HD ** (-0.5))) for s, p in zip(scores, peaks)]
    totals = [jnp.sum(power, axis=-1, keepdims=True) for power in powers]
    return [power * (1.0 / total) for power, total in zip(powers, totals)]


def joined(prev_ref, halo_ref, cur_ref, at_first, lo):
    before = jnp.where(
        at_first, halo_ref[:, lo - 2 * HP : lo - HP], prev_ref[:, lo : lo + HP]
    )
    return jnp.concatenate([before, cur_ref[:, lo : lo + HP]], axis=0)


def tiles_of(rows):
    return [(h, at, first_key(at, rows)) for h in range(2) for at in range(0, rows, SUB)]


def attend_kernel(info_ref, cur_ref, prev_ref, halo_ref, *refs):
    flat_ref, kept_ref = refs[-2:]
    stream, block = pl.program_id(0), pl.program_id(1)
    at_first = block == 0
    cut = jnp.where(at_first & (info_ref[2 + stream] == 1), WINDOW, 0)
    rows = cur_ref.shape[0]
    tiles = tiles_of(rows)
    keys = [joined(prev_ref, halo_ref, cur_ref, at_first, (2 + h) * HP) for h in range(2)]
    values = [joined(prev_ref, halo_ref, cur_ref, at_first, (4 + h) * HP) for h in range(2)]
    raws = [
        (at, dot(cur_ref[at : at + SUB, h * HP : (h + 1) * HP], keys[h][lo : lo + SPAN], NT))
        for h, at, lo in tiles
    ]
    shares = [share.astype(BF) for share in shares_of(raws, cut, rows)]
    mixes = [dot(share, values[h][lo : lo + SPAN]) for share, (h, at, lo) in zip(shares, tiles)]
    for mixed, (h, at, lo) in zip(mixes, tiles):
        mixed = mixed.astype(BF)
        flat_ref[at : at + SUB, h * HP : (h + 1) * HP] = mixed
        kept_ref[at : at + SUB, h * HP : (h + 1) * HP] = mixed


def attend(qkv, halo, info, *others):
    rows, blocks = qkv.shape[1], qkv.shape[0] // 2
    mine = lambda s, b, info: (2 * (b ^ info[0]) + s, 0, 0)
    before = lambda s, b, info: (2 * (jnp.maximum(b - 1, 0) ^ info[0]) + s, rows // WINDOW - 1, 0)
    spec = pltpu.PrefetchScalarGridSpec(
        num_scalar_prefetch=1,
        grid=(2, blocks),
        in_specs=[
            pl.BlockSpec((None, rows, 6 * HP), mine),
            pl.BlockSpec((None, WINDOW, 6 * HP), before),
            pl.BlockSpec((None, WINDOW, 4 * HP), lambda s, b, info: (s, 0, 0)),
        ]
        + [ANY] * len(others),
        out_specs=[
            pl.BlockSpec((None, rows, 2 * HP), lambda s, b, info: (2 * b + (s ^ info[1]), 0, 0)),
            pl.BlockSpec((None, rows, 2 * HP), mine),
        ],
    )
    shape = jax.ShapeDtypeStruct((2 * blocks, rows, 2 * HP), BF)
    return pl.pallas_call(
        attend_kernel,
        grid_spec=spec,
        out_shape=[shape, pltpu.HBM(shape.shape, shape.dtype)],
        cost_estimate=cost(8),
        compiler_params=pltpu.CompilerParams(vmem_limit_bytes=32 * 2**20),
    )(info, qkv, qkv, halo, *others)


def attend_back_kernel(
    info_ref, cur_ref, prev_ref, halo_ref, top_ref, *refs
):
    out_ref, tail_ref, lead_ref, keep, acc = refs[-5:]
    stream, step = pl.program_id(0), pl.program_id(1)
    blocks = pl.num_programs(1)
    at_first = step == blocks - 1
    cut = jnp.where(at_first & (info_ref[2 + stream] == 1), WINDOW, 0)
    rows = cur_ref.shape[0]

    @pl.when(step == 0)
    def _():
        keep[...] = jnp.zeros_like(keep)

    acc[...] = jnp.zeros_like(acc)
    tiles = tiles_of(rows)
    keys = [joined(prev_ref, halo_ref, cur_ref, at_first, (2 + h) * HP) for h in range(2)]
    values = [joined(prev_ref, halo_ref, cur_ref, at_first, (4 + h) * HP) for h in range(2)]
    queries = [cur_ref[at : at + SUB, h * HP : (h + 1) * HP] for h, at, lo in tiles]
    tops = [top_ref[at : at + SUB, h * HP : (h + 1) * HP] for h, at, lo in tiles]
    raws = [
        (at, dot(query, keys[h][lo : lo + SPAN], NT)) for query, (h, at, lo) in zip(queries, tiles)
    ]
    grads = [dot(top, values[h][lo : lo + SPAN], NT) for top, (h, at, lo) in zip(tops, tiles)]
    shares = shares_of(raws, cut, rows)
    spent = [
        jnp.sum(share * grad, axis=-1, keepdims=True) for share, grad in zip(shares, grads)
    ]
    grads = [
        (share * ((grad - sum_) * (HD ** (-0.5)))).astype(BF)
        for share, grad, sum_ in zip(shares, grads, spent)
    ]
    shares = [share.astype(BF) for share in shares]
    for share, grad, query, top, (h, at, lo) in zip(shares, grads, queries, tops, tiles):
        left, right = h * HP, (h + 1) * HP
        out_ref[at : at + SUB, left:right] = dot(grad, keys[h][lo : lo + SPAN]).astype(BF)
        acc[lo : lo + SPAN, left:right] += dot(grad, query, TN)
        acc[lo : lo + SPAN, 2 * HP + left : 2 * HP + right] += dot(share, top, TN)
    last = acc[rows : rows + WINDOW, :] + keep[...]
    out_ref[: rows - WINDOW, 2 * HP :] = acc[WINDOW:rows, :].astype(BF)
    out_ref[rows - WINDOW :, 2 * HP :] = last.astype(BF)
    keep[...] = acc[:WINDOW, :]

    @pl.when(step == 0)
    def _():
        tail_ref[...] = last

    @pl.when(at_first)
    def _():
        lead_ref[...] = acc[:WINDOW, :].astype(BF)


def attend_back(qkv, halo, top, info, *others):
    rows, blocks = qkv.shape[1], qkv.shape[0] // 2
    at = lambda t: blocks - 1 - t
    mine = lambda s, t, info: (2 * (at(t) ^ info[0]) + s, 0, 0)
    before = lambda s, t, info: (
        2 * (jnp.maximum(at(t) - 1, 0) ^ info[0]) + s,
        rows // WINDOW - 1,
        0,
    )
    side = lambda s, t, info: (s, 0, 0)
    spec = pltpu.PrefetchScalarGridSpec(
        num_scalar_prefetch=1,
        grid=(2, blocks),
        in_specs=[
            pl.BlockSpec((None, rows, 6 * HP), mine),
            pl.BlockSpec((None, WINDOW, 6 * HP), before),
            pl.BlockSpec((None, WINDOW, 4 * HP), side),
            pl.BlockSpec(
                (None, rows, 2 * HP), lambda s, t, info: (2 * at(t) + (s ^ info[1]), 0, 0)
            ),
        ]
        + [ANY] * len(others),
        out_specs=[
            pl.BlockSpec((None, rows, 6 * HP), mine),
            pl.BlockSpec((None, WINDOW, 4 * HP), side),
            pl.BlockSpec((None, WINDOW, 4 * HP), side),
        ],
        scratch_shapes=[
            pltpu.VMEM((WINDOW, 4 * HP), F32),
            pltpu.VMEM((rows + WINDOW, 4 * HP), F32),
        ],
    )
    return pl.pallas_call(
        attend_back_kernel,
        grid_spec=spec,
        out_shape=[
            jax.ShapeDtypeStruct(qkv.shape, BF),
            jax.ShapeDtypeStruct(halo.shape, F32),
            jax.ShapeDtypeStruct(halo.shape, BF),
        ],
        cost_estimate=cost(17),
        compiler_params=pltpu.CompilerParams(vmem_limit_bytes=32 * 2**20),
    )(info, qkv, qkv, halo, top, *others)


def body(
    inputs,
    starts,
    attn_gain,
    query_weight,
    key_weight,
    value_weight,
    out_weight,
    ffn_gain,
    gate_weight,
    up_weight,
    down_weight,
    cotangent,
):
    rows, width = inputs.shape[1:]
    layers = lax.axis_size("z")
    devices = 8 * layers
    share = query_weight.shape[0]
    part = down_weight.shape[0]
    units = -(-part // 16) * 16 * layers
    me_z = lax.axis_index("z")
    me_block = 2 * lax.axis_index("y") + lax.axis_index("x")
    me_core = lax.axis_index("c")

    own = inputs[0]
    top = cotangent[0]
    own_gains = jnp.stack([attn_gain, ffn_gain]).astype(F32)
    heads = head_sheet(query_weight, key_weight, value_weight, own_gains, starts)
    down = jnp.pad(down_weight, ((0, units // layers - part), (0, 0)))
    down = lax.all_gather(down, "z", axis=0, tiled=True)
    heads = lax.all_to_all(heads, PLANE, 0, 0, tiled=True)
    opened = heads[:2, 0, extra_column(2, share)].astype(jnp.int32)
    opened = jnp.where(me_core == 0, opened, opened[::-1])
    info = jnp.concatenate([jnp.stack([me_block, me_core]), opened, me_z[None]]).astype(jnp.int32)
    from_x, from_y = neighbours(held(own, heads))
    far = join(*diagonal(from_x, from_y))
    streams = both_cores([own, from_x, from_y, far])
    attn_weight = attn_sheet(heads, out_weight, down, from_x, from_y)
    attn_weight = lax.all_gather(attn_weight, "z", axis=0, tiled=True)
    stream = jnp.concatenate(streams, axis=0)
    factor = normalize(stream.astype(F32))[1]
    sheet = unit_sheet(gate_weight, up_weight, layers, part, units, heads)
    sheet = lax.all_to_all(sheet, PLANE, 0, 0, tiled=True).reshape(8 * share, 2 * units)
    gate_up = lax.all_gather(sheet, "z", axis=0, tiled=True)
    from_x, from_y = neighbours(held(top, streams[6]))
    first, second = halves(from_x, from_y)
    tops = [top, from_x, from_y]
    far_top = swap(first, "x"), swap(second, "y")

    hidden1, qkv, gains = enter(stream, factor, attn_weight, rows, share, first)
    gain_attn, gain_ffn = gains[0:1], gains[1:2]
    qkv = qkv.reshape(8, rows, 6 * HP)
    last = 2 * (3 ^ me_block)
    rim = lax.dynamic_slice(qkv, (last, rows - WINDOW, 2 * HP), (2, WINDOW, 4 * HP))
    halo = lax.ppermute(rim, "z", [(i, i + 1) for i in range(layers - 1)])
    own_out = attn_weight[:, 6 * HP :]
    from_x, from_y = neighbours(own_out)
    far = diagonal(from_x, from_y, halo)
    flat, kept = attend(qkv, halo, info)
    full_out = both_cores([own_out, from_x, from_y, join(*far, flat)])
    full_out = out_sheet(full_out, info, layers)
    tops = both_cores(tops + [join(*far_top, flat)])
    rim = lax.dynamic_slice(
        hidden1.reshape(8, rows, width), (last, rows - WINDOW, 0), (2, WINDOW, width)
    )
    rim = lax.ppermute(rim, "z", [(i, i + 1) for i in range(layers - 1)])
    mixed = lax.all_to_all(flat, PLANE, 0, 0, tiled=True)
    middle, hidden2 = project(mixed, full_out, own, gain_ffn, tops[6])

    from_x, from_y = neighbours(hidden2)
    far = diagonal(from_x, from_y)
    carried, near = ffn(
        both_cores([hidden2, from_x, from_y]), tops[:6], gate_up, down, 0
    )
    far = join(*far, carried[0])
    (inner, grads, hidden2, tops), far = ffn(
        both_cores([far]), tops[6:], gate_up, down, 3, carried
    )
    terms, sent, far = plane_sum([near[:2], near[2:4], near[4:], far])
    ffn_part = unit_sums(hidden2, grads, layers, width // 256 * units // layers, far, rim)
    ffn_part = down_sums(inner, tops, ffn_part, *sent)
    out_parts = split(inner, down, NN, (3, 2, 1, 0), rows, [ffn_part])
    ffn_sum = lax.psum_scatter(ffn_part, "z", scatter_dimension=0, tiled=True)[0]

    grad_mixed, grad_middle, grad_branch = unproject(
        terms, middle, top, gain_ffn, full_out, out_parts[3][0]
    )

    grad_mixed = lax.all_to_all(grad_mixed, PLANE, 0, 0, tiled=True)
    from_x, from_y = neighbours(grad_branch)
    grad_qkv, tail, lead = attend_back(qkv, halo, grad_mixed, info)
    back = lax.ppermute(lead, "z", [(i + 1, i) for i in range(layers - 1)])
    out_terms, sent, _ = plane_sum(out_parts, tail)
    attn_part = head_sums(
        hidden1,
        grad_qkv.reshape(8 * rows, 6 * HP),
        rim.reshape(2 * WINDOW, width),
        lead.reshape(2 * WINDOW, 4 * HP),
        layers,
        8 * share,
    )
    branches = join(*diagonal(from_x, from_y, attn_part))
    branches = both_cores([grad_branch, from_x, from_y, branches])
    grad_qkv = mend(info, tail, back, grad_qkv, attn_part).reshape(8 * rows, 6 * HP)
    attn_part = out_sums(branches, kept, attn_part, grad_qkv, *sent)
    attn_sum = lax.psum_scatter(attn_part, "z", scatter_dimension=0, tiled=True)[0]
    layer_out = (middle + total(out_terms)).astype(BF)
    above = 2 * units // 256 * 8 * share
    gate_up_sum = ffn_sum[:above].reshape(-1, 8, share, 256).swapaxes(0, 1)
    gate_up_sum = lax.all_to_all(gate_up_sum, PLANE, 0, 0, tiled=True)
    gate_grad, up_grad, ffn_gain_grad = unit_owner(
        gate_up_sum, (gate_weight, up_weight), own_gains[1:2], layers, part
    )
    down_grad = ffn_sum[above:].reshape(width // 256, -1, 256).swapaxes(0, 1)
    down_grad = down_grad[:part].reshape(part, width).astype(F32)
    parts = split(grad_qkv, attn_weight, NT, (3, 2, 1, 0), rows, [attn_part])
    terms, _, _ = plane_sum(parts, *out_terms[1:])
    input_grad = leave(terms, own, grad_middle, gain_attn, gate_grad)

    qkv_sum, out_sum = part_sheet(attn_sum, share, input_grad, layer_out)
    qkv_sum = lax.all_to_all(qkv_sum, PLANE, 0, 0, tiled=True)
    query_grad, key_grad, value_grad, attn_gain_grad = head_owner(
        qkv_sum, (query_weight, key_weight, value_weight), own_gains[0:1]
    )
    route = [(8 * z + p, layers * p + z) for z in range(layers) for p in range(8)]
    output_grad = out_owner(lax.ppermute(out_sum, ALL, route), share, width)
    return (
        layer_out[None],
        input_grad[None],
        attn_gain_grad[0],
        query_grad,
        key_grad,
        value_grad,
        output_grad,
        ffn_gain_grad[0],
        gate_grad,
        up_grad,
        down_grad,
    )


def solution(mesh):
    blocks = mesh.shape["seq"]
    fine = Mesh(mesh.devices.reshape(blocks // 4, 2, 2, 2), ALL)
    tokens = P("c", ("z", "y", "x"), None)
    weight = P(ALL, None)
    gain = P(ALL)
    in_specs = (
        tokens,
        P("c", ("z", "y", "x")),
        gain,
        weight,
        weight,
        weight,
        weight,
        gain,
        weight,
        weight,
        weight,
        tokens,
    )
    out_specs = (
        tokens,
        tokens,
        gain,
        weight,
        weight,
        weight,
        weight,
        gain,
        weight,
        weight,
        weight,
    )
    return jax.shard_map(body, mesh=fine, in_specs=in_specs, out_specs=out_specs, check_vma=False)
```

time: 709 us -> 591 us (0.83)
  Pallas kernels: 107 us -> 194 us
  waiting for transfers between devices: 253 us -> 193 us
  matrix products: 52.9 us -> 0 us
  starting transfers between devices: 120 us -> 70.8 us
  local copies, waits for them, and re-layouts: 97.8 us -> 65.9 us
    pallas_call x7 -> x33, Pallas kernels: 67 us -> 165 us  [the longest x2 45.8 us: ffn(): pl.pallas_call(functools.partial(ffn_kernel, count, len(carried) + len(ot...]
    dot_general x8 -> x0, matrix products: 52.9 us -> none  [dot(): return lax.dot_general(left, right, dims, preferred_element_type=F32)]
    ppermute x10 -> x2, waiting for transfers between devices: 51.2 us -> 17.2 us  [the longest x1 17.2 us: body(): output_grad = out_owner(lax.ppermute(out_sum, ALL, route), share, width)]
    all_to_all x5 -> x3, starting transfers between devices: 40.1 us -> 15.1 us  [the longest x1 5.48 us: body(): gate_up_sum = lax.all_to_all(gate_up_sum, PLANE, 0, 0, tiled=True)]
    ppermute x10 -> x2, starting transfers between devices: 22 us -> 3.46 us  [the longest x1 1.92 us: body(): output_grad = out_owner(lax.ppermute(out_sum, ALL, route), share, width)]
    all_gather x1 -> x2, waiting for transfers between devices: 0.01 us -> 16.8 us  [the longest x1 9.9 us: body(): attn_weight = lax.all_gather(attn_weight, 'z', axis=0, tiled=True)]
    ppermute x56 -> x64, waiting for transfers between devices: 130 us -> 113 us  [swap(): return lax.ppermute(block, axis, SWAP)]
    all_to_all x5 -> x3, waiting for transfers between devices: 43.6 us -> 27.5 us  [the longest x1 19.1 us: body(): gate_up_sum = lax.all_to_all(gate_up_sum, PLANE, 0, 0, tiled=True)]
  transfers between devices with their start and end apart: 81 -> 78, of which waited for: 31 -> 27; matrix products, arithmetic and copies ran while one was open for 23% -> 9% of each run, Pallas kernels for 12% -> 31%
where the time goes in v3:
time: 591 us; the launch traced here: 582 us
  Pallas kernels  194 us (33%)
  waiting for transfers between devices  193 us (33%)
  starting transfers between devices  70.8 us (12%)
  local copies, waits for them, and re-layouts  65.9 us (11%)
  other arithmetic  28.7 us (5%)
  between operations  15.5 us (3%)
  blocking collectives  14.1 us (2%)
    ppermute x64, waiting for transfers between devices, swap(): return lax.ppermute(block, axis, SWAP)  113 us
    unnamed x162, local copies, waits for them, and re-layouts  51.6 us
    pallas_call x2, Pallas kernels, ffn(): pl.pallas_call(functools.partial(ffn_kernel, count, len(carried) + len(ot...  45.8 us
    ppermute x64, starting transfers between devices, swap(): return lax.ppermute(block, axis, SWAP)  37.1 us
    pallas_call x2, Pallas kernels, split(): pl.pallas_call(functools.partial(split_kernel, order, dims), grid=(len(or...  25.3 us
    all_to_all x1, waiting for transfers between devices, body(): gate_up_sum = lax.all_to_all(gate_up_sum, PLANE, 0, 0, tiled=True)  19.1 us
    ppermute x1, waiting for transfers between devices, body(): output_grad = out_owner(lax.ppermute(out_sum, ALL, route), share, width)  17.2 us
    pallas_call x1, Pallas kernels, unit_sums(): pl.pallas_call(unit_sums_kernel, grid=(2,), in_specs=[pl.BlockSpec((token...  15.4 us
  transfers between devices with their start and end apart: 78, of which 27 were waited for; matrix products, arithmetic and copies ran while one was open for 9% of the time, Pallas kernels for 31%

profile of v3, /device:TPU:26, one launch (start us, length us, event | category | flops | bytes accessed | tf_op | source)
XLA Modules:
  0.0 581.7 jit_solution(16122710827456164904)
XLA Ops:
  14.0 14.1 %all_to_all.30.refs_0_.heads_ref = bf16[8,56,768]{2,1,0:T(8,128)(2,1)S(1)} all-to-all(bf16[8,56,768]{2,1,0:T(8,128)(2,1)S(1)} %shard_map.203), channel_id=1, replica_groups=mesh['z'=4,'y'=2,'x'=2,'c'=2] {'y','x','c'}, dimensions={0} | all-to-all | bytes 1376256 | tf_op jit(solution)/shard_map/all_to_all | solution.py:1050
  30.2 20.3 %collective-permute-done.1.x_ref.refs_1_ = bf16[256,1792]{1,0:T(8,128)(2,1)S(1)} collective-permute-done((bf16[256,1792]{1,0:T(8,128)(2,1)S(1)}, bf16[256,1792]{1,0:T(8,128)(2,1)S(1)}, u32[]{:S(2)}, u32[]{:S(2)}) %collective-permute-start.1) | collective-permute-done | bytes 917536 | tf_op jit(solution)/shard_map/ppermute | solution.py:34
  51.4 6.9 %all-gather.4.cloned.1.call-done.refs_0_.refs_13_.refs_5_.right_ref = bf16[640,1792]{1,0:T(8,128)(2,1)} async-done(((bf16[160,1792]{1,0:T(8,128)(2,1)}), bf16[640,1792]{1,0:T(8,128)(2,1)}) %all-gather.4.cloned.1.call-update) | async-done | bytes 2293776 | tf_op jit(solution)/shard_map/all_gather | solution.py:1049
  65.8 4.5 all-to-all-start.2
  78.0 7.4 %all-to-all-done.2 = bf16[8,56,1280]{2,1,0:T(8,128)(2,1)} async-done(((bf16[8,56,1280]{2,1,0:T(8,128)(2,1)}), bf16[8,56,1280]{2,1,0:T(8,128)(2,1)}, u32[]{:S(2)}, u32[]{:S(2)}) %all-to-all-start.2) | async-done | bytes 1146912 | tf_op jit(solution)/shard_map/all_to_all | solution.py:1062
  85.4 8.6 %collective-permute-done.5.first_ref = bf16[128,1792]{1,0:T(8,128)(2,1)S(1)} collective-permute-done((bf16[128,1792]{1,0:T(8,128)(2,1)}, bf16[128,1792]{1,0:T(8,128)(2,1)S(1)}, u32[]{:S(2)}, u32[]{:S(2)}) %collective-permute-start.5) | collective-permute-done | bytes 458784 | tf_op jit(solution)/shard_map/ppermute | solution.py:34
  99.3 2.2 constant_dynamic-update-slice_fusion.4
  106.7 4.6 multiply_reduce_fusion
  111.7 8.6 %collective-permute-done.8.x_ref.refs_8_ = bf16[256,1792]{1,0:T(8,128)(2,1)} collective-permute-done((bf16[256,1792]{1,0:T(8,128)(2,1)}, bf16[256,1792]{1,0:T(8,128)(2,1)}, u32[]{:S(2)}, u32[]{:S(2)}) %collective-permute-start.8) | collective-permute-done | bytes 917536 | tf_op jit(solution)/shard_map/ppermute | solution.py:34
  122.9 9.9 %all-gather.6.cloned.1.call-done.weight_ref.right_ref = bf16[1792,1024]{1,0:T(8,128)(2,1)} async-done(((bf16[448,1024]{1,0:T(8,128)(2,1)}), bf16[1792,1024]{1,0:T(8,128)(2,1)}) %all-gather.6.cloned.1.call-update) | async-done | bytes 3670032 | tf_op jit(solution)/shard_map/all_gather | solution.py:1058
  138.3 11.8 %shard_map.210 = (bf16[2048,1792]{1,0:T(8,128)(2,1)}, bf16[2048,768]{1,0:T(8,128)(2,1)}, f32[8,1792]{1,0:T(8,128)S(1)}) custom-call(bf16[2048,1792]{1,0:T(8,128)(2,1)} %constant_dynamic-update-slice_fusion.stream_ref, f32[2048,1]{1,0:T(8,128)S(1)} %copy.31.factor_ref, bf16[1792,1024]{1,0:T(8,128)(2,1)S(1)} %copy-done.12, bf16[128,1792]{1,0:T(8,128)(2,1)S(1)} %copy-done.33), custom_call_target="tpu_custom_call" | custom-call | flops 13200000000 | bytes 42000000 | tf_op jit(solution)/shard_map/pallas_call | solution.py:400
  153.6 11.2 %collective-permute-done.10.halo_ref.refs_0_ = bf16[2,64,512]{2,1,0:T(8,128)(2,1)S(1)} collective-permute-done((bf16[2,64,512]{2,1,0:T(8,128)(2,1)S(1)}, bf16[2,64,512]{2,1,0:T(8,128)(2,1)S(1)}, u32[]{:S(2)}, u32[]{:S(2)}) %collective-permute-start.10) | collective-permute-done | bytes 131104 | tf_op jit(solution)/shard_map/ppermute | solution.py:1074
  168.5 6.2 %shard_map.211 = (bf16[8,256,256]{2,1,0:T(8,128)(2,1)}, bf16[8,256,256]{2,1,0:T(8,128)(2,1)}) custom-call(s32[5]{0:T(128)S(1)} %pad_add_fusion.info_ref, bf16[8,256,768]{2,1,0:T(8,128)(2,1)S(1)} %bitcast.41, bf16[8,256,768]{2,1,0:T(8,128)(2,1)S(1)} %bitcast.42, bf16[2,64,512]{2,1,0:T(8,128)(2,1)S(1)} %collective-permute-done.10.halo_ref.refs_0_), custom_call_target="tpu_custom_call" | custom-call | flops 8800000000 | bytes 28000000 | tf_op jit(solution)/shard_map/pallas_call | solution.py:914
  174.7 3.8 collective-permute-done.16.first_ref
  181.9 4.5 all-to-all-start.1
  186.7 14.0 %collective-permute-done.20.second_ref = bf16[128,1792]{1,0:T(8,128)(2,1)} collective-permute-done((bf16[128,1792]{1,0:T(8,128)(2,1)S(1)}, bf16[128,1792]{1,0:T(8,128)(2,1)}, u32[]{:S(2)}, u32[]{:S(2)}) %collective-permute-start.20) | collective-permute-done | bytes 458784 | tf_op jit(solution)/shard_map/ppermute | solution.py:34
  203.8 7.9 %shard_map.214 = bf16[4,8,64,1792]{3,2,1,0:T(8,128)(2,1)} custom-call(s32[5]{0:T(128)S(1)} %pad_add_fusion.info_ref, bf16[1792,256]{1,0:T(8,128)(2,1)S(1)} %slice.117.refs_0_, bf16[1792,256]{1,0:T(8,128)(2,1)} %collective-permute-done.11.refs_1_, bf16[1792,256]{1,0:T(8,128)(2,1)} %collective-permute-done.12.x_ref.refs_2_, ...), custom_call_target="tpu_custom_call" | custom-call | flops 6600000000 | bytes 21000000 | tf_op jit(solution)/shard_map/pallas_call | solution.py:272
  212.9 3.1 copy-done.47
  216.0 3.8 shard_map.216
  221.1 21.6 %collective-permute-done.21.x_ref.refs_2_ = bf16[256,1792]{1,0:T(8,128)(2,1)S(1)} collective-permute-done((bf16[256,1792]{1,0:T(8,128)(2,1)S(1)}, bf16[256,1792]{1,0:T(8,128)(2,1)S(1)}, u32[]{:S(2)}, u32[]{:S(2)}) %collective-permute-start.21) | collective-permute-done | bytes 917536 | tf_op jit(solution)/shard_map/ppermute | solution.py:34
  247.1 30.0 %shard_map.219 = (bf16[2048,640]{1,0:T(8,128)(2,1)}, bf16[2048,1280]{1,0:T(8,128)(2,1)}, bf16[2048,1792]{1,0:T(8,128)(2,1)}, bf16[2048,1792]{1,0:T(8,128)(2,1)},...) custom-call(bf16[256,1792]{1,0:T(8,128)(2,1)} %copy-done.24, ...), custom_call_target="tpu_custom_call" | custom-call | flops 28600000512 | bytes 91000000 | tf_op jit(solution)/shard_map/pallas_call | solution.py:566
  284.5 15.8 %shard_map.221 = (bf16[2048,640]{1,0:T(8,128)(2,1)}, bf16[2048,1280]{1,0:T(8,128)(2,1)}, bf16[2048,1792]{1,0:T(8,128)(2,1)}, bf16[2048,1792]{1,0:T(8,128)(2,1)},...) custom-call(bf16[256,1792]{1,0:T(8,128)(2,1)} %copy-done.27, ...), custom_call_target="tpu_custom_call", output_to_operand_aliasing={{0}: (6, {}), {1}: (7, {}), {2}: (8, {}), {3}: (9, {})} | custom-call | flops 11000000512 | bytes 35000000 | tf_op jit(solution)/shard_map/pallas_call | solution.py:566
  307.5 15.4 %shard_map.223.refs_0_ = bf16[4,3360,256]{2,1,0:T(8,128)(2,1)} custom-call(bf16[2048,1792]{1,0:T(8,128)(2,1)} %get-tuple-element.94.hidden_ref, bf16[2048,1280]{1,0:T(8,128)(2,1)} %get-tuple-element.95.grads_ref, bf16[256,1792]{1,0:T(8,128)(2,1)} %copy-done.10, bf16[2,64,1792]{2,1,0:T(8,128)(2,1)} %collective-permute-done.34.refs_1_), custom_call_target="tpu_custom_call" | custom-call | flops 15399999488 | bytes 49000000 | tf_op jit(solution)/shard_map/pallas_call | solution.py:652
  325.1 10.5 %shard_map.224.refs_0_ = bf16[4,3360,256]{2,1,0:T(8,128)(2,1)} custom-call(bf16[2048,640]{1,0:T(8,128)(2,1)} %get-tuple-element.92.inner_ref.left_ref, bf16[2048,1792]{1,0:T(8,128)(2,1)} %get-tuple-element.93.top_ref, bf16[4,3360,256]{2,1,0:T(8,128)(2,1)} %shard_map.223.refs_0_, ...), custom_call_target="tpu_custom_call", output_to_operand_aliasing={{}: (2, {})} | custom-call | flops 11000000512 | bytes 35000000 | tf_op jit(solution)/shard_map/pallas_call | solution.py:673
  336.8 2.5 collective-permute-done.42
  342.4 12.9 %shard_map.225 = (bf16[256,1792]{1,0:T(8,128)(2,1)}, bf16[256,1792]{1,0:T(8,128)(2,1)}, bf16[256,1792]{1,0:T(8,128)(2,1)}, bf16[256,1792]{1,0:T(8,128)(2,1)}, bf...) custom-call(bf16[2048,640]{1,0:T(8,128)(2,1)} %get-tuple-element.92., ...), custom_call_target="tpu_custom_call" | custom-call | flops 15399999488 | bytes 49000000 | tf_op jit(solution)/shard_map/pallas_call | solution.py:611
  355.4 7.7 %collective-permute-done.43.x_ref = bf16[256,1792]{1,0:T(8,128)(2,1)S(1)} collective-permute-done((bf16[256,1792]{1,0:T(8,128)(2,1)S(1)}, bf16[256,1792]{1,0:T(8,128)(2,1)S(1)}, u32[]{:S(2)}, u32[]{:S(2)}) %collective-permute-start.43) | collective-permute-done | bytes 917536 | tf_op jit(solution)/shard_map/ppermute | solution.py:34
  365.5 10.8 %shard_map.226 = (bf16[8,256,256]{2,1,0:T(8,128)(2,1)}, f32[256,1792]{1,0:T(8,128)}, bf16[256,1792]{1,0:T(8,128)(2,1)S(1)}) custom-call(f32[256,1792]{1,0:T(8,128)} %convert_add_fusion.4.here_ref, bf16[256,1792]{1,0:T(8,128)(2,1)S(1)} %collective-permute-done.43.x_ref, bf16[256,1792]{1,0:T(8,128)(2,1)S(1)} %collective-permute-done.44.y_ref, ...), custom_call_target="tpu_custom_call" | custom-call | flops 13200000000 | bytes 42000000 | tf_op jit(solution)/shard_map/pallas_call | solution.py:478
  376.3 4.4 all-to-all-start.3
  383.4 2.9 convert_add_fusion.3
  386.3 8.4 %all-to-all-done.3.top_ref = bf16[8,256,256]{2,1,0:T(8,128)(2,1)S(1)} async-done(((bf16[8,256,256]{2,1,0:T(8,128)(2,1)}), bf16[8,256,256]{2,1,0:T(8,128)(2,1)S(1)}, u32[]{:S(2)}, u32[]{:S(2)}) %all-to-all-start.3) | async-done | bytes 1048608 | tf_op jit(solution)/shard_map/all_to_all | solution.py:1108
  396.5 8.5 %shard_map.227 = (bf16[8,256,768]{2,1,0:T(8,128)(2,1)S(1)}, f32[2,64,512]{2,1,0:T(8,128)S(1)}, bf16[2,64,512]{2,1,0:T(8,128)(2,1)S(1)}) custom-call(s32[5]{0:T(128)S(1)} %pad_add_fusion.info_ref, bf16[8,256,768]{2,1,0:T(8,128)(2,1)S(1)} %bitcast.43, bf16[8,256,768]{2,1,0:T(8,128)(2,1)S(1)} %bitcast.44, ...), custom_call_target="tpu_custom_call" | custom-call | flops 18699999232 | bytes 59500000 | tf_op jit(solution)/shard_map/pallas_call | solution.py:1007
  407.4 11.1 %shard_map.229.refs_0_.refs_9_ = bf16[4,1792,256]{2,1,0:T(8,128)(2,1)} custom-call(bf16[2048,1792]{1,0:T(8,128)(2,1)} %get-tuple-element.98.hidden_ref, bf16[2048,768]{1,0:T(8,128)(2,1)} %bitcast.32, bf16[128,1792]{1,0:T(8,128)(2,1)} %bitcast.14.rim_ref, bf16[128,512]{1,0:T(8,128)(2,1)} %bitcast.50), custom_call_target="tpu_custom_call" | custom-call | flops 12099999744 | bytes 38500000 | tf_op jit(solution)/shard_map/pallas_call | solution.py:763
  418.6 4.5 collective-permute-start.50
  427.8 2.3 shard_map.231
  432.5 2.7 slice.169
  437.2 2.5 shard_map.230
  439.7 8.3 %collective-permute-done.56.first_ref = bf16[128,1792]{1,0:T(8,128)(2,1)S(1)} collective-permute-done((bf16[128,1792]{1,0:T(8,128)(2,1)}, bf16[128,1792]{1,0:T(8,128)(2,1)S(1)}, u32[]{:S(2)}, u32[]{:S(2)}) %collective-permute-start.56) | collective-permute-done | bytes 458784 | tf_op jit(solution)/shard_map/ppermute | solution.py:34
  457.0 6.1 %shard_map.233.refs_0_ = bf16[4,1792,256]{2,1,0:T(8,128)(2,1)S(1)} custom-call(bf16[256,1792]{1,0:T(8,128)(2,1)S(1)} %get-tuple-element.117.refs_0_, bf16[256,1792]{1,0:T(8,128)(2,1)S(1)} %collective-permute-done.51.refs_1_, bf16[256,1792]{1,0:T(8,128)(2,1)} %collective-permute-done.52.x_ref.refs_2_, ...), custom_call_target="tpu_custom_call", output_to_operand_aliasing={{}: (9, {})} | custom-call | flops 6600000000 | bytes 21000000 | tf_op jit(solution)/shard_map/pallas_call | solution.py:786
  465.0 12.4 %shard_map.234 = (bf16[256,1792]{1,0:T(8,128)(2,1)}, bf16[256,1792]{1,0:T(8,128)(2,1)}, bf16[256,1792]{1,0:T(8,128)(2,1)}, bf16[256,1792]{1,0:T(8,128)(2,1)}, bf...) custom-call(bf16[2048,768]{1,0:T(8,128)(2,1)} %bitcast.33, ...), custom_call_target="tpu_custom_call" | custom-call | flops 15399999488 | bytes 49000000 | tf_op jit(solution)/shard_map/pallas_call | solution.py:611
  487.3 6.8 %collective-permute-done.62 = bf16[128,1792]{1,0:T(8,128)(2,1)S(1)} collective-permute-done((bf16[128,1792]{1,0:T(8,128)(2,1)S(1)}, bf16[128,1792]{1,0:T(8,128)(2,1)S(1)}, u32[]{:S(2)}, u32[]{:S(2)}) %collective-permute-start.62) | collective-permute-done | bytes 458784 | tf_op jit(solution)/shard_map/ppermute | solution.py:34
  503.8 5.5 all-to-all-start.4
  509.4 3.5 add_convert_fusion.refs_1_
  514.4 19.1 %all-to-all-done.4.sheet_ref = bf16[8,5,56,256]{3,2,1,0:T(8,128)(2,1)S(1)} async-done(((bf16[8,5,56,256]{3,2,1,0:T(8,128)(2,1)}), bf16[8,5,56,256]{3,2,1,0:T(8,128)(2,1)S(1)}, u32[]{:S(2)}, u32[]{:S(2)}) %all-to-all-start.4) | async-done | bytes 1146912 | tf_op jit(solution)/shard_map/all_to_all | solution.py:1129
  534.6 2.9 shard_map.236
  538.8 4.0 shard_map.237.refs_0_
  546.5 5.3 all-to-all-start.5
  555.5 17.2 %collective-permute-done.67.piece_ref = bf16[448,256]{1,0:T(8,128)(2,1)S(1)} collective-permute-done((bf16[448,256]{1,0:T(8,128)(2,1)S(1)}, bf16[448,256]{1,0:T(8,128)(2,1)S(1)}, u32[]{:S(2)}, u32[]{:S(2)}) %collective-permute-start.67) | collective-permute-done | bytes 229408 | tf_op jit(solution)/shard_map/ppermute | solution.py:1145
  (366 shorter events, 147.4 us)
Async XLA Ops:
  7.2 51.2 %all-gather.4.cloned.1.call-start = ((), (), s32[]{:S(2)}) async-start(), calls=%async_computation.8 | async-start | bytes 2867200 | tf_op jit(solution)/shard_map/all_gather | solution.py:1049
  9.1 123.7 %all-gather.6.cloned.1.call-start = ((), (), s32[]{:S(2)}) async-start(), calls=%async_computation.9 | async-start | bytes 4587520 | tf_op jit(solution)/shard_map/all_gather | solution.py:1058
  28.1 22.3 %collective-permute-start.1 = (bf16[256,1792]{1,0:T(8,128)(2,1)S(1)}, bf16[256,1792]{1,0:T(8,128)(2,1)S(1)}, u32[]{:S(2)}, u32[]{:S(2)}) collective-permute-start(bf16[256,1792]{1,0:T(8,128)(2,1)S(1)} %shard_map.204), channel_id=1, source_target_pairs={{0,2},{2,0},{1,3},{3,1},{4,6},{6,4},{5,7},{7,5},{8,10},{10,8},{9,1... | collective-permute-start | bytes 2752520 | tf_op jit(solution)/shard_map/ppermute | solution.py:34
  29.7 21.8 %collective-permute-start.3 = (bf16[256,1792]{1,0:T(8,128)(2,1)S(1)}, bf16[256,1792]{1,0:T(8,128)(2,1)S(1)}, u32[]{:S(2)}, u32[]{:S(2)}) collective-permute-start(bf16[256,1792]{1,0:T(8,128)(2,1)S(1)} %shard_map.204), channel_id=1, source_target_pairs={{0,4},{4,0},{1,5},{5,1},{2,6},{6,2},{3,7},{7,3},{8,12},{12,8},{9,1... | collective-permute-start | bytes 2752520 | tf_op jit(solution)/shard_map/ppermute | solution.py:34
  70.2 176.8 %all-gather.8.cloned.1.call-start = ((), (), s32[]{:S(2)}) async-start(), calls=%async_computation.10 | async-start | bytes 5734400 | tf_op jit(solution)/shard_map/all_gather | solution.py:1063
  71.5 27.8 %collective-permute-start.2 = (bf16[256,1792]{1,0:T(8,128)(2,1)S(1)}, bf16[256,1792]{1,0:T(8,128)(2,1)}, u32[]{:S(2)}, u32[]{:S(2)}) collective-permute-start(bf16[256,1792]{1,0:T(8,128)(2,1)S(1)} %collective-permute-done.1.x_ref.refs_1_), channel_id=1, source_target_pairs={{0,1},{1,0},{2,3},{3,2},{4,5},{5,4},{6,7},{7,6},{8,9},{9,8},{10,11... | collective-permute-start | bytes 2752520 | tf_op jit(solution)/shard_map/ppermute | solution.py:34
  72.7 21.3 %collective-permute-start.5 = (bf16[128,1792]{1,0:T(8,128)(2,1)}, bf16[128,1792]{1,0:T(8,128)(2,1)S(1)}, u32[]{:S(2)}, u32[]{:S(2)}) collective-permute-start(bf16[128,1792]{1,0:T(8,128)(2,1)} %get-tuple-element.75), channel_id=1, source_target_pairs={{0,2},{2,0},{1,3},{3,1},{4,6},{6,4},{5,7},{7,5},{8,10},{10,8},{9,1... | collective-permute-start | bytes 1376264 | tf_op jit(solution)/shard_map/ppermute | solution.py:34
  73.1 22.1 %collective-permute-start.6 = (bf16[128,1792]{1,0:T(8,128)(2,1)}, bf16[128,1792]{1,0:T(8,128)(2,1)}, u32[]{:S(2)}, u32[]{:S(2)}) collective-permute-start(bf16[128,1792]{1,0:T(8,128)(2,1)} %get-tuple-element.76), channel_id=1, source_target_pairs={{0,4},{4,0},{1,5},{5,1},{2,6},{6,2},{3,7},{7,3},{8,12},{12,8},{9,1... | collective-permute-start | bytes 1376264 | tf_op jit(solution)/shard_map/ppermute | solution.py:34
  76.9 25.6 %collective-permute-start.4 = (bf16[256,1792]{1,0:T(8,128)(2,1)S(1)}, bf16[256,1792]{1,0:T(8,128)(2,1)}, u32[]{:S(2)}, u32[]{:S(2)}) collective-permute-start(bf16[256,1792]{1,0:T(8,128)(2,1)S(1)} %collective-permute-done.3.y_ref.refs_2_), channel_id=1, source_target_pairs={{0,1},{1,0},{2,3},{3,2},{4,5},{5,4},{6,7},{7,6},{8,9},{9,8},{10,11... | collective-permute-start | bytes 2752520 | tf_op jit(solution)/shard_map/ppermute | solution.py:34
  97.3 23.0 %collective-permute-start.8 = (bf16[256,1792]{1,0:T(8,128)(2,1)}, bf16[256,1792]{1,0:T(8,128)(2,1)}, u32[]{:S(2)}, u32[]{:S(2)}) collective-permute-start(bf16[256,1792]{1,0:T(8,128)(2,1)} %shard_map.208), channel_id=1, source_target_pairs={{0,2},{2,0},{1,3},{3,1},{4,6},{6,4},{5,7},{7,5},{8,10},{10,8},{9,1... | collective-permute-start | bytes 2752520 | tf_op jit(solution)/shard_map/ppermute | solution.py:34
  97.9 22.8 %collective-permute-start.9 = (bf16[256,1792]{1,0:T(8,128)(2,1)}, bf16[256,1792]{1,0:T(8,128)(2,1)}, u32[]{:S(2)}, u32[]{:S(2)}) collective-permute-start(bf16[256,1792]{1,0:T(8,128)(2,1)} %shard_map.208), channel_id=1, source_target_pairs={{0,4},{4,0},{1,5},{5,1},{2,6},{6,2},{3,7},{7,3},{8,12},{12,8},{9,1... | collective-permute-start | bytes 2752520 | tf_op jit(solution)/shard_map/ppermute | solution.py:34
  134.1 30.7 %collective-permute-start.12 = (bf16[1792,256]{1,0:T(8,128)(2,1)S(1)}, bf16[1792,256]{1,0:T(8,128)(2,1)}, u32[]{:S(2)}, u32[]{:S(2)}) collective-permute-start(bf16[1792,256]{1,0:T(8,128)(2,1)S(1)} %slice.117.refs_0_), channel_id=1, source_target_pairs={{0,2},{2,0},{1,3},{3,1},{4,6},{6,4},{5,7},{7,5},{8,10},{10,8},{9,1... | collective-permute-start | bytes 2752520 | tf_op jit(solution)/shard_map/ppermute | solution.py:34
  134.5 30.3 %collective-permute-start.14 = (bf16[1792,256]{1,0:T(8,128)(2,1)S(1)}, bf16[1792,256]{1,0:T(8,128)(2,1)}, u32[]{:S(2)}, u32[]{:S(2)}) collective-permute-start(bf16[1792,256]{1,0:T(8,128)(2,1)S(1)} %slice.117.refs_0_), channel_id=1, source_target_pairs={{0,4},{4,0},{1,5},{5,1},{2,6},{6,2},{3,7},{7,3},{8,12},{12,8},{9,1... | collective-permute-start | bytes 2752520 | tf_op jit(solution)/shard_map/ppermute | solution.py:34
  152.4 28.5 %collective-permute-start.19 = (bf16[128,1792]{1,0:T(8,128)(2,1)S(1)}, bf16[128,1792]{1,0:T(8,128)(2,1)S(1)}, u32[]{:S(2)}, u32[]{:S(2)}) collective-permute-start(bf16[128,1792]{1,0:T(8,128)(2,1)S(1)} %copy-done.33), channel_id=1, source_target_pairs={{0,2},{2,0},{1,3},{3,1},{4,6},{6,4},{5,7},{7,5},{8,10},{10,8},{9,1... | collective-permute-start | bytes 1376264 | tf_op jit(solution)/shard_map/ppermute | solution.py:34
  153.6 50.1 %collective-permute-start.11 = (bf16[1792,256]{1,0:T(8,128)(2,1)S(1)}, bf16[1792,256]{1,0:T(8,128)(2,1)}, u32[]{:S(2)}, u32[]{:S(2)}) collective-permute-start(bf16[1792,256]{1,0:T(8,128)(2,1)S(1)} %slice.117.refs_0_), channel_id=1, source_target_pairs={{0,1},{1,0},{2,3},{3,2},{4,5},{5,4},{6,7},{7,6},{8,9},{9,8},{10,11... | collective-permute-start | bytes 2752520 | tf_op jit(solution)/shard_map/ppermute | solution.py:34
  174.7 29.1 %collective-permute-start.13 = (bf16[1792,256]{1,0:T(8,128)(2,1)}, bf16[1792,256]{1,0:T(8,128)(2,1)}, u32[]{:S(2)}, u32[]{:S(2)}) collective-permute-start(bf16[1792,256]{1,0:T(8,128)(2,1)} %collective-permute-done.12.x_ref.refs_2_), channel_id=1, source_target_pairs={{0,1},{1,0},{2,3},{3,2},{4,5},{5,4},{6,7},{7,6},{8,9},{9,8},{10,11... | collective-permute-start | bytes 2752520 | tf_op jit(solution)/shard_map/ppermute | solution.py:34
  178.4 25.3 %collective-permute-start.15 = (bf16[1792,256]{1,0:T(8,128)(2,1)}, bf16[1792,256]{1,0:T(8,128)(2,1)}, u32[]{:S(2)}, u32[]{:S(2)}) collective-permute-start(bf16[1792,256]{1,0:T(8,128)(2,1)} %collective-permute-done.14.y_ref.refs_4_), channel_id=1, source_target_pairs={{0,1},{1,0},{2,3},{3,2},{4,5},{5,4},{6,7},{7,6},{8,9},{9,8},{10,11... | collective-permute-start | bytes 2752520 | tf_op jit(solution)/shard_map/ppermute | solution.py:34
  180.9 22.9 %collective-permute-start.18 = (bf16[1792,256]{1,0:T(8,128)(2,1)}, bf16[1792,256]{1,0:T(8,128)(2,1)}, u32[]{:S(2)}, u32[]{:S(2)}) collective-permute-start(bf16[1792,256]{1,0:T(8,128)(2,1)} %shard_map.213.refs_6_), channel_id=1, source_target_pairs={{0,1},{1,0},{2,3},{3,2},{4,5},{5,4},{6,7},{7,6},{8,9},{9,8},{10,11... | collective-permute-start | bytes 2752520 | tf_op jit(solution)/shard_map/ppermute | solution.py:34
  181.9 29.7 %all-to-all-start.1 = ((bf16[8,256,256]{2,1,0:T(8,128)(2,1)}), bf16[8,256,256]{2,1,0:T(8,128)(2,1)S(1)}, u32[]{:S(2)}, u32[]{:S(2)}) async-start(bf16[8,256,256]{2,1,0:T(8,128)(2,1)} %get-tuple-element.79.refs_0_), calls=%async_computation.1 | async-start | bytes 2097152 | tf_op jit(solution)/shard_map/all_to_all | solution.py:1086
  186.4 315.1 %reduce-scatter.3.cloned.1.call-start = ((), (), s32[]{:S(2)}) async-start(), calls=%async_computation.11 | async-start | bytes 8601600 | tf_op jit(solution)/shard_map/reduce_scatter | solution.py:1102
  219.8 22.9 %collective-permute-start.21 = (bf16[256,1792]{1,0:T(8,128)(2,1)S(1)}, bf16[256,1792]{1,0:T(8,128)(2,1)S(1)}, u32[]{:S(2)}, u32[]{:S(2)}) collective-permute-start(bf16[256,1792]{1,0:T(8,128)(2,1)S(1)} %get-tuple-element.85.refs_0_), channel_id=1, source_target_pairs={{0,2},{2,0},{1,3},{3,1},{4,6},{6,4},{5,7},{7,5},{8,10},{10,8},{9,1... | collective-permute-start | bytes 2752520 | tf_op jit(solution)/shard_map/ppermute | solution.py:34
  219.8 22.9 %collective-permute-start.22 = (bf16[256,1792]{1,0:T(8,128)(2,1)S(1)}, bf16[256,1792]{1,0:T(8,128)(2,1)S(1)}, u32[]{:S(2)}, u32[]{:S(2)}) collective-permute-start(bf16[256,1792]{1,0:T(8,128)(2,1)S(1)} %get-tuple-element.85.refs_0_), channel_id=1, source_target_pairs={{0,4},{4,0},{1,5},{5,1},{2,6},{6,2},{3,7},{7,3},{8,12},{12,8},{9,1... | collective-permute-start | bytes 2752520 | tf_op jit(solution)/shard_map/ppermute | solution.py:34
  220.2 23.8 %collective-permute-start.29 = (bf16[256,1792]{1,0:T(8,128)(2,1)}, bf16[256,1792]{1,0:T(8,128)(2,1)S(1)}, u32[]{:S(2)}, u32[]{:S(2)}) collective-permute-start(bf16[256,1792]{1,0:T(8,128)(2,1)} %collective-permute-done.8.x_ref.refs_8_), channel_id=1, source_target_pairs={{0,1},{1,0},{2,3},{3,2},{4,5},{5,4},{6,7},{7,6},{8,9},{9,8},{10,11... | collective-permute-start | bytes 2752520 | tf_op jit(solution)/shard_map/ppermute | solution.py:34
  220.5 23.8 %collective-permute-start.30 = (bf16[256,1792]{1,0:T(8,128)(2,1)}, bf16[256,1792]{1,0:T(8,128)(2,1)S(1)}, u32[]{:S(2)}, u32[]{:S(2)}) collective-permute-start(bf16[256,1792]{1,0:T(8,128)(2,1)} %collective-permute-done.9.y_ref.refs_10_), channel_id=1, source_target_pairs={{0,1},{1,0},{2,3},{3,2},{4,5},{5,4},{6,7},{7,6},{8,9},{9,8},{10,11... | collective-permute-start | bytes 2752520 | tf_op jit(solution)/shard_map/ppermute | solution.py:34
  220.7 25.1 %collective-permute-start.25 = (bf16[256,1792]{1,0:T(8,128)(2,1)S(1)}, bf16[256,1792]{1,0:T(8,128)(2,1)S(1)}, u32[]{:S(2)}, u32[]{:S(2)}) collective-permute-start(bf16[256,1792]{1,0:T(8,128)(2,1)S(1)} %get-tuple-element.85.refs_0_), channel_id=1, source_target_pairs={{0,1},{1,0},{2,3},{3,2},{4,5},{5,4},{6,7},{7,6},{8,9},{9,8},{10,11... | collective-permute-start | bytes 2752520 | tf_op jit(solution)/shard_map/ppermute | solution.py:34
  244.0 39.5 %collective-permute-start.32 = (bf16[256,1792]{1,0:T(8,128)(2,1)S(1)}, bf16[256,1792]{1,0:T(8,128)(2,1)}, u32[]{:S(2)}, u32[]{:S(2)}) collective-permute-start(bf16[256,1792]{1,0:T(8,128)(2,1)S(1)} %copy-done.23), channel_id=1, source_target_pairs={{0,1},{1,0},{2,3},{3,2},{4,5},{5,4},{6,7},{7,6},{8,9},{9,8},{10,11... | collective-permute-start | bytes 2752520 | tf_op jit(solution)/shard_map/ppermute | solution.py:34
  244.3 32.7 %collective-permute-start.23 = (bf16[128,1792]{1,0:T(8,128)(2,1)}, bf16[128,1792]{1,0:T(8,128)(2,1)}, u32[]{:S(2)}, u32[]{:S(2)}) collective-permute-start(bf16[128,1792]{1,0:T(8,128)(2,1)} %get-tuple-element.86), channel_id=1, source_target_pairs={{0,2},{2,0},{1,3},{3,1},{4,6},{6,4},{5,7},{7,5},{8,10},{10,8},{9,1... | collective-permute-start | bytes 1376264 | tf_op jit(solution)/shard_map/ppermute | solution.py:34
  246.8 30.3 %collective-permute-start.24 = (bf16[128,1792]{1,0:T(8,128)(2,1)S(1)}, bf16[128,1792]{1,0:T(8,128)(2,1)}, u32[]{:S(2)}, u32[]{:S(2)}) collective-permute-start(bf16[128,1792]{1,0:T(8,128)(2,1)S(1)} %get-tuple-element.87), channel_id=1, source_target_pairs={{0,4},{4,0},{1,5},{5,1},{2,6},{6,2},{3,7},{7,3},{8,12},{12,8},{9,1... | collective-permute-start | bytes 1376264 | tf_op jit(solution)/shard_map/ppermute | solution.py:34
  281.4 26.1 %collective-permute-start.34 = (bf16[2,64,1792]{2,1,0:T(8,128)(2,1)S(1)}, bf16[2,64,1792]{2,1,0:T(8,128)(2,1)}, u32[]{:S(2)}, u32[]{:S(2)}) collective-permute-start(bf16[2,64,1792]{2,1,0:T(8,128)(2,1)S(1)} %constant_dynamic-slice_fusion), channel_id=1, source_target_pairs={{0,8},{8,16},{16,24},{1,9},{9,17},{17,25},{2,10},{10,18},{18,26},{... | collective-permute-start | bytes 1376264 | tf_op jit(solution)/shard_map/ppermute | solution.py:1085
  340.7 22.4 %collective-permute-start.43 = (bf16[256,1792]{1,0:T(8,128)(2,1)S(1)}, bf16[256,1792]{1,0:T(8,128)(2,1)S(1)}, u32[]{:S(2)}, u32[]{:S(2)}) collective-permute-start(bf16[256,1792]{1,0:T(8,128)(2,1)S(1)} %copy-done.69), channel_id=1, source_target_pairs={{0,2},{2,0},{1,3},{3,1},{4,6},{6,4},{5,7},{7,5},{8,10},{10,8},{9,1... | collective-permute-start | bytes 2752520 | tf_op jit(solution)/shard_map/ppermute | solution.py:34
  342.2 22.1 %collective-permute-start.44 = (bf16[256,1792]{1,0:T(8,128)(2,1)S(1)}, bf16[256,1792]{1,0:T(8,128)(2,1)S(1)}, u32[]{:S(2)}, u32[]{:S(2)}) collective-permute-start(bf16[256,1792]{1,0:T(8,128)(2,1)S(1)} %copy-done.70), channel_id=1, source_target_pairs={{0,4},{4,0},{1,5},{5,1},{2,6},{6,2},{3,7},{7,3},{8,12},{12,8},{9,1... | collective-permute-start | bytes 2752520 | tf_op jit(solution)/shard_map/ppermute | solution.py:34
  355.4 26.3 %collective-permute-start.47 = (bf16[256,1792]{1,0:T(8,128)(2,1)}, bf16[256,1792]{1,0:T(8,128)(2,1)}, u32[]{:S(2)}, u32[]{:S(2)}) collective-permute-start(bf16[256,1792]{1,0:T(8,128)(2,1)} %get-tuple-element.114), channel_id=1, source_target_pairs={{0,1},{1,0},{2,3},{3,2},{4,5},{5,4},{6,7},{7,6},{8,9},{9,8},{10,11... | collective-permute-start | bytes 2752520 | tf_op jit(solution)/shard_map/ppermute | solution.py:34
  380.7 162.2 %reduce-scatter.5.cloned.1.call-start = ((), (), s32[]{:S(2)}) async-start(), calls=%async_computation.12 | async-start | bytes 4587520 | tf_op jit(solution)/shard_map/reduce_scatter | solution.py:1125
  380.7 37.9 %collective-permute-start.41 = (bf16[256,1792]{1,0:T(8,128)(2,1)}, bf16[256,1792]{1,0:T(8,128)(2,1)}, u32[]{:S(2)}, u32[]{:S(2)}) collective-permute-start(bf16[256,1792]{1,0:T(8,128)(2,1)} %get-tuple-element.108), channel_id=1, source_target_pairs={{0,1},{1,0},{2,3},{3,2},{4,5},{5,4},{6,7},{7,6},{8,9},{9,8},{10,11... | collective-permute-start | bytes 2752520 | tf_op jit(solution)/shard_map/ppermute | solution.py:34
  380.8 49.4 %collective-permute-start.40 = (bf16[256,1792]{1,0:T(8,128)(2,1)}, bf16[256,1792]{1,0:T(8,128)(2,1)}, u32[]{:S(2)}, u32[]{:S(2)}) collective-permute-start(bf16[256,1792]{1,0:T(8,128)(2,1)} %get-tuple-element.106), channel_id=1, source_target_pairs={{0,1},{1,0},{2,3},{3,2},{4,5},{5,4},{6,7},{7,6},{8,9},{9,8},{10,11... | collective-permute-start | bytes 2752520 | tf_op jit(solution)/shard_map/ppermute | solution.py:34
  381.2 75.5 %collective-permute-start.51 = (bf16[256,1792]{1,0:T(8,128)(2,1)S(1)}, bf16[256,1792]{1,0:T(8,128)(2,1)S(1)}, u32[]{:S(2)}, u32[]{:S(2)}) collective-permute-start(bf16[256,1792]{1,0:T(8,128)(2,1)S(1)} %get-tuple-element.117.refs_0_), channel_id=1, source_target_pairs={{0,1},{1,0},{2,3},{3,2},{4,5},{5,4},{6,7},{7,6},{8,9},{9,8},{10,11... | collective-permute-start | bytes 2752520 | tf_op jit(solution)/shard_map/ppermute | solution.py:34
  381.3 44.3 %collective-permute-start.52 = (bf16[256,1792]{1,0:T(8,128)(2,1)S(1)}, bf16[256,1792]{1,0:T(8,128)(2,1)}, u32[]{:S(2)}, u32[]{:S(2)}) collective-permute-start(bf16[256,1792]{1,0:T(8,128)(2,1)S(1)} %get-tuple-element.117.refs_0_), channel_id=1, source_target_pairs={{0,2},{2,0},{1,3},{3,1},{4,6},{6,4},{5,7},{7,5},{8,10},{10,8},{9,1... | collective-permute-start | bytes 2752520 | tf_op jit(solution)/shard_map/ppermute | solution.py:34
  381.7 46.1 %collective-permute-start.54 = (bf16[256,1792]{1,0:T(8,128)(2,1)S(1)}, bf16[256,1792]{1,0:T(8,128)(2,1)}, u32[]{:S(2)}, u32[]{:S(2)}) collective-permute-start(bf16[256,1792]{1,0:T(8,128)(2,1)S(1)} %get-tuple-element.117.refs_0_), channel_id=1, source_target_pairs={{0,4},{4,0},{1,5},{5,1},{2,6},{6,2},{3,7},{7,3},{8,12},{12,8},{9,1... | collective-permute-start | bytes 2752520 | tf_op jit(solution)/shard_map/ppermute | solution.py:34
  425.7 24.7 %collective-permute-start.48 = (bf16[128,1792]{1,0:T(8,128)(2,1)}, bf16[128,1792]{1,0:T(8,128)(2,1)}, u32[]{:S(2)}, u32[]{:S(2)}) collective-permute-start(bf16[128,1792]{1,0:T(8,128)(2,1)} %get-tuple-element.142), channel_id=1, source_target_pairs={{0,2},{2,0},{1,3},{3,1},{4,6},{6,4},{5,7},{7,5},{8,10},{10,8},{9,1... | collective-permute-start | bytes 1376264 | tf_op jit(solution)/shard_map/ppermute | solution.py:34
  454.1 23.9 %collective-permute-start.49 = (bf16[256,1792]{1,0:T(8,128)(2,1)}, bf16[256,1792]{1,0:T(8,128)(2,1)}, u32[]{:S(2)}, u32[]{:S(2)}) collective-permute-start(bf16[256,1792]{1,0:T(8,128)(2,1)} %pad_maximum_fusion.3.refs_12_), channel_id=1, source_target_pairs={{0,4},{4,0},{1,5},{5,1},{2,6},{6,2},{3,7},{7,3},{8,12},{12,8},{9,1... | collective-permute-start | bytes 2752520 | tf_op jit(solution)/shard_map/ppermute | solution.py:34
  456.7 22.3 %collective-permute-start.46 = (bf16[256,1792]{1,0:T(8,128)(2,1)}, bf16[256,1792]{1,0:T(8,128)(2,1)}, u32[]{:S(2)}, u32[]{:S(2)}) collective-permute-start(bf16[256,1792]{1,0:T(8,128)(2,1)} %pad_maximum_fusion.2.refs_11_), channel_id=1, source_target_pairs={{0,2},{2,0},{1,3},{3,1},{4,6},{6,4},{5,7},{7,5},{8,10},{10,8},{9,1... | collective-permute-start | bytes 2752520 | tf_op jit(solution)/shard_map/ppermute | solution.py:34
  477.9 31.5 %collective-permute-start.39 = (bf16[256,1792]{1,0:T(8,128)(2,1)}, bf16[256,1792]{1,0:T(8,128)(2,1)}, u32[]{:S(2)}, u32[]{:S(2)}) collective-permute-start(bf16[256,1792]{1,0:T(8,128)(2,1)} %get-tuple-element.104), channel_id=1, source_target_pairs={{0,1},{1,0},{2,3},{3,2},{4,5},{5,4},{6,7},{7,6},{8,9},{9,8},{10,11... | collective-permute-start | bytes 2752520 | tf_op jit(solution)/shard_map/ppermute | solution.py:34
  478.0 34.9 %collective-permute-start.59 = (bf16[256,1792]{1,0:T(8,128)(2,1)}, bf16[256,1792]{1,0:T(8,128)(2,1)}, u32[]{:S(2)}, u32[]{:S(2)}) collective-permute-start(bf16[256,1792]{1,0:T(8,128)(2,1)} %get-tuple-element.122), channel_id=1, source_target_pairs={{0,1},{1,0},{2,3},{3,2},{4,5},{5,4},{6,7},{7,6},{8,9},{9,8},{10,11... | collective-permute-start | bytes 2752520 | tf_op jit(solution)/shard_map/ppermute | solution.py:34
  495.2 42.3 %collective-permute-start.63 = (bf16[256,1792]{1,0:T(8,128)(2,1)}, bf16[256,1792]{1,0:T(8,128)(2,1)}, u32[]{:S(2)}, u32[]{:S(2)}) collective-permute-start(bf16[256,1792]{1,0:T(8,128)(2,1)} %pad_maximum_fusion.4), channel_id=1, source_target_pairs={{0,2},{2,0},{1,3},{3,1},{4,6},{6,4},{5,7},{7,5},{8,10},{10,8},{9,1... | collective-permute-start | bytes 2752520 | tf_op jit(solution)/shard_map/ppermute | solution.py:34
  500.0 37.5 %collective-permute-start.66 = (bf16[256,1792]{1,0:T(8,128)(2,1)}, bf16[256,1792]{1,0:T(8,128)(2,1)}, u32[]{:S(2)}, u32[]{:S(2)}) collective-permute-start(bf16[256,1792]{1,0:T(8,128)(2,1)} %pad_maximum_fusion.5), channel_id=1, source_target_pairs={{0,4},{4,0},{1,5},{5,1},{2,6},{6,2},{3,7},{7,3},{8,12},{12,8},{9,1... | collective-permute-start | bytes 2752520 | tf_op jit(solution)/shard_map/ppermute | solution.py:34
  503.8 29.7 %all-to-all-start.4 = ((bf16[8,5,56,256]{3,2,1,0:T(8,128)(2,1)}), bf16[8,5,56,256]{3,2,1,0:T(8,128)(2,1)S(1)}, u32[]{:S(2)}, u32[]{:S(2)}) async-start(bf16[8,5,56,256]{3,2,1,0:T(8,128)(2,1)} %bitcast.55), calls=%async_computation.5 | async-start | bytes 2293760 | tf_op jit(solution)/shard_map/all_to_all | solution.py:1129
  546.5 26.9 %all-to-all-start.5 = ((bf16[8,3,56,256]{3,2,1,0:T(8,128)(2,1)}), bf16[8,3,56,256]{3,2,1,0:T(8,128)(2,1)S(1)}, u32[]{:S(2)}, u32[]{:S(2)}) async-start(bf16[8,3,56,256]{3,2,1,0:T(8,128)(2,1)} %get-tuple-element.131), calls=%async_computation.7 | async-start | bytes 1376256 | tf_op jit(solution)/shard_map/all_to_all | solution.py:1140
  552.1 20.6 %collective-permute-start.67 = (bf16[448,256]{1,0:T(8,128)(2,1)S(1)}, bf16[448,256]{1,0:T(8,128)(2,1)S(1)}, u32[]{:S(2)}, u32[]{:S(2)}) collective-permute-start(bf16[448,256]{1,0:T(8,128)(2,1)S(1)} %get-tuple-element.136), channel_id=1, source_target_pairs={{0,0},{1,4},{2,8},{3,12},{4,16},{5,20},{6,24},{7,28},{8,1},{9,5},{... | collective-permute-start | bytes 688136 | tf_op jit(solution)/shard_map/ppermute | solution.py:1145
  (109 other events, 988.2 us)
Sparse Core Ops, SparseCore 0:
  10.2 48.1 all-gather.3
  62.1 70.7 all-gather.5
  134.4 88.4 all-gather.7
  335.8 122.6 reduce-scatter.2
  465.1 68.9 reduce-scatter.4

commit v4 on v3

--- a/solution.py
+++ b/solution.py
@@ -90,6 +90,10 @@
 
 def neighbours(own):
     return swap(own, "x"), swap(own, "y")
+
+
+def across(own):
+    return lax.ppermute(own, ("y", "x"), [(i, i ^ 3) for i in range(4)])
 
 
 def join_kernel(first_ref, second_ref, *refs):
@@ -1051,9 +1055,10 @@
     opened = heads[:2, 0, extra_column(2, share)].astype(jnp.int32)
     opened = jnp.where(me_core == 0, opened, opened[::-1])
     info = jnp.concatenate([jnp.stack([me_block, me_core]), opened, me_z[None]]).astype(jnp.int32)
-    from_x, from_y = neighbours(held(own, heads))
-    far = join(*diagonal(from_x, from_y))
-    streams = both_cores([own, from_x, from_y, far])
+    ready = held(own, heads)
+    from_x, from_y = neighbours(ready)
+    streams = both_cores([own, from_x, from_y, across(ready)])
+    top_ready = held(top, from_x, from_y)
     attn_weight = attn_sheet(heads, out_weight, down, from_x, from_y)
     attn_weight = lax.all_gather(attn_weight, "z", axis=0, tiled=True)
     stream = jnp.concatenate(streams, axis=0)
@@ -1061,12 +1066,9 @@
     sheet = unit_sheet(gate_weight, up_weight, layers, part, units, heads)
     sheet = lax.all_to_all(sheet, PLANE, 0, 0, tiled=True).reshape(8 * share, 2 * units)
     gate_up = lax.all_gather(sheet, "z", axis=0, tiled=True)
-    from_x, from_y = neighbours(held(top, streams[6]))
-    first, second = halves(from_x, from_y)
-    tops = [top, from_x, from_y]
-    far_top = swap(first, "x"), swap(second, "y")
-
-    hidden1, qkv, gains = enter(stream, factor, attn_weight, rows, share, first)
+    tops = both_cores([top, *neighbours(top_ready), across(top_ready)])
+
+    hidden1, qkv, gains = enter(stream, factor, attn_weight, rows, share, *tops[2::2])
     gain_attn, gain_ffn = gains[0:1], gains[1:2]
     qkv = qkv.reshape(8, rows, 6 * HP)
     last = 2 * (3 ^ me_block)
@@ -1078,13 +1080,12 @@
     flat, kept = attend(qkv, halo, info)
     full_out = both_cores([own_out, from_x, from_y, join(*far, flat)])
     full_out = out_sheet(full_out, info, layers)
-    tops = both_cores(tops + [join(*far_top, flat)])
     rim = lax.dynamic_slice(
         hidden1.reshape(8, rows, width), (last, rows - WINDOW, 0), (2, WINDOW, width)
     )
     rim = lax.ppermute(rim, "z", [(i, i + 1) for i in range(layers - 1)])
     mixed = lax.all_to_all(flat, PLANE, 0, 0, tiled=True)
-    middle, hidden2 = project(mixed, full_out, own, gain_ffn, tops[6])
+    middle, hidden2 = project(mixed, full_out, own, gain_ffn)
 
     from_x, from_y = neighbours(hidden2)
     far = diagonal(from_x, from_y)

time: 591 us -> 576 us (0.975)
  waiting for transfers between devices: 193 us -> 184 us
  local copies, waits for them, and re-layouts: 65.9 us -> 59.3 us
    ppermute x64 -> x60, waiting for transfers between devices: 113 us -> 77.2 us  [swap(): return lax.ppermute(block, axis, SWAP)]
    all_to_all x1, waiting for transfers between devices: 7.39 us -> 16.8 us  [body(): lax.all_to_all(sheet, PLANE, 0, 0, tiled=True).reshape(8 * share, 2 * units)]
    all_gather x1, waiting for transfers between devices: 9.9 us -> 18.8 us  [body(): attn_weight = lax.all_gather(attn_weight, 'z', axis=0, tiled=True)]
    unnamed x162 -> x146, local copies, waits for them, and re-layouts: 51.6 us -> 45 us
    ppermute x64 -> x60, starting transfers between devices: 37.1 us -> 36.7 us  [swap(): return lax.ppermute(block, axis, SWAP)]
  transfers between devices with their start and end apart: 78 -> 76, of which waited for: 27 -> 25; matrix products, arithmetic and copies ran while one was open for 9% -> 9% of each run, Pallas kernels for 31% -> 31%
where the time goes in v4:
time: 576 us; the launch traced here: 568 us
  Pallas kernels  191 us (33%)
  waiting for transfers between devices  184 us (32%)
  starting transfers between devices  75 us (13%)
  local copies, waits for them, and re-layouts  59.3 us (10%)
  other arithmetic  28.8 us (5%)
  between operations  15.4 us (3%)
  blocking collectives  14.1 us (2%)
    ppermute x60, waiting for transfers between devices, swap(): return lax.ppermute(block, axis, SWAP)  77.2 us
    pallas_call x2, Pallas kernels, ffn(): pl.pallas_call(functools.partial(ffn_kernel, count, len(carried) + len(ot...  45.8 us
    unnamed x146, local copies, waits for them, and re-layouts  45 us
    ppermute x60, starting transfers between devices, swap(): return lax.ppermute(block, axis, SWAP)  36.7 us
    pallas_call x2, Pallas kernels, split(): pl.pallas_call(functools.partial(split_kernel, order, dims), grid=(len(or...  25.3 us
    all_to_all x1, waiting for transfers between devices, body(): gate_up_sum = lax.all_to_all(gate_up_sum, PLANE, 0, 0, tiled=True)  19.1 us
    all_gather x1, waiting for transfers between devices, body(): attn_weight = lax.all_gather(attn_weight, 'z', axis=0, tiled=True)  18.8 us
    ppermute x1, waiting for transfers between devices, body(): output_grad = out_owner(lax.ppermute(out_sum, ALL, route), share, width)  17.2 us
  transfers between devices with their start and end apart: 76, of which 25 were waited for; matrix products, arithmetic and copies ran while one was open for 9% of the time, Pallas kernels for 31%

profile of v4, /device:TPU:26, one launch (start us, length us, event | category | flops | bytes accessed | tf_op | source)
XLA Modules:
  0.0 567.6 jit_solution(2971596076368347532)
XLA Ops:
  14.0 14.1 %all_to_all.30.refs_0_.heads_ref = bf16[8,56,768]{2,1,0:T(8,128)(2,1)S(1)} all-to-all(bf16[8,56,768]{2,1,0:T(8,128)(2,1)S(1)} %shard_map.203), channel_id=1, replica_groups=mesh['z'=4,'y'=2,'x'=2,'c'=2] {'y','x','c'}, dimensions={0} | all-to-all | bytes 1376256 | tf_op jit(solution)/shard_map/all_to_all | solution.py:1054
  30.2 20.3 %collective-permute-done.1.refs_1_.refs_0_ = bf16[256,1792]{1,0:T(8,128)(2,1)S(1)} collective-permute-done((bf16[256,1792]{1,0:T(8,128)(2,1)S(1)}, bf16[256,1792]{1,0:T(8,128)(2,1)S(1)}, u32[]{:S(2)}, u32[]{:S(2)}) %collective-permute-start.1) | collective-permute-done | bytes 917536 | tf_op jit(solution)/shard_map/ppermute | solution.py:34
  51.4 6.9 %all-gather.4.cloned.1.call-done.refs_0_.refs_13_.refs_5_.right_ref = bf16[640,1792]{1,0:T(8,128)(2,1)} async-done(((bf16[160,1792]{1,0:T(8,128)(2,1)}), bf16[640,1792]{1,0:T(8,128)(2,1)}) %all-gather.4.cloned.1.call-update) | async-done | bytes 2293776 | tf_op jit(solution)/shard_map/all_gather | solution.py:1053
  67.3 5.6 all-to-all-start.2
  82.1 16.8 %all-to-all-done.2 = bf16[8,56,1280]{2,1,0:T(8,128)(2,1)} async-done(((bf16[8,56,1280]{2,1,0:T(8,128)(2,1)}), bf16[8,56,1280]{2,1,0:T(8,128)(2,1)}, u32[]{:S(2)}, u32[]{:S(2)}) %all-to-all-start.2) | async-done | bytes 1146912 | tf_op jit(solution)/shard_map/all_to_all | solution.py:1067
  100.4 2.3 constant_dynamic-update-slice_fusion.4
  103.7 2.2 constant_dynamic-update-slice_fusion.2
  105.9 2.2 constant_dynamic-update-slice_fusion.1
  109.1 4.6 multiply_reduce_fusion
  114.1 18.8 %all-gather.6.cloned.1.call-done.weight_ref.right_ref = bf16[1792,1024]{1,0:T(8,128)(2,1)} async-done(((bf16[448,1024]{1,0:T(8,128)(2,1)}), bf16[1792,1024]{1,0:T(8,128)(2,1)}) %all-gather.6.cloned.1.call-update) | async-done | bytes 3670032 | tf_op jit(solution)/shard_map/all_gather | solution.py:1063
  139.8 11.8 %shard_map.207 = (bf16[2048,1792]{1,0:T(8,128)(2,1)}, bf16[2048,768]{1,0:T(8,128)(2,1)}, f32[8,1792]{1,0:T(8,128)S(1)}) custom-call(bf16[2048,1792]{1,0:T(8,128)(2,1)} %constant_dynamic-update-slice_fusion.stream_ref, f32[2048,1]{1,0:T(8,128)S(1)} %copy.31.factor_ref, bf16[1792,1024]{1,0:T(8,128)(2,1)S(1)} %copy-done.12, ...), custom_call_target="tpu_custom_call" | custom-call | flops 13200000000 | bytes 42000000 | tf_op jit(solution)/shard_map/pallas_call | solution.py:404
  153.9 12.4 %collective-permute-done.10.halo_ref.refs_0_ = bf16[2,64,512]{2,1,0:T(8,128)(2,1)S(1)} collective-permute-done((bf16[2,64,512]{2,1,0:T(8,128)(2,1)S(1)}, bf16[2,64,512]{2,1,0:T(8,128)(2,1)S(1)}, u32[]{:S(2)}, u32[]{:S(2)}) %collective-permute-start.10) | collective-permute-done | bytes 131104 | tf_op jit(solution)/shard_map/ppermute | solution.py:1076
  170.3 6.2 %shard_map.208 = (bf16[8,256,256]{2,1,0:T(8,128)(2,1)}, bf16[8,256,256]{2,1,0:T(8,128)(2,1)}) custom-call(s32[5]{0:T(128)S(1)} %pad_add_fusion.info_ref, bf16[8,256,768]{2,1,0:T(8,128)(2,1)S(1)} %bitcast.41, bf16[8,256,768]{2,1,0:T(8,128)(2,1)S(1)} %bitcast.42, bf16[2,64,512]{2,1,0:T(8,128)(2,1)S(1)} %collective-permute-done.10.halo_ref.refs_0_), custom_call_target="tpu_custom_call" | custom-call | flops 8800000000 | bytes 28000000 | tf_op jit(solution)/shard_map/pallas_call | solution.py:918
  177.1 3.2 collective-permute-done.16.first_ref
  182.0 5.0 all-to-all-start.1
  187.3 8.0 %shard_map.211 = bf16[4,8,64,1792]{3,2,1,0:T(8,128)(2,1)} custom-call(s32[5]{0:T(128)S(1)} %pad_add_fusion.info_ref, bf16[1792,256]{1,0:T(8,128)(2,1)S(1)} %slice.117.refs_0_, bf16[1792,256]{1,0:T(8,128)(2,1)} %collective-permute-done.11.refs_1_, bf16[1792,256]{1,0:T(8,128)(2,1)} %collective-permute-done.12.x_ref.refs_2_, ...), custom_call_target="tpu_custom_call" | custom-call | flops 6600000000 | bytes 21000000 | tf_op jit(solution)/shard_map/pallas_call | solution.py:276
  195.2 5.7 all-to-all-done.1.mixed_ref
  200.9 3.1 copy-done.38
  204.0 4.0 shard_map.212
  210.7 19.8 %collective-permute-done.19.x_ref.refs_2_ = bf16[256,1792]{1,0:T(8,128)(2,1)S(1)} collective-permute-done((bf16[256,1792]{1,0:T(8,128)(2,1)S(1)}, bf16[256,1792]{1,0:T(8,128)(2,1)S(1)}, u32[]{:S(2)}, u32[]{:S(2)}) %collective-permute-start.19) | collective-permute-done | bytes 917536 | tf_op jit(solution)/shard_map/ppermute | solution.py:34
  235.0 30.1 %shard_map.215 = (bf16[2048,640]{1,0:T(8,128)(2,1)}, bf16[2048,1280]{1,0:T(8,128)(2,1)}, bf16[2048,1792]{1,0:T(8,128)(2,1)}, bf16[2048,1792]{1,0:T(8,128)(2,1)},...) custom-call(bf16[256,1792]{1,0:T(8,128)(2,1)} %copy-done.21, ...), custom_call_target="tpu_custom_call" | custom-call | flops 28600000512 | bytes 91000000 | tf_op jit(solution)/shard_map/pallas_call | solution.py:570
  272.5 15.7 %shard_map.217 = (bf16[2048,640]{1,0:T(8,128)(2,1)}, bf16[2048,1280]{1,0:T(8,128)(2,1)}, bf16[2048,1792]{1,0:T(8,128)(2,1)}, bf16[2048,1792]{1,0:T(8,128)(2,1)},...) custom-call(bf16[256,1792]{1,0:T(8,128)(2,1)} %copy-done.24, ...), custom_call_target="tpu_custom_call", output_to_operand_aliasing={{0}: (6, {}), {1}: (7, {}), {2}: (8, {}), {3}: (9, {})} | custom-call | flops 11000000512 | bytes 35000000 | tf_op jit(solution)/shard_map/pallas_call | solution.py:570
  295.5 15.4 %shard_map.219.refs_0_ = bf16[4,3360,256]{2,1,0:T(8,128)(2,1)} custom-call(bf16[2048,1792]{1,0:T(8,128)(2,1)} %get-tuple-element.86.hidden_ref, bf16[2048,1280]{1,0:T(8,128)(2,1)} %get-tuple-element.87.grads_ref, bf16[256,1792]{1,0:T(8,128)(2,1)} %copy-done.10, bf16[2,64,1792]{2,1,0:T(8,128)(2,1)} %collective-permute-done.32.refs_1_), custom_call_target="tpu_custom_call" | custom-call | flops 15399999488 | bytes 49000000 | tf_op jit(solution)/shard_map/pallas_call | solution.py:656
  313.1 10.5 %shard_map.220.refs_0_ = bf16[4,3360,256]{2,1,0:T(8,128)(2,1)} custom-call(bf16[2048,640]{1,0:T(8,128)(2,1)} %get-tuple-element.84.inner_ref.left_ref, bf16[2048,1792]{1,0:T(8,128)(2,1)} %get-tuple-element.85.top_ref, bf16[4,3360,256]{2,1,0:T(8,128)(2,1)} %shard_map.219.refs_0_, ...), custom_call_target="tpu_custom_call", output_to_operand_aliasing={{}: (2, {})} | custom-call | flops 11000000512 | bytes 35000000 | tf_op jit(solution)/shard_map/pallas_call | solution.py:677
  324.8 2.5 collective-permute-done.40
  330.4 12.9 %shard_map.221 = (bf16[256,1792]{1,0:T(8,128)(2,1)}, bf16[256,1792]{1,0:T(8,128)(2,1)}, bf16[256,1792]{1,0:T(8,128)(2,1)}, bf16[256,1792]{1,0:T(8,128)(2,1)}, bf...) custom-call(bf16[2048,640]{1,0:T(8,128)(2,1)} %get-tuple-element.84., ...), custom_call_target="tpu_custom_call" | custom-call | flops 15399999488 | bytes 49000000 | tf_op jit(solution)/shard_map/pallas_call | solution.py:615
  343.4 7.7 %collective-permute-done.41.x_ref = bf16[256,1792]{1,0:T(8,128)(2,1)S(1)} collective-permute-done((bf16[256,1792]{1,0:T(8,128)(2,1)S(1)}, bf16[256,1792]{1,0:T(8,128)(2,1)S(1)}, u32[]{:S(2)}, u32[]{:S(2)}) %collective-permute-start.41) | collective-permute-done | bytes 917536 | tf_op jit(solution)/shard_map/ppermute | solution.py:34
  353.4 11.1 %shard_map.222 = (bf16[8,256,256]{2,1,0:T(8,128)(2,1)}, f32[256,1792]{1,0:T(8,128)}, bf16[256,1792]{1,0:T(8,128)(2,1)S(1)}) custom-call(f32[256,1792]{1,0:T(8,128)} %convert_add_fusion.4.here_ref, bf16[256,1792]{1,0:T(8,128)(2,1)S(1)} %collective-permute-done.41.x_ref, bf16[256,1792]{1,0:T(8,128)(2,1)S(1)} %collective-permute-done.42.y_ref, ...), custom_call_target="tpu_custom_call" | custom-call | flops 13200000000 | bytes 42000000 | tf_op jit(solution)/shard_map/pallas_call | solution.py:482
  364.5 4.4 all-to-all-start.3
  371.6 2.8 convert_add_fusion.3
  374.5 8.4 %all-to-all-done.3.top_ref = bf16[8,256,256]{2,1,0:T(8,128)(2,1)S(1)} async-done(((bf16[8,256,256]{2,1,0:T(8,128)(2,1)}), bf16[8,256,256]{2,1,0:T(8,128)(2,1)S(1)}, u32[]{:S(2)}, u32[]{:S(2)}) %all-to-all-start.3) | async-done | bytes 1048608 | tf_op jit(solution)/shard_map/all_to_all | solution.py:1109
  384.8 8.6 %shard_map.223 = (bf16[8,256,768]{2,1,0:T(8,128)(2,1)S(1)}, f32[2,64,512]{2,1,0:T(8,128)S(1)}, bf16[2,64,512]{2,1,0:T(8,128)(2,1)S(1)}) custom-call(s32[5]{0:T(128)S(1)} %pad_add_fusion.info_ref, bf16[8,256,768]{2,1,0:T(8,128)(2,1)S(1)} %bitcast.43, bf16[8,256,768]{2,1,0:T(8,128)(2,1)S(1)} %bitcast.44, ...), custom_call_target="tpu_custom_call" | custom-call | flops 18699999232 | bytes 59500000 | tf_op jit(solution)/shard_map/pallas_call | solution.py:1011
  395.7 11.1 %shard_map.225.refs_0_.refs_9_ = bf16[4,1792,256]{2,1,0:T(8,128)(2,1)} custom-call(bf16[2048,1792]{1,0:T(8,128)(2,1)} %get-tuple-element.90.hidden_ref, bf16[2048,768]{1,0:T(8,128)(2,1)} %bitcast.32, bf16[128,1792]{1,0:T(8,128)(2,1)} %bitcast.14.rim_ref, bf16[128,512]{1,0:T(8,128)(2,1)} %bitcast.46), custom_call_target="tpu_custom_call" | custom-call | flops 12099999744 | bytes 38500000 | tf_op jit(solution)/shard_map/pallas_call | solution.py:767
  406.8 4.5 collective-permute-start.48
  416.0 2.3 shard_map.227
  420.7 2.7 slice.169
  425.4 2.5 shard_map.226
  427.9 8.3 %collective-permute-done.54.first_ref = bf16[128,1792]{1,0:T(8,128)(2,1)S(1)} collective-permute-done((bf16[128,1792]{1,0:T(8,128)(2,1)}, bf16[128,1792]{1,0:T(8,128)(2,1)S(1)}, u32[]{:S(2)}, u32[]{:S(2)}) %collective-permute-start.54) | collective-permute-done | bytes 458784 | tf_op jit(solution)/shard_map/ppermute | solution.py:34
  442.8 6.1 %shard_map.229.refs_0_ = bf16[4,1792,256]{2,1,0:T(8,128)(2,1)S(1)} custom-call(bf16[256,1792]{1,0:T(8,128)(2,1)S(1)} %get-tuple-element.109.refs_0_, bf16[256,1792]{1,0:T(8,128)(2,1)S(1)} %collective-permute-done.49.refs_1_, bf16[256,1792]{1,0:T(8,128)(2,1)} %collective-permute-done.50.x_ref.refs_2_, ...), custom_call_target="tpu_custom_call", output_to_operand_aliasing={{}: (9, {})} | custom-call | flops 6600000000 | bytes 21000000 | tf_op jit(solution)/shard_map/pallas_call | solution.py:790
  450.8 12.4 %shard_map.230 = (bf16[256,1792]{1,0:T(8,128)(2,1)}, bf16[256,1792]{1,0:T(8,128)(2,1)}, bf16[256,1792]{1,0:T(8,128)(2,1)}, bf16[256,1792]{1,0:T(8,128)(2,1)}, bf...) custom-call(bf16[2048,768]{1,0:T(8,128)(2,1)} %bitcast.33, ...), custom_call_target="tpu_custom_call" | custom-call | flops 15399999488 | bytes 49000000 | tf_op jit(solution)/shard_map/pallas_call | solution.py:615
  473.2 6.8 %collective-permute-done.60 = bf16[128,1792]{1,0:T(8,128)(2,1)S(1)} collective-permute-done((bf16[128,1792]{1,0:T(8,128)(2,1)S(1)}, bf16[128,1792]{1,0:T(8,128)(2,1)S(1)}, u32[]{:S(2)}, u32[]{:S(2)}) %collective-permute-start.60) | collective-permute-done | bytes 458784 | tf_op jit(solution)/shard_map/ppermute | solution.py:34
  489.8 5.4 all-to-all-start.4
  495.3 3.5 add_convert_fusion.refs_1_
  500.3 19.1 %all-to-all-done.4.sheet_ref = bf16[8,5,56,256]{3,2,1,0:T(8,128)(2,1)S(1)} async-done(((bf16[8,5,56,256]{3,2,1,0:T(8,128)(2,1)}), bf16[8,5,56,256]{3,2,1,0:T(8,128)(2,1)S(1)}, u32[]{:S(2)}, u32[]{:S(2)}) %all-to-all-start.4) | async-done | bytes 1146912 | tf_op jit(solution)/shard_map/all_to_all | solution.py:1130
  520.5 2.9 shard_map.232
  524.7 4.0 shard_map.233.refs_0_
  532.3 5.3 all-to-all-start.5
  541.3 17.2 %collective-permute-done.65.piece_ref = bf16[448,256]{1,0:T(8,128)(2,1)S(1)} collective-permute-done((bf16[448,256]{1,0:T(8,128)(2,1)S(1)}, bf16[448,256]{1,0:T(8,128)(2,1)S(1)}, u32[]{:S(2)}, u32[]{:S(2)}) %collective-permute-start.65) | collective-permute-done | bytes 229408 | tf_op jit(solution)/shard_map/ppermute | solution.py:1146
  (342 shorter events, 135.2 us)
Async XLA Ops:
  7.2 51.2 %all-gather.4.cloned.1.call-start = ((), (), s32[]{:S(2)}) async-start(), calls=%async_computation.8 | async-start | bytes 2867200 | tf_op jit(solution)/shard_map/all_gather | solution.py:1053
  9.1 123.7 %all-gather.6.cloned.1.call-start = ((), (), s32[]{:S(2)}) async-start(), calls=%async_computation.9 | async-start | bytes 4587520 | tf_op jit(solution)/shard_map/all_gather | solution.py:1063
  28.2 22.3 %collective-permute-start.1 = (bf16[256,1792]{1,0:T(8,128)(2,1)S(1)}, bf16[256,1792]{1,0:T(8,128)(2,1)S(1)}, u32[]{:S(2)}, u32[]{:S(2)}) collective-permute-start(bf16[256,1792]{1,0:T(8,128)(2,1)S(1)} %shard_map.204), channel_id=1, source_target_pairs={{0,2},{2,0},{1,3},{3,1},{4,6},{6,4},{5,7},{7,5},{8,10},{10,8},{9,1... | collective-permute-start | bytes 2752520 | tf_op jit(solution)/shard_map/ppermute | solution.py:34
  29.7 21.8 %collective-permute-start.3 = (bf16[256,1792]{1,0:T(8,128)(2,1)S(1)}, bf16[256,1792]{1,0:T(8,128)(2,1)S(1)}, u32[]{:S(2)}, u32[]{:S(2)}) collective-permute-start(bf16[256,1792]{1,0:T(8,128)(2,1)S(1)} %shard_map.204), channel_id=1, source_target_pairs={{0,4},{4,0},{1,5},{5,1},{2,6},{6,2},{3,7},{7,3},{8,12},{12,8},{9,1... | collective-permute-start | bytes 2752520 | tf_op jit(solution)/shard_map/ppermute | solution.py:34
  62.1 36.8 %collective-permute-start.5 = (bf16[256,1792]{1,0:T(8,128)(2,1)}, bf16[256,1792]{1,0:T(8,128)(2,1)}, u32[]{:S(2)}, u32[]{:S(2)}) collective-permute-start(bf16[256,1792]{1,0:T(8,128)(2,1)} %copy-done.20), channel_id=1, source_target_pairs={{0,6},{2,4},{4,2},{6,0},{1,7},{3,5},{5,3},{7,1},{8,14},{10,12},{12... | collective-permute-start | bytes 2752520 | tf_op jit(solution)/shard_map/ppermute | solution.py:96
  67.3 31.6 %all-to-all-start.2 = ((bf16[8,56,1280]{2,1,0:T(8,128)(2,1)}), bf16[8,56,1280]{2,1,0:T(8,128)(2,1)}, u32[]{:S(2)}, u32[]{:S(2)}) async-start(bf16[8,56,1280]{2,1,0:T(8,128)(2,1)} %shard_map.214), calls=%async_computation.2 | async-start | bytes 2293760 | tf_op jit(solution)/shard_map/all_to_all | solution.py:1067
  72.9 162.1 %all-gather.8.cloned.1.call-start = ((), (), s32[]{:S(2)}) async-start(), calls=%async_computation.10 | async-start | bytes 5734400 | tf_op jit(solution)/shard_map/all_gather | solution.py:1068
  72.9 27.5 %collective-permute-start.2 = (bf16[256,1792]{1,0:T(8,128)(2,1)S(1)}, bf16[256,1792]{1,0:T(8,128)(2,1)}, u32[]{:S(2)}, u32[]{:S(2)}) collective-permute-start(bf16[256,1792]{1,0:T(8,128)(2,1)S(1)} %collective-permute-done.1.refs_1_.refs_0_), channel_id=1, source_target_pairs={{0,1},{1,0},{2,3},{3,2},{4,5},{5,4},{6,7},{7,6},{8,9},{9,8},{10,11... | collective-permute-start | bytes 2752520 | tf_op jit(solution)/shard_map/ppermute | solution.py:34
  76.5 27.2 %collective-permute-start.4 = (bf16[256,1792]{1,0:T(8,128)(2,1)S(1)}, bf16[256,1792]{1,0:T(8,128)(2,1)}, u32[]{:S(2)}, u32[]{:S(2)}) collective-permute-start(bf16[256,1792]{1,0:T(8,128)(2,1)S(1)} %collective-permute-done.3.refs_2_.refs_1_), channel_id=1, source_target_pairs={{0,1},{1,0},{2,3},{3,2},{4,5},{5,4},{6,7},{7,6},{8,9},{9,8},{10,11... | collective-permute-start | bytes 2752520 | tf_op jit(solution)/shard_map/ppermute | solution.py:34
  79.0 57.1 %collective-permute-start.7 = (bf16[256,1792]{1,0:T(8,128)(2,1)}, bf16[256,1792]{1,0:T(8,128)(2,1)}, u32[]{:S(2)}, u32[]{:S(2)}) collective-permute-start(bf16[256,1792]{1,0:T(8,128)(2,1)} %shard_map.206), channel_id=1, source_target_pairs={{0,2},{2,0},{1,3},{3,1},{4,6},{6,4},{5,7},{7,5},{8,10},{10,8},{9,1... | collective-permute-start | bytes 2752520 | tf_op jit(solution)/shard_map/ppermute | solution.py:34
  79.3 56.9 %collective-permute-start.8 = (bf16[256,1792]{1,0:T(8,128)(2,1)}, bf16[256,1792]{1,0:T(8,128)(2,1)}, u32[]{:S(2)}, u32[]{:S(2)}) collective-permute-start(bf16[256,1792]{1,0:T(8,128)(2,1)} %shard_map.206), channel_id=1, source_target_pairs={{0,4},{4,0},{1,5},{5,1},{2,6},{6,2},{3,7},{7,3},{8,12},{12,8},{9,1... | collective-permute-start | bytes 2752520 | tf_op jit(solution)/shard_map/ppermute | solution.py:34
  98.9 38.9 %collective-permute-start.9 = (bf16[256,1792]{1,0:T(8,128)(2,1)}, bf16[256,1792]{1,0:T(8,128)(2,1)}, u32[]{:S(2)}, u32[]{:S(2)}) collective-permute-start(bf16[256,1792]{1,0:T(8,128)(2,1)} %shard_map.206), channel_id=1, source_target_pairs={{0,6},{2,4},{4,2},{6,0},{1,7},{3,5},{5,3},{7,1},{8,14},{10,12},{12... | collective-permute-start | bytes 2752520 | tf_op jit(solution)/shard_map/ppermute | solution.py:96
  134.1 32.2 %collective-permute-start.12 = (bf16[1792,256]{1,0:T(8,128)(2,1)S(1)}, bf16[1792,256]{1,0:T(8,128)(2,1)}, u32[]{:S(2)}, u32[]{:S(2)}) collective-permute-start(bf16[1792,256]{1,0:T(8,128)(2,1)S(1)} %slice.117.refs_0_), channel_id=1, source_target_pairs={{0,2},{2,0},{1,3},{3,1},{4,6},{6,4},{5,7},{7,5},{8,10},{10,8},{9,1... | collective-permute-start | bytes 2752520 | tf_op jit(solution)/shard_map/ppermute | solution.py:34
  134.4 31.9 %collective-permute-start.14 = (bf16[1792,256]{1,0:T(8,128)(2,1)S(1)}, bf16[1792,256]{1,0:T(8,128)(2,1)}, u32[]{:S(2)}, u32[]{:S(2)}) collective-permute-start(bf16[1792,256]{1,0:T(8,128)(2,1)S(1)} %slice.117.refs_0_), channel_id=1, source_target_pairs={{0,4},{4,0},{1,5},{5,1},{2,6},{6,2},{3,7},{7,3},{8,12},{12,8},{9,1... | collective-permute-start | bytes 2752520 | tf_op jit(solution)/shard_map/ppermute | solution.py:34
  153.9 33.3 %collective-permute-start.11 = (bf16[1792,256]{1,0:T(8,128)(2,1)S(1)}, bf16[1792,256]{1,0:T(8,128)(2,1)}, u32[]{:S(2)}, u32[]{:S(2)}) collective-permute-start(bf16[1792,256]{1,0:T(8,128)(2,1)S(1)} %slice.117.refs_0_), channel_id=1, source_target_pairs={{0,1},{1,0},{2,3},{3,2},{4,5},{5,4},{6,7},{7,6},{8,9},{9,8},{10,11... | collective-permute-start | bytes 2752520 | tf_op jit(solution)/shard_map/ppermute | solution.py:34
  181.5 29.1 %collective-permute-start.26 = (bf16[256,1792]{1,0:T(8,128)(2,1)}, bf16[256,1792]{1,0:T(8,128)(2,1)}, u32[]{:S(2)}, u32[]{:S(2)}) collective-permute-start(bf16[256,1792]{1,0:T(8,128)(2,1)} %bitcast.7.source_ref.refs_6_.top_ref), channel_id=1, source_target_pairs={{0,1},{1,0},{2,3},{3,2},{4,5},{5,4},{6,7},{7,6},{8,9},{9,8},{10,11... | collective-permute-start | bytes 2752520 | tf_op jit(solution)/shard_map/ppermute | solution.py:34
  182.0 18.9 %all-to-all-start.1 = ((bf16[8,256,256]{2,1,0:T(8,128)(2,1)}), bf16[8,256,256]{2,1,0:T(8,128)(2,1)S(1)}, u32[]{:S(2)}, u32[]{:S(2)}) async-start(bf16[8,256,256]{2,1,0:T(8,128)(2,1)} %get-tuple-element.72.refs_0_), calls=%async_computation.1 | async-start | bytes 2097152 | tf_op jit(solution)/shard_map/all_to_all | solution.py:1087
  187.0 300.5 %reduce-scatter.3.cloned.1.call-start = ((), (), s32[]{:S(2)}) async-start(), calls=%async_computation.11 | async-start | bytes 8601600 | tf_op jit(solution)/shard_map/reduce_scatter | solution.py:1103
  208.0 22.5 %collective-permute-start.19 = (bf16[256,1792]{1,0:T(8,128)(2,1)S(1)}, bf16[256,1792]{1,0:T(8,128)(2,1)S(1)}, u32[]{:S(2)}, u32[]{:S(2)}) collective-permute-start(bf16[256,1792]{1,0:T(8,128)(2,1)S(1)} %get-tuple-element.77.refs_0_), channel_id=1, source_target_pairs={{0,2},{2,0},{1,3},{3,1},{4,6},{6,4},{5,7},{7,5},{8,10},{10,8},{9,1... | collective-permute-start | bytes 2752520 | tf_op jit(solution)/shard_map/ppermute | solution.py:34
  209.6 21.0 %collective-permute-start.20 = (bf16[256,1792]{1,0:T(8,128)(2,1)S(1)}, bf16[256,1792]{1,0:T(8,128)(2,1)S(1)}, u32[]{:S(2)}, u32[]{:S(2)}) collective-permute-start(bf16[256,1792]{1,0:T(8,128)(2,1)S(1)} %get-tuple-element.77.refs_0_), channel_id=1, source_target_pairs={{0,4},{4,0},{1,5},{5,1},{2,6},{6,2},{3,7},{7,3},{8,12},{12,8},{9,1... | collective-permute-start | bytes 2752520 | tf_op jit(solution)/shard_map/ppermute | solution.py:34
  210.1 21.8 %collective-permute-start.27 = (bf16[256,1792]{1,0:T(8,128)(2,1)}, bf16[256,1792]{1,0:T(8,128)(2,1)S(1)}, u32[]{:S(2)}, u32[]{:S(2)}) collective-permute-start(bf16[256,1792]{1,0:T(8,128)(2,1)} %collective-permute-done.7.refs_0_.refs_8_), channel_id=1, source_target_pairs={{0,1},{1,0},{2,3},{3,2},{4,5},{5,4},{6,7},{7,6},{8,9},{9,8},{10,11... | collective-permute-start | bytes 2752520 | tf_op jit(solution)/shard_map/ppermute | solution.py:34
  210.2 22.1 %collective-permute-start.28 = (bf16[256,1792]{1,0:T(8,128)(2,1)}, bf16[256,1792]{1,0:T(8,128)(2,1)S(1)}, u32[]{:S(2)}, u32[]{:S(2)}) collective-permute-start(bf16[256,1792]{1,0:T(8,128)(2,1)} %collective-permute-done.8.refs_1_.refs_10_), channel_id=1, source_target_pairs={{0,1},{1,0},{2,3},{3,2},{4,5},{5,4},{6,7},{7,6},{8,9},{9,8},{10,11... | collective-permute-start | bytes 2752520 | tf_op jit(solution)/shard_map/ppermute | solution.py:34
  210.7 23.1 %collective-permute-start.23 = (bf16[256,1792]{1,0:T(8,128)(2,1)S(1)}, bf16[256,1792]{1,0:T(8,128)(2,1)S(1)}, u32[]{:S(2)}, u32[]{:S(2)}) collective-permute-start(bf16[256,1792]{1,0:T(8,128)(2,1)S(1)} %get-tuple-element.77.refs_0_), channel_id=1, source_target_pairs={{0,1},{1,0},{2,3},{3,2},{4,5},{5,4},{6,7},{7,6},{8,9},{9,8},{10,11... | collective-permute-start | bytes 2752520 | tf_op jit(solution)/shard_map/ppermute | solution.py:34
  232.0 39.6 %collective-permute-start.30 = (bf16[256,1792]{1,0:T(8,128)(2,1)}, bf16[256,1792]{1,0:T(8,128)(2,1)}, u32[]{:S(2)}, u32[]{:S(2)}) collective-permute-start(bf16[256,1792]{1,0:T(8,128)(2,1)} %collective-permute-done.9.refs_2_), channel_id=1, source_target_pairs={{0,1},{1,0},{2,3},{3,2},{4,5},{5,4},{6,7},{7,6},{8,9},{9,8},{10,11... | collective-permute-start | bytes 2752520 | tf_op jit(solution)/shard_map/ppermute | solution.py:34
  232.2 32.8 %collective-permute-start.21 = (bf16[128,1792]{1,0:T(8,128)(2,1)}, bf16[128,1792]{1,0:T(8,128)(2,1)}, u32[]{:S(2)}, u32[]{:S(2)}) collective-permute-start(bf16[128,1792]{1,0:T(8,128)(2,1)} %get-tuple-element.78), channel_id=1, source_target_pairs={{0,2},{2,0},{1,3},{3,1},{4,6},{6,4},{5,7},{7,5},{8,10},{10,8},{9,1... | collective-permute-start | bytes 1376264 | tf_op jit(solution)/shard_map/ppermute | solution.py:34
  234.7 30.4 %collective-permute-start.22 = (bf16[128,1792]{1,0:T(8,128)(2,1)S(1)}, bf16[128,1792]{1,0:T(8,128)(2,1)S(1)}, u32[]{:S(2)}, u32[]{:S(2)}) collective-permute-start(bf16[128,1792]{1,0:T(8,128)(2,1)S(1)} %get-tuple-element.79), channel_id=1, source_target_pairs={{0,4},{4,0},{1,5},{5,1},{2,6},{6,2},{3,7},{7,3},{8,12},{12,8},{9,1... | collective-permute-start | bytes 1376264 | tf_op jit(solution)/shard_map/ppermute | solution.py:34
  269.4 26.1 %collective-permute-start.32 = (bf16[2,64,1792]{2,1,0:T(8,128)(2,1)S(1)}, bf16[2,64,1792]{2,1,0:T(8,128)(2,1)}, u32[]{:S(2)}, u32[]{:S(2)}) collective-permute-start(bf16[2,64,1792]{2,1,0:T(8,128)(2,1)S(1)} %constant_dynamic-slice_fusion), channel_id=1, source_target_pairs={{0,8},{8,16},{16,24},{1,9},{9,17},{17,25},{2,10},{10,18},{18,26},{... | collective-permute-start | bytes 1376264 | tf_op jit(solution)/shard_map/ppermute | solution.py:1086
  271.3 20.0 %collective-permute-start.35 = (bf16[256,1792]{1,0:T(8,128)(2,1)}, bf16[256,1792]{1,0:T(8,128)(2,1)}, u32[]{:S(2)}, u32[]{:S(2)}) collective-permute-start(bf16[256,1792]{1,0:T(8,128)(2,1)} %get-tuple-element.94), channel_id=1, source_target_pairs={{0,1},{1,0},{2,3},{3,2},{4,5},{5,4},{6,7},{7,6},{8,9},{9,8},{10,11... | collective-permute-start | bytes 2752520 | tf_op jit(solution)/shard_map/ppermute | solution.py:34
  328.7 22.4 %collective-permute-start.41 = (bf16[256,1792]{1,0:T(8,128)(2,1)S(1)}, bf16[256,1792]{1,0:T(8,128)(2,1)S(1)}, u32[]{:S(2)}, u32[]{:S(2)}) collective-permute-start(bf16[256,1792]{1,0:T(8,128)(2,1)S(1)} %copy-done.60), channel_id=1, source_target_pairs={{0,2},{2,0},{1,3},{3,1},{4,6},{6,4},{5,7},{7,5},{8,10},{10,8},{9,1... | collective-permute-start | bytes 2752520 | tf_op jit(solution)/shard_map/ppermute | solution.py:34
  330.1 22.1 %collective-permute-start.42 = (bf16[256,1792]{1,0:T(8,128)(2,1)S(1)}, bf16[256,1792]{1,0:T(8,128)(2,1)S(1)}, u32[]{:S(2)}, u32[]{:S(2)}) collective-permute-start(bf16[256,1792]{1,0:T(8,128)(2,1)S(1)} %copy-done.61), channel_id=1, source_target_pairs={{0,4},{4,0},{1,5},{5,1},{2,6},{6,2},{3,7},{7,3},{8,12},{12,8},{9,1... | collective-permute-start | bytes 2752520 | tf_op jit(solution)/shard_map/ppermute | solution.py:34
  343.3 26.6 %collective-permute-start.45 = (bf16[256,1792]{1,0:T(8,128)(2,1)}, bf16[256,1792]{1,0:T(8,128)(2,1)}, u32[]{:S(2)}, u32[]{:S(2)}) collective-permute-start(bf16[256,1792]{1,0:T(8,128)(2,1)} %get-tuple-element.106), channel_id=1, source_target_pairs={{0,1},{1,0},{2,3},{3,2},{4,5},{5,4},{6,7},{7,6},{8,9},{9,8},{10,11... | collective-permute-start | bytes 2752520 | tf_op jit(solution)/shard_map/ppermute | solution.py:34
  364.5 18.4 %all-to-all-start.3 = ((bf16[8,256,256]{2,1,0:T(8,128)(2,1)}), bf16[8,256,256]{2,1,0:T(8,128)(2,1)S(1)}, u32[]{:S(2)}, u32[]{:S(2)}) async-start(bf16[8,256,256]{2,1,0:T(8,128)(2,1)} %get-tuple-element.103), calls=%async_computation.3 | async-start | bytes 2097152 | tf_op jit(solution)/shard_map/all_to_all | solution.py:1109
  368.9 159.8 %reduce-scatter.5.cloned.1.call-start = ((), (), s32[]{:S(2)}) async-start(), calls=%async_computation.12 | async-start | bytes 4587520 | tf_op jit(solution)/shard_map/reduce_scatter | solution.py:1126
  368.9 37.9 %collective-permute-start.39 = (bf16[256,1792]{1,0:T(8,128)(2,1)}, bf16[256,1792]{1,0:T(8,128)(2,1)}, u32[]{:S(2)}, u32[]{:S(2)}) collective-permute-start(bf16[256,1792]{1,0:T(8,128)(2,1)} %get-tuple-element.100), channel_id=1, source_target_pairs={{0,1},{1,0},{2,3},{3,2},{4,5},{5,4},{6,7},{7,6},{8,9},{9,8},{10,11... | collective-permute-start | bytes 2752520 | tf_op jit(solution)/shard_map/ppermute | solution.py:34
  369.1 49.3 %collective-permute-start.38 = (bf16[256,1792]{1,0:T(8,128)(2,1)}, bf16[256,1792]{1,0:T(8,128)(2,1)}, u32[]{:S(2)}, u32[]{:S(2)}) collective-permute-start(bf16[256,1792]{1,0:T(8,128)(2,1)} %get-tuple-element.98), channel_id=1, source_target_pairs={{0,1},{1,0},{2,3},{3,2},{4,5},{5,4},{6,7},{7,6},{8,9},{9,8},{10,11... | collective-permute-start | bytes 2752520 | tf_op jit(solution)/shard_map/ppermute | solution.py:34
  369.4 73.0 %collective-permute-start.49 = (bf16[256,1792]{1,0:T(8,128)(2,1)S(1)}, bf16[256,1792]{1,0:T(8,128)(2,1)S(1)}, u32[]{:S(2)}, u32[]{:S(2)}) collective-permute-start(bf16[256,1792]{1,0:T(8,128)(2,1)S(1)} %get-tuple-element.109.refs_0_), channel_id=1, source_target_pairs={{0,1},{1,0},{2,3},{3,2},{4,5},{5,4},{6,7},{7,6},{8,9},{9,8},{10,11... | collective-permute-start | bytes 2752520 | tf_op jit(solution)/shard_map/ppermute | solution.py:34
  369.6 44.3 %collective-permute-start.50 = (bf16[256,1792]{1,0:T(8,128)(2,1)S(1)}, bf16[256,1792]{1,0:T(8,128)(2,1)}, u32[]{:S(2)}, u32[]{:S(2)}) collective-permute-start(bf16[256,1792]{1,0:T(8,128)(2,1)S(1)} %get-tuple-element.109.refs_0_), channel_id=1, source_target_pairs={{0,2},{2,0},{1,3},{3,1},{4,6},{6,4},{5,7},{7,5},{8,10},{10,8},{9,1... | collective-permute-start | bytes 2752520 | tf_op jit(solution)/shard_map/ppermute | solution.py:34
  369.9 46.1 %collective-permute-start.52 = (bf16[256,1792]{1,0:T(8,128)(2,1)S(1)}, bf16[256,1792]{1,0:T(8,128)(2,1)}, u32[]{:S(2)}, u32[]{:S(2)}) collective-permute-start(bf16[256,1792]{1,0:T(8,128)(2,1)S(1)} %get-tuple-element.109.refs_0_), channel_id=1, source_target_pairs={{0,4},{4,0},{1,5},{5,1},{2,6},{6,2},{3,7},{7,3},{8,12},{12,8},{9,1... | collective-permute-start | bytes 2752520 | tf_op jit(solution)/shard_map/ppermute | solution.py:34
  413.9 22.9 %collective-permute-start.46 = (bf16[128,1792]{1,0:T(8,128)(2,1)}, bf16[128,1792]{1,0:T(8,128)(2,1)}, u32[]{:S(2)}, u32[]{:S(2)}) collective-permute-start(bf16[128,1792]{1,0:T(8,128)(2,1)} %get-tuple-element.134), channel_id=1, source_target_pairs={{0,2},{2,0},{1,3},{3,1},{4,6},{6,4},{5,7},{7,5},{8,10},{10,8},{9,1... | collective-permute-start | bytes 1376264 | tf_op jit(solution)/shard_map/ppermute | solution.py:34
  439.9 23.9 %collective-permute-start.47 = (bf16[256,1792]{1,0:T(8,128)(2,1)}, bf16[256,1792]{1,0:T(8,128)(2,1)}, u32[]{:S(2)}, u32[]{:S(2)}) collective-permute-start(bf16[256,1792]{1,0:T(8,128)(2,1)} %pad_maximum_fusion.3.refs_12_), channel_id=1, source_target_pairs={{0,4},{4,0},{1,5},{5,1},{2,6},{6,2},{3,7},{7,3},{8,12},{12,8},{9,1... | collective-permute-start | bytes 2752520 | tf_op jit(solution)/shard_map/ppermute | solution.py:34
  442.5 22.4 %collective-permute-start.44 = (bf16[256,1792]{1,0:T(8,128)(2,1)}, bf16[256,1792]{1,0:T(8,128)(2,1)}, u32[]{:S(2)}, u32[]{:S(2)}) collective-permute-start(bf16[256,1792]{1,0:T(8,128)(2,1)} %pad_maximum_fusion.2.refs_11_), channel_id=1, source_target_pairs={{0,2},{2,0},{1,3},{3,1},{4,6},{6,4},{5,7},{7,5},{8,10},{10,8},{9,1... | collective-permute-start | bytes 2752520 | tf_op jit(solution)/shard_map/ppermute | solution.py:34
  463.8 31.5 %collective-permute-start.37 = (bf16[256,1792]{1,0:T(8,128)(2,1)}, bf16[256,1792]{1,0:T(8,128)(2,1)}, u32[]{:S(2)}, u32[]{:S(2)}) collective-permute-start(bf16[256,1792]{1,0:T(8,128)(2,1)} %get-tuple-element.96), channel_id=1, source_target_pairs={{0,1},{1,0},{2,3},{3,2},{4,5},{5,4},{6,7},{7,6},{8,9},{9,8},{10,11... | collective-permute-start | bytes 2752520 | tf_op jit(solution)/shard_map/ppermute | solution.py:34
  463.8 35.0 %collective-permute-start.57 = (bf16[256,1792]{1,0:T(8,128)(2,1)}, bf16[256,1792]{1,0:T(8,128)(2,1)}, u32[]{:S(2)}, u32[]{:S(2)}) collective-permute-start(bf16[256,1792]{1,0:T(8,128)(2,1)} %get-tuple-element.114), channel_id=1, source_target_pairs={{0,1},{1,0},{2,3},{3,2},{4,5},{5,4},{6,7},{7,6},{8,9},{9,8},{10,11... | collective-permute-start | bytes 2752520 | tf_op jit(solution)/shard_map/ppermute | solution.py:34
  481.1 42.3 %collective-permute-start.61 = (bf16[256,1792]{1,0:T(8,128)(2,1)}, bf16[256,1792]{1,0:T(8,128)(2,1)}, u32[]{:S(2)}, u32[]{:S(2)}) collective-permute-start(bf16[256,1792]{1,0:T(8,128)(2,1)} %pad_maximum_fusion.4), channel_id=1, source_target_pairs={{0,2},{2,0},{1,3},{3,1},{4,6},{6,4},{5,7},{7,5},{8,10},{10,8},{9,1... | collective-permute-start | bytes 2752520 | tf_op jit(solution)/shard_map/ppermute | solution.py:34
  485.9 37.5 %collective-permute-start.64 = (bf16[256,1792]{1,0:T(8,128)(2,1)}, bf16[256,1792]{1,0:T(8,128)(2,1)}, u32[]{:S(2)}, u32[]{:S(2)}) collective-permute-start(bf16[256,1792]{1,0:T(8,128)(2,1)} %pad_maximum_fusion.5), channel_id=1, source_target_pairs={{0,4},{4,0},{1,5},{5,1},{2,6},{6,2},{3,7},{7,3},{8,12},{12,8},{9,1... | collective-permute-start | bytes 2752520 | tf_op jit(solution)/shard_map/ppermute | solution.py:34
  489.8 29.6 %all-to-all-start.4 = ((bf16[8,5,56,256]{3,2,1,0:T(8,128)(2,1)}), bf16[8,5,56,256]{3,2,1,0:T(8,128)(2,1)S(1)}, u32[]{:S(2)}, u32[]{:S(2)}) async-start(bf16[8,5,56,256]{3,2,1,0:T(8,128)(2,1)} %bitcast.51), calls=%async_computation.5 | async-start | bytes 2293760 | tf_op jit(solution)/shard_map/all_to_all | solution.py:1130
  532.3 26.9 %all-to-all-start.5 = ((bf16[8,3,56,256]{3,2,1,0:T(8,128)(2,1)}), bf16[8,3,56,256]{3,2,1,0:T(8,128)(2,1)S(1)}, u32[]{:S(2)}, u32[]{:S(2)}) async-start(bf16[8,3,56,256]{3,2,1,0:T(8,128)(2,1)} %get-tuple-element.123), calls=%async_computation.7 | async-start | bytes 1376256 | tf_op jit(solution)/shard_map/all_to_all | solution.py:1141
  537.9 20.6 %collective-permute-start.65 = (bf16[448,256]{1,0:T(8,128)(2,1)S(1)}, bf16[448,256]{1,0:T(8,128)(2,1)S(1)}, u32[]{:S(2)}, u32[]{:S(2)}) collective-permute-start(bf16[448,256]{1,0:T(8,128)(2,1)S(1)} %get-tuple-element.128), channel_id=1, source_target_pairs={{0,0},{1,4},{2,8},{3,12},{4,16},{5,20},{6,24},{7,28},{8,1},{9,5},{... | collective-permute-start | bytes 688136 | tf_op jit(solution)/shard_map/ppermute | solution.py:1146
  (99 other events, 885.5 us)
Sparse Core Ops, SparseCore 0:
  10.2 48.1 all-gather.3
  62.1 70.7 all-gather.5
  134.4 88.4 all-gather.7
  323.7 122.7 reduce-scatter.2
  451.0 68.9 reduce-scatter.4

commit v5 on v4

--- a/solution.py
+++ b/solution.py
@@ -1087,12 +1087,10 @@
     mixed = lax.all_to_all(flat, PLANE, 0, 0, tiled=True)
     middle, hidden2 = project(mixed, full_out, own, gain_ffn)
 
-    from_x, from_y = neighbours(hidden2)
-    far = diagonal(from_x, from_y)
-    carried, near = ffn(
-        both_cores([hidden2, from_x, from_y]), tops[:6], gate_up, down, 0
-    )
-    far = join(*far, carried[0])
+    blocks = both_cores([hidden2, *neighbours(hidden2)])
+    far = across(hidden2)
+    carried, near = ffn(blocks, tops[:6], gate_up, down, 0)
+    far = held(far, carried[0])
     (inner, grads, hidden2, tops), far = ffn(
         both_cores([far]), tops[6:], gate_up, down, 3, carried
     )
@@ -1135,9 +1133,9 @@
     down_grad = down_grad[:part].reshape(part, width).astype(F32)
     parts = split(grad_qkv, attn_weight, NT, (3, 2, 1, 0), rows, [attn_part])
     terms, _, _ = plane_sum(parts, *out_terms[1:])
-    input_grad = leave(terms, own, grad_middle, gain_attn, gate_grad)
-
-    qkv_sum, out_sum = part_sheet(attn_sum, share, input_grad, layer_out)
+    input_grad = leave(terms, own, grad_middle, gain_attn)
+
+    qkv_sum, out_sum = part_sheet(attn_sum, share, input_grad, gate_grad, layer_out)
     qkv_sum = lax.all_to_all(qkv_sum, PLANE, 0, 0, tiled=True)
     query_grad, key_grad, value_grad, attn_gain_grad = head_owner(
         qkv_sum, (query_weight, key_weight, value_weight), own_gains[0:1]

time: 576 us -> 572 us (level)
    all_to_all x1, waiting for transfers between devices: 19.1 us -> 0.01 us  [body(): gate_up_sum = lax.all_to_all(gate_up_sum, PLANE, 0, 0, tiled=True)]
    ppermute x60 -> x58, waiting for transfers between devices: 77.2 us -> 95.1 us  [swap(): return lax.ppermute(block, axis, SWAP)]
    ppermute x60 -> x58, starting transfers between devices: 36.7 us -> 35 us  [swap(): return lax.ppermute(block, axis, SWAP)]
    unnamed x146 -> x140, local copies, waits for them, and re-layouts: 45 us -> 45.6 us
  transfers between devices with their start and end apart: 76 -> 75, of which waited for: 25 -> 28; matrix products, arithmetic and copies ran while one was open for 9% -> 9% of each run, Pallas kernels for 31% -> 31%
where the time goes in v5:
time: 572 us; the launch traced here: 563 us
  Pallas kernels  189 us (33%)
  waiting for transfers between devices  183 us (32%)
  starting transfers between devices  74.6 us (13%)
  local copies, waits for them, and re-layouts  60.1 us (11%)
  other arithmetic  27.4 us (5%)
  between operations  15.4 us (3%)
  blocking collectives  14.1 us (2%)
    ppermute x58, waiting for transfers between devices, swap(): return lax.ppermute(block, axis, SWAP)  95.1 us
    pallas_call x2, Pallas kernels, ffn(): pl.pallas_call(functools.partial(ffn_kernel, count, len(carried) + len(ot...  45.9 us
    unnamed x140, local copies, waits for them, and re-layouts  45.6 us
    ppermute x58, starting transfers between devices, swap(): return lax.ppermute(block, axis, SWAP)  35 us
    pallas_call x2, Pallas kernels, split(): pl.pallas_call(functools.partial(split_kernel, order, dims), grid=(len(or...  25.3 us
    all_gather x1, waiting for transfers between devices, body(): attn_weight = lax.all_gather(attn_weight, 'z', axis=0, tiled=True)  18.8 us
    ppermute x1, waiting for transfers between devices, body(): output_grad = out_owner(lax.ppermute(out_sum, ALL, route), share, width)  17.2 us
    all_to_all x1, waiting for transfers between devices, body(): lax.all_to_all(sheet, PLANE, 0, 0, tiled=True).reshape(8 * share, 2 * units)  16.7 us
  transfers between devices with their start and end apart: 75, of which 28 were waited for; matrix products, arithmetic and copies ran while one was open for 9% of the time, Pallas kernels for 31%

profile of v5, /device:TPU:26, one launch (start us, length us, event | category | flops | bytes accessed | tf_op | source)
XLA Modules:
  0.0 563.2 jit_solution(8693679484512308177)
XLA Ops:
  14.0 14.1 %all_to_all.30.refs_0_.heads_ref = bf16[8,56,768]{2,1,0:T(8,128)(2,1)S(1)} all-to-all(bf16[8,56,768]{2,1,0:T(8,128)(2,1)S(1)} %shard_map.203), channel_id=1, replica_groups=mesh['z'=4,'y'=2,'x'=2,'c'=2] {'y','x','c'}, dimensions={0} | all-to-all | bytes 1376256 | tf_op jit(solution)/shard_map/all_to_all | solution.py:1054
  30.2 20.3 %collective-permute-done.1.refs_1_.refs_0_ = bf16[256,1792]{1,0:T(8,128)(2,1)S(1)} collective-permute-done((bf16[256,1792]{1,0:T(8,128)(2,1)S(1)}, bf16[256,1792]{1,0:T(8,128)(2,1)S(1)}, u32[]{:S(2)}, u32[]{:S(2)}) %collective-permute-start.1) | collective-permute-done | bytes 917536 | tf_op jit(solution)/shard_map/ppermute | solution.py:34
  51.4 6.9 %all-gather.4.cloned.1.call-done.refs_0_.refs_13_.refs_5_.right_ref = bf16[640,1792]{1,0:T(8,128)(2,1)} async-done(((bf16[160,1792]{1,0:T(8,128)(2,1)}), bf16[640,1792]{1,0:T(8,128)(2,1)}) %all-gather.4.cloned.1.call-update) | async-done | bytes 2293776 | tf_op jit(solution)/shard_map/all_gather | solution.py:1053
  67.3 5.6 all-to-all-start.2
  82.1 16.7 %all-to-all-done.2 = bf16[8,56,1280]{2,1,0:T(8,128)(2,1)} async-done(((bf16[8,56,1280]{2,1,0:T(8,128)(2,1)}), bf16[8,56,1280]{2,1,0:T(8,128)(2,1)}, u32[]{:S(2)}, u32[]{:S(2)}) %all-to-all-start.2) | async-done | bytes 1146912 | tf_op jit(solution)/shard_map/all_to_all | solution.py:1067
  100.4 2.2 constant_dynamic-update-slice_fusion.4
  105.8 2.2 constant_dynamic-update-slice_fusion.1
  109.0 4.6 multiply_reduce_fusion
  114.0 18.8 %all-gather.6.cloned.1.call-done.weight_ref.right_ref = bf16[1792,1024]{1,0:T(8,128)(2,1)} async-done(((bf16[448,1024]{1,0:T(8,128)(2,1)}), bf16[1792,1024]{1,0:T(8,128)(2,1)}) %all-gather.6.cloned.1.call-update) | async-done | bytes 3670032 | tf_op jit(solution)/shard_map/all_gather | solution.py:1063
  139.8 11.8 %shard_map.207 = (bf16[2048,1792]{1,0:T(8,128)(2,1)}, bf16[2048,768]{1,0:T(8,128)(2,1)}, f32[8,1792]{1,0:T(8,128)S(1)}) custom-call(bf16[2048,1792]{1,0:T(8,128)(2,1)} %constant_dynamic-update-slice_fusion.stream_ref, f32[2048,1]{1,0:T(8,128)S(1)} %copy.31.factor_ref, bf16[1792,1024]{1,0:T(8,128)(2,1)S(1)} %copy-done.12, ...), custom_call_target="tpu_custom_call" | custom-call | flops 13200000000 | bytes 42000000 | tf_op jit(solution)/shard_map/pallas_call | solution.py:404
  153.9 12.4 %collective-permute-done.10.halo_ref.refs_0_ = bf16[2,64,512]{2,1,0:T(8,128)(2,1)S(1)} collective-permute-done((bf16[2,64,512]{2,1,0:T(8,128)(2,1)S(1)}, bf16[2,64,512]{2,1,0:T(8,128)(2,1)S(1)}, u32[]{:S(2)}, u32[]{:S(2)}) %collective-permute-start.10) | collective-permute-done | bytes 131104 | tf_op jit(solution)/shard_map/ppermute | solution.py:1076
  170.4 6.2 %shard_map.208 = (bf16[8,256,256]{2,1,0:T(8,128)(2,1)}, bf16[8,256,256]{2,1,0:T(8,128)(2,1)}) custom-call(s32[5]{0:T(128)S(1)} %pad_add_fusion.info_ref, bf16[8,256,768]{2,1,0:T(8,128)(2,1)S(1)} %bitcast.41, bf16[8,256,768]{2,1,0:T(8,128)(2,1)S(1)} %bitcast.42, bf16[2,64,512]{2,1,0:T(8,128)(2,1)S(1)} %collective-permute-done.10.halo_ref.refs_0_), custom_call_target="tpu_custom_call" | custom-call | flops 8800000000 | bytes 28000000 | tf_op jit(solution)/shard_map/pallas_call | solution.py:918
  177.1 3.2 collective-permute-done.16.first_ref
  182.0 5.0 all-to-all-start.1
  187.3 7.9 %shard_map.211 = bf16[4,8,64,1792]{3,2,1,0:T(8,128)(2,1)} custom-call(s32[5]{0:T(128)S(1)} %pad_add_fusion.info_ref, bf16[1792,256]{1,0:T(8,128)(2,1)S(1)} %slice.117.refs_0_, bf16[1792,256]{1,0:T(8,128)(2,1)} %collective-permute-done.11.refs_1_, bf16[1792,256]{1,0:T(8,128)(2,1)} %collective-permute-done.12.x_ref.refs_2_, ...), custom_call_target="tpu_custom_call" | custom-call | flops 6600000000 | bytes 21000000 | tf_op jit(solution)/shard_map/pallas_call | solution.py:276
  195.2 5.7 %all-to-all-done.1.mixed_ref = bf16[8,256,256]{2,1,0:T(8,128)(2,1)S(1)} async-done(((bf16[8,256,256]{2,1,0:T(8,128)(2,1)}), bf16[8,256,256]{2,1,0:T(8,128)(2,1)S(1)}, u32[]{:S(2)}, u32[]{:S(2)}) %all-to-all-start.1) | async-done | bytes 1048608 | tf_op jit(solution)/shard_map/all_to_all | solution.py:1087
  200.9 3.1 copy-done.36
  204.0 4.0 shard_map.212
  211.8 20.0 %collective-permute-done.21.refs_2_ = bf16[256,1792]{1,0:T(8,128)(2,1)} collective-permute-done((bf16[256,1792]{1,0:T(8,128)(2,1)S(1)}, bf16[256,1792]{1,0:T(8,128)(2,1)}, u32[]{:S(2)}, u32[]{:S(2)}) %collective-permute-start.21) | collective-permute-done | bytes 917536 | tf_op jit(solution)/shard_map/ppermute | solution.py:34
  234.6 2.6 collective-permute-done.24.refs_5_
  237.2 30.0 %shard_map.214 = (bf16[2048,640]{1,0:T(8,128)(2,1)}, bf16[2048,1280]{1,0:T(8,128)(2,1)}, bf16[2048,1792]{1,0:T(8,128)(2,1)}, bf16[2048,1792]{1,0:T(8,128)(2,1)},...) custom-call(bf16[256,1792]{1,0:T(8,128)(2,1)} %copy-done.21, ...), custom_call_target="tpu_custom_call" | custom-call | flops 28600000512 | bytes 91000000 | tf_op jit(solution)/shard_map/pallas_call | solution.py:570
  273.8 15.8 %shard_map.216 = (bf16[2048,640]{1,0:T(8,128)(2,1)}, bf16[2048,1280]{1,0:T(8,128)(2,1)}, bf16[2048,1792]{1,0:T(8,128)(2,1)}, bf16[2048,1792]{1,0:T(8,128)(2,1)},...) custom-call(bf16[256,1792]{1,0:T(8,128)(2,1)} %copy-done.22, ...), custom_call_target="tpu_custom_call", output_to_operand_aliasing={{0}: (6, {}), {1}: (7, {}), {2}: (8, {}), {3}: (9, {})} | custom-call | flops 11000000512 | bytes 35000000 | tf_op jit(solution)/shard_map/pallas_call | solution.py:570
  295.2 15.4 %shard_map.218.refs_0_ = bf16[4,3360,256]{2,1,0:T(8,128)(2,1)} custom-call(bf16[2048,1792]{1,0:T(8,128)(2,1)} %get-tuple-element.82.hidden_ref, bf16[2048,1280]{1,0:T(8,128)(2,1)} %get-tuple-element.83.grads_ref, bf16[256,1792]{1,0:T(8,128)(2,1)} %copy-done.10, bf16[2,64,1792]{2,1,0:T(8,128)(2,1)} %collective-permute-done.31.refs_1_), custom_call_target="tpu_custom_call" | custom-call | flops 15399999488 | bytes 49000000 | tf_op jit(solution)/shard_map/pallas_call | solution.py:656
  312.7 10.5 %shard_map.219.refs_0_ = bf16[4,3360,256]{2,1,0:T(8,128)(2,1)} custom-call(bf16[2048,640]{1,0:T(8,128)(2,1)} %get-tuple-element.80.inner_ref.left_ref, bf16[2048,1792]{1,0:T(8,128)(2,1)} %get-tuple-element.81.top_ref, bf16[4,3360,256]{2,1,0:T(8,128)(2,1)} %shard_map.218.refs_0_, ...), custom_call_target="tpu_custom_call", output_to_operand_aliasing={{}: (2, {})} | custom-call | flops 11000000512 | bytes 35000000 | tf_op jit(solution)/shard_map/pallas_call | solution.py:677
  324.7 2.2 collective-permute-done.39
  331.7 12.9 %shard_map.220 = (bf16[256,1792]{1,0:T(8,128)(2,1)}, bf16[256,1792]{1,0:T(8,128)(2,1)}, bf16[256,1792]{1,0:T(8,128)(2,1)}, bf16[256,1792]{1,0:T(8,128)(2,1)}, bf...) custom-call(bf16[2048,640]{1,0:T(8,128)(2,1)} %get-tuple-element.80., ...), custom_call_target="tpu_custom_call" | custom-call | flops 15399999488 | bytes 49000000 | tf_op jit(solution)/shard_map/pallas_call | solution.py:615
  344.6 6.3 %collective-permute-done.40.x_ref = bf16[256,1792]{1,0:T(8,128)(2,1)S(1)} collective-permute-done((bf16[256,1792]{1,0:T(8,128)(2,1)S(1)}, bf16[256,1792]{1,0:T(8,128)(2,1)S(1)}, u32[]{:S(2)}, u32[]{:S(2)}) %collective-permute-start.40) | collective-permute-done | bytes 917536 | tf_op jit(solution)/shard_map/ppermute | solution.py:34
  353.3 11.1 %shard_map.221 = (bf16[8,256,256]{2,1,0:T(8,128)(2,1)}, f32[256,1792]{1,0:T(8,128)}, bf16[256,1792]{1,0:T(8,128)(2,1)S(1)}) custom-call(f32[256,1792]{1,0:T(8,128)} %convert_add_fusion.4.here_ref, bf16[256,1792]{1,0:T(8,128)(2,1)S(1)} %collective-permute-done.40.x_ref, bf16[256,1792]{1,0:T(8,128)(2,1)S(1)} %collective-permute-done.41.y_ref, ...), custom_call_target="tpu_custom_call" | custom-call | flops 13200000000 | bytes 42000000 | tf_op jit(solution)/shard_map/pallas_call | solution.py:482
  364.4 4.4 all-to-all-start.3
  371.6 2.9 convert_add_fusion.3
  374.4 8.4 %all-to-all-done.3.top_ref = bf16[8,256,256]{2,1,0:T(8,128)(2,1)S(1)} async-done(((bf16[8,256,256]{2,1,0:T(8,128)(2,1)}), bf16[8,256,256]{2,1,0:T(8,128)(2,1)S(1)}, u32[]{:S(2)}, u32[]{:S(2)}) %all-to-all-start.3) | async-done | bytes 1048608 | tf_op jit(solution)/shard_map/all_to_all | solution.py:1107
  384.7 8.6 %shard_map.222 = (bf16[8,256,768]{2,1,0:T(8,128)(2,1)S(1)}, f32[2,64,512]{2,1,0:T(8,128)S(1)}, bf16[2,64,512]{2,1,0:T(8,128)(2,1)S(1)}) custom-call(s32[5]{0:T(128)S(1)} %pad_add_fusion.info_ref, bf16[8,256,768]{2,1,0:T(8,128)(2,1)S(1)} %bitcast.43, bf16[8,256,768]{2,1,0:T(8,128)(2,1)S(1)} %bitcast.44, ...), custom_call_target="tpu_custom_call" | custom-call | flops 18699999232 | bytes 59500000 | tf_op jit(solution)/shard_map/pallas_call | solution.py:1011
  395.6 11.1 %shard_map.224.refs_0_.refs_9_ = bf16[4,1792,256]{2,1,0:T(8,128)(2,1)} custom-call(bf16[2048,1792]{1,0:T(8,128)(2,1)} %get-tuple-element.86.hidden_ref, bf16[2048,768]{1,0:T(8,128)(2,1)} %bitcast.32, bf16[128,1792]{1,0:T(8,128)(2,1)} %bitcast.14.rim_ref, bf16[128,512]{1,0:T(8,128)(2,1)} %bitcast.46), custom_call_target="tpu_custom_call" | custom-call | flops 12099999744 | bytes 38500000 | tf_op jit(solution)/shard_map/pallas_call | solution.py:767
  406.8 4.2 collective-permute-start.47
  415.6 2.3 shard_map.226
  420.5 2.7 slice.169
  425.0 2.5 shard_map.225
  427.5 8.4 %collective-permute-done.53.first_ref = bf16[128,1792]{1,0:T(8,128)(2,1)S(1)} collective-permute-done((bf16[128,1792]{1,0:T(8,128)(2,1)}, bf16[128,1792]{1,0:T(8,128)(2,1)S(1)}, u32[]{:S(2)}, u32[]{:S(2)}) %collective-permute-start.53) | collective-permute-done | bytes 458784 | tf_op jit(solution)/shard_map/ppermute | solution.py:34
  442.5 6.1 %shard_map.228.refs_0_ = bf16[4,1792,256]{2,1,0:T(8,128)(2,1)S(1)} custom-call(bf16[256,1792]{1,0:T(8,128)(2,1)S(1)} %get-tuple-element.105.refs_0_, bf16[256,1792]{1,0:T(8,128)(2,1)S(1)} %collective-permute-done.48.refs_1_, bf16[256,1792]{1,0:T(8,128)(2,1)} %collective-permute-done.49.x_ref.refs_2_, ...), custom_call_target="tpu_custom_call", output_to_operand_aliasing={{}: (9, {})} | custom-call | flops 6600000000 | bytes 21000000 | tf_op jit(solution)/shard_map/pallas_call | solution.py:790
  450.6 12.5 %shard_map.229 = (bf16[256,1792]{1,0:T(8,128)(2,1)}, bf16[256,1792]{1,0:T(8,128)(2,1)}, bf16[256,1792]{1,0:T(8,128)(2,1)}, bf16[256,1792]{1,0:T(8,128)(2,1)}, bf...) custom-call(bf16[2048,768]{1,0:T(8,128)(2,1)} %bitcast.33, ...), custom_call_target="tpu_custom_call" | custom-call | flops 15399999488 | bytes 49000000 | tf_op jit(solution)/shard_map/pallas_call | solution.py:615
  473.0 6.8 %collective-permute-done.59 = bf16[128,1792]{1,0:T(8,128)(2,1)S(1)} collective-permute-done((bf16[128,1792]{1,0:T(8,128)(2,1)S(1)}, bf16[128,1792]{1,0:T(8,128)(2,1)S(1)}, u32[]{:S(2)}, u32[]{:S(2)}) %collective-permute-start.59) | collective-permute-done | bytes 458784 | tf_op jit(solution)/shard_map/ppermute | solution.py:34
  492.0 5.4 all-to-all-start.4
  499.3 5.1 collective-permute-done.60.x_ref
  504.4 10.9 %collective-permute-done.63.y_ref = bf16[256,1792]{1,0:T(8,128)(2,1)} collective-permute-done((bf16[256,1792]{1,0:T(8,128)(2,1)}, bf16[256,1792]{1,0:T(8,128)(2,1)}, u32[]{:S(2)}, u32[]{:S(2)}) %collective-permute-start.63) | collective-permute-done | bytes 917536 | tf_op jit(solution)/shard_map/ppermute | solution.py:34
  515.3 3.8 shard_map.231.refs_0_
  520.2 2.9 shard_map.232
  528.0 5.3 all-to-all-start.5
  537.0 17.2 %collective-permute-done.64.piece_ref = bf16[448,256]{1,0:T(8,128)(2,1)S(1)} collective-permute-done((bf16[448,256]{1,0:T(8,128)(2,1)S(1)}, bf16[448,256]{1,0:T(8,128)(2,1)S(1)}, u32[]{:S(2)}, u32[]{:S(2)}) %collective-permute-start.64) | collective-permute-done | bytes 229408 | tf_op jit(solution)/shard_map/ppermute | solution.py:1144
  (333 shorter events, 138.8 us)
Async XLA Ops:
  7.2 51.2 %all-gather.4.cloned.1.call-start = ((), (), s32[]{:S(2)}) async-start(), calls=%async_computation.8 | async-start | bytes 2867200 | tf_op jit(solution)/shard_map/all_gather | solution.py:1053
  9.1 123.7 %all-gather.6.cloned.1.call-start = ((), (), s32[]{:S(2)}) async-start(), calls=%async_computation.9 | async-start | bytes 4587520 | tf_op jit(solution)/shard_map/all_gather | solution.py:1063
  28.2 22.3 %collective-permute-start.1 = (bf16[256,1792]{1,0:T(8,128)(2,1)S(1)}, bf16[256,1792]{1,0:T(8,128)(2,1)S(1)}, u32[]{:S(2)}, u32[]{:S(2)}) collective-permute-start(bf16[256,1792]{1,0:T(8,128)(2,1)S(1)} %shard_map.204), channel_id=1, source_target_pairs={{0,2},{2,0},{1,3},{3,1},{4,6},{6,4},{5,7},{7,5},{8,10},{10,8},{9,1... | collective-permute-start | bytes 2752520 | tf_op jit(solution)/shard_map/ppermute | solution.py:34
  29.7 21.8 %collective-permute-start.3 = (bf16[256,1792]{1,0:T(8,128)(2,1)S(1)}, bf16[256,1792]{1,0:T(8,128)(2,1)S(1)}, u32[]{:S(2)}, u32[]{:S(2)}) collective-permute-start(bf16[256,1792]{1,0:T(8,128)(2,1)S(1)} %shard_map.204), channel_id=1, source_target_pairs={{0,4},{4,0},{1,5},{5,1},{2,6},{6,2},{3,7},{7,3},{8,12},{12,8},{9,1... | collective-permute-start | bytes 2752520 | tf_op jit(solution)/shard_map/ppermute | solution.py:34
  62.1 36.8 %collective-permute-start.5 = (bf16[256,1792]{1,0:T(8,128)(2,1)}, bf16[256,1792]{1,0:T(8,128)(2,1)}, u32[]{:S(2)}, u32[]{:S(2)}) collective-permute-start(bf16[256,1792]{1,0:T(8,128)(2,1)} %copy-done.20), channel_id=1, source_target_pairs={{0,6},{2,4},{4,2},{6,0},{1,7},{3,5},{5,3},{7,1},{8,14},{10,12},{12... | collective-permute-start | bytes 2752520 | tf_op jit(solution)/shard_map/ppermute | solution.py:96
  67.3 31.6 %all-to-all-start.2 = ((bf16[8,56,1280]{2,1,0:T(8,128)(2,1)}), bf16[8,56,1280]{2,1,0:T(8,128)(2,1)}, u32[]{:S(2)}, u32[]{:S(2)}) async-start(bf16[8,56,1280]{2,1,0:T(8,128)(2,1)} %shard_map.213), calls=%async_computation.2 | async-start | bytes 2293760 | tf_op jit(solution)/shard_map/all_to_all | solution.py:1067
  72.9 160.9 %all-gather.8.cloned.1.call-start = ((), (), s32[]{:S(2)}) async-start(), calls=%async_computation.10 | async-start | bytes 5734400 | tf_op jit(solution)/shard_map/all_gather | solution.py:1068
  72.9 27.5 %collective-permute-start.2 = (bf16[256,1792]{1,0:T(8,128)(2,1)S(1)}, bf16[256,1792]{1,0:T(8,128)(2,1)}, u32[]{:S(2)}, u32[]{:S(2)}) collective-permute-start(bf16[256,1792]{1,0:T(8,128)(2,1)S(1)} %collective-permute-done.1.refs_1_.refs_0_), channel_id=1, source_target_pairs={{0,1},{1,0},{2,3},{3,2},{4,5},{5,4},{6,7},{7,6},{8,9},{9,8},{10,11... | collective-permute-start | bytes 2752520 | tf_op jit(solution)/shard_map/ppermute | solution.py:34
  76.5 27.1 %collective-permute-start.4 = (bf16[256,1792]{1,0:T(8,128)(2,1)S(1)}, bf16[256,1792]{1,0:T(8,128)(2,1)}, u32[]{:S(2)}, u32[]{:S(2)}) collective-permute-start(bf16[256,1792]{1,0:T(8,128)(2,1)S(1)} %collective-permute-done.3.refs_2_.refs_1_), channel_id=1, source_target_pairs={{0,1},{1,0},{2,3},{3,2},{4,5},{5,4},{6,7},{7,6},{8,9},{9,8},{10,11... | collective-permute-start | bytes 2752520 | tf_op jit(solution)/shard_map/ppermute | solution.py:34
  79.1 57.1 %collective-permute-start.7 = (bf16[256,1792]{1,0:T(8,128)(2,1)}, bf16[256,1792]{1,0:T(8,128)(2,1)}, u32[]{:S(2)}, u32[]{:S(2)}) collective-permute-start(bf16[256,1792]{1,0:T(8,128)(2,1)} %shard_map.206), channel_id=1, source_target_pairs={{0,2},{2,0},{1,3},{3,1},{4,6},{6,4},{5,7},{7,5},{8,10},{10,8},{9,1... | collective-permute-start | bytes 2752520 | tf_op jit(solution)/shard_map/ppermute | solution.py:34
  79.3 56.9 %collective-permute-start.8 = (bf16[256,1792]{1,0:T(8,128)(2,1)}, bf16[256,1792]{1,0:T(8,128)(2,1)}, u32[]{:S(2)}, u32[]{:S(2)}) collective-permute-start(bf16[256,1792]{1,0:T(8,128)(2,1)} %shard_map.206), channel_id=1, source_target_pairs={{0,4},{4,0},{1,5},{5,1},{2,6},{6,2},{3,7},{7,3},{8,12},{12,8},{9,1... | collective-permute-start | bytes 2752520 | tf_op jit(solution)/shard_map/ppermute | solution.py:34
  98.9 38.9 %collective-permute-start.9 = (bf16[256,1792]{1,0:T(8,128)(2,1)}, bf16[256,1792]{1,0:T(8,128)(2,1)}, u32[]{:S(2)}, u32[]{:S(2)}) collective-permute-start(bf16[256,1792]{1,0:T(8,128)(2,1)} %shard_map.206), channel_id=1, source_target_pairs={{0,6},{2,4},{4,2},{6,0},{1,7},{3,5},{5,3},{7,1},{8,14},{10,12},{12... | collective-permute-start | bytes 2752520 | tf_op jit(solution)/shard_map/ppermute | solution.py:96
  134.1 32.2 %collective-permute-start.12 = (bf16[1792,256]{1,0:T(8,128)(2,1)S(1)}, bf16[1792,256]{1,0:T(8,128)(2,1)}, u32[]{:S(2)}, u32[]{:S(2)}) collective-permute-start(bf16[1792,256]{1,0:T(8,128)(2,1)S(1)} %slice.117.refs_0_), channel_id=1, source_target_pairs={{0,2},{2,0},{1,3},{3,1},{4,6},{6,4},{5,7},{7,5},{8,10},{10,8},{9,1... | collective-permute-start | bytes 2752520 | tf_op jit(solution)/shard_map/ppermute | solution.py:34
  134.4 31.9 %collective-permute-start.14 = (bf16[1792,256]{1,0:T(8,128)(2,1)S(1)}, bf16[1792,256]{1,0:T(8,128)(2,1)}, u32[]{:S(2)}, u32[]{:S(2)}) collective-permute-start(bf16[1792,256]{1,0:T(8,128)(2,1)S(1)} %slice.117.refs_0_), channel_id=1, source_target_pairs={{0,4},{4,0},{1,5},{5,1},{2,6},{6,2},{3,7},{7,3},{8,12},{12,8},{9,1... | collective-permute-start | bytes 2752520 | tf_op jit(solution)/shard_map/ppermute | solution.py:34
  153.9 33.3 %collective-permute-start.11 = (bf16[1792,256]{1,0:T(8,128)(2,1)S(1)}, bf16[1792,256]{1,0:T(8,128)(2,1)}, u32[]{:S(2)}, u32[]{:S(2)}) collective-permute-start(bf16[1792,256]{1,0:T(8,128)(2,1)S(1)} %slice.117.refs_0_), channel_id=1, source_target_pairs={{0,1},{1,0},{2,3},{3,2},{4,5},{5,4},{6,7},{7,6},{8,9},{9,8},{10,11... | collective-permute-start | bytes 2752520 | tf_op jit(solution)/shard_map/ppermute | solution.py:34
  181.5 30.3 %collective-permute-start.25 = (bf16[256,1792]{1,0:T(8,128)(2,1)}, bf16[256,1792]{1,0:T(8,128)(2,1)}, u32[]{:S(2)}, u32[]{:S(2)}) collective-permute-start(bf16[256,1792]{1,0:T(8,128)(2,1)} %bitcast.7.source_ref.refs_6_.top_ref), channel_id=1, source_target_pairs={{0,1},{1,0},{2,3},{3,2},{4,5},{5,4},{6,7},{7,6},{8,9},{9,8},{10,11... | collective-permute-start | bytes 2752520 | tf_op jit(solution)/shard_map/ppermute | solution.py:34
  182.0 18.9 %all-to-all-start.1 = ((bf16[8,256,256]{2,1,0:T(8,128)(2,1)}), bf16[8,256,256]{2,1,0:T(8,128)(2,1)S(1)}, u32[]{:S(2)}, u32[]{:S(2)}) async-start(bf16[8,256,256]{2,1,0:T(8,128)(2,1)} %get-tuple-element.70.refs_0_), calls=%async_computation.1 | async-start | bytes 2097152 | tf_op jit(solution)/shard_map/all_to_all | solution.py:1087
  187.0 302.3 %reduce-scatter.5.cloned.1.call-start = ((), (), s32[]{:S(2)}) async-start(), calls=%async_computation.12 | async-start | bytes 8601600 | tf_op jit(solution)/shard_map/reduce_scatter | solution.py:1101
  209.2 22.5 %collective-permute-start.21 = (bf16[256,1792]{1,0:T(8,128)(2,1)S(1)}, bf16[256,1792]{1,0:T(8,128)(2,1)}, u32[]{:S(2)}, u32[]{:S(2)}) collective-permute-start(bf16[256,1792]{1,0:T(8,128)(2,1)S(1)} %get-tuple-element.75.refs_0_), channel_id=1, source_target_pairs={{0,2},{2,0},{1,3},{3,1},{4,6},{6,4},{5,7},{7,5},{8,10},{10,8},{9,1... | collective-permute-start | bytes 2752520 | tf_op jit(solution)/shard_map/ppermute | solution.py:34
  210.8 21.0 %collective-permute-start.23 = (bf16[256,1792]{1,0:T(8,128)(2,1)S(1)}, bf16[256,1792]{1,0:T(8,128)(2,1)}, u32[]{:S(2)}, u32[]{:S(2)}) collective-permute-start(bf16[256,1792]{1,0:T(8,128)(2,1)S(1)} %get-tuple-element.75.refs_0_), channel_id=1, source_target_pairs={{0,4},{4,0},{1,5},{5,1},{2,6},{6,2},{3,7},{7,3},{8,12},{12,8},{9,1... | collective-permute-start | bytes 2752520 | tf_op jit(solution)/shard_map/ppermute | solution.py:34
  211.3 21.0 %collective-permute-start.26 = (bf16[256,1792]{1,0:T(8,128)(2,1)}, bf16[256,1792]{1,0:T(8,128)(2,1)}, u32[]{:S(2)}, u32[]{:S(2)}) collective-permute-start(bf16[256,1792]{1,0:T(8,128)(2,1)} %collective-permute-done.7.refs_0_.refs_8_), channel_id=1, source_target_pairs={{0,1},{1,0},{2,3},{3,2},{4,5},{5,4},{6,7},{7,6},{8,9},{9,8},{10,11... | collective-permute-start | bytes 2752520 | tf_op jit(solution)/shard_map/ppermute | solution.py:34
  211.3 21.1 %collective-permute-start.27 = (bf16[256,1792]{1,0:T(8,128)(2,1)}, bf16[256,1792]{1,0:T(8,128)(2,1)}, u32[]{:S(2)}, u32[]{:S(2)}) collective-permute-start(bf16[256,1792]{1,0:T(8,128)(2,1)} %collective-permute-done.8.refs_1_.refs_10_), channel_id=1, source_target_pairs={{0,1},{1,0},{2,3},{3,2},{4,5},{5,4},{6,7},{7,6},{8,9},{9,8},{10,11... | collective-permute-start | bytes 2752520 | tf_op jit(solution)/shard_map/ppermute | solution.py:34
  211.8 22.0 %collective-permute-start.20 = (bf16[256,1792]{1,0:T(8,128)(2,1)S(1)}, bf16[256,1792]{1,0:T(8,128)(2,1)}, u32[]{:S(2)}, u32[]{:S(2)}) collective-permute-start(bf16[256,1792]{1,0:T(8,128)(2,1)S(1)} %get-tuple-element.75.refs_0_), channel_id=1, source_target_pairs={{0,1},{1,0},{2,3},{3,2},{4,5},{5,4},{6,7},{7,6},{8,9},{9,8},{10,11... | collective-permute-start | bytes 2752520 | tf_op jit(solution)/shard_map/ppermute | solution.py:34
  232.3 40.3 %collective-permute-start.29 = (bf16[256,1792]{1,0:T(8,128)(2,1)}, bf16[256,1792]{1,0:T(8,128)(2,1)S(1)}, u32[]{:S(2)}, u32[]{:S(2)}) collective-permute-start(bf16[256,1792]{1,0:T(8,128)(2,1)} %collective-permute-done.9.refs_2_), channel_id=1, source_target_pairs={{0,1},{1,0},{2,3},{3,2},{4,5},{5,4},{6,7},{7,6},{8,9},{9,8},{10,11... | collective-permute-start | bytes 2752520 | tf_op jit(solution)/shard_map/ppermute | solution.py:34
  232.4 34.9 %collective-permute-start.19 = (bf16[256,1792]{1,0:T(8,128)(2,1)S(1)}, bf16[256,1792]{1,0:T(8,128)(2,1)S(1)}, u32[]{:S(2)}, u32[]{:S(2)}) collective-permute-start(bf16[256,1792]{1,0:T(8,128)(2,1)S(1)} %get-tuple-element.75.refs_0_), channel_id=1, source_target_pairs={{0,6},{2,4},{4,2},{6,0},{1,7},{3,5},{5,3},{7,1},{8,14},{10,12},{12... | collective-permute-start | bytes 2752520 | tf_op jit(solution)/shard_map/ppermute | solution.py:96
  270.5 24.6 %collective-permute-start.31 = (bf16[2,64,1792]{2,1,0:T(8,128)(2,1)S(1)}, bf16[2,64,1792]{2,1,0:T(8,128)(2,1)}, u32[]{:S(2)}, u32[]{:S(2)}) collective-permute-start(bf16[2,64,1792]{2,1,0:T(8,128)(2,1)S(1)} %constant_dynamic-slice_fusion), channel_id=1, source_target_pairs={{0,8},{8,16},{16,24},{1,9},{9,17},{17,25},{2,10},{10,18},{18,26},{... | collective-permute-start | bytes 1376264 | tf_op jit(solution)/shard_map/ppermute | solution.py:1086
  272.3 20.1 %collective-permute-start.34 = (bf16[256,1792]{1,0:T(8,128)(2,1)}, bf16[256,1792]{1,0:T(8,128)(2,1)}, u32[]{:S(2)}, u32[]{:S(2)}) collective-permute-start(bf16[256,1792]{1,0:T(8,128)(2,1)} %get-tuple-element.90), channel_id=1, source_target_pairs={{0,1},{1,0},{2,3},{3,2},{4,5},{5,4},{6,7},{7,6},{8,9},{9,8},{10,11... | collective-permute-start | bytes 2752520 | tf_op jit(solution)/shard_map/ppermute | solution.py:34
  328.4 22.5 %collective-permute-start.40 = (bf16[256,1792]{1,0:T(8,128)(2,1)S(1)}, bf16[256,1792]{1,0:T(8,128)(2,1)S(1)}, u32[]{:S(2)}, u32[]{:S(2)}) collective-permute-start(bf16[256,1792]{1,0:T(8,128)(2,1)S(1)} %copy-done.59), channel_id=1, source_target_pairs={{0,2},{2,0},{1,3},{3,1},{4,6},{6,4},{5,7},{7,5},{8,10},{10,8},{9,1... | collective-permute-start | bytes 2752520 | tf_op jit(solution)/shard_map/ppermute | solution.py:34
  330.0 22.1 %collective-permute-start.41 = (bf16[256,1792]{1,0:T(8,128)(2,1)S(1)}, bf16[256,1792]{1,0:T(8,128)(2,1)S(1)}, u32[]{:S(2)}, u32[]{:S(2)}) collective-permute-start(bf16[256,1792]{1,0:T(8,128)(2,1)S(1)} %copy-done.60), channel_id=1, source_target_pairs={{0,4},{4,0},{1,5},{5,1},{2,6},{6,2},{3,7},{7,3},{8,12},{12,8},{9,1... | collective-permute-start | bytes 2752520 | tf_op jit(solution)/shard_map/ppermute | solution.py:34
  344.5 25.3 %collective-permute-start.44 = (bf16[256,1792]{1,0:T(8,128)(2,1)}, bf16[256,1792]{1,0:T(8,128)(2,1)}, u32[]{:S(2)}, u32[]{:S(2)}) collective-permute-start(bf16[256,1792]{1,0:T(8,128)(2,1)} %get-tuple-element.102), channel_id=1, source_target_pairs={{0,1},{1,0},{2,3},{3,2},{4,5},{5,4},{6,7},{7,6},{8,9},{9,8},{10,11... | collective-permute-start | bytes 2752520 | tf_op jit(solution)/shard_map/ppermute | solution.py:34
  364.4 18.4 %all-to-all-start.3 = ((bf16[8,256,256]{2,1,0:T(8,128)(2,1)}), bf16[8,256,256]{2,1,0:T(8,128)(2,1)S(1)}, u32[]{:S(2)}, u32[]{:S(2)}) async-start(bf16[8,256,256]{2,1,0:T(8,128)(2,1)} %get-tuple-element.99), calls=%async_computation.3 | async-start | bytes 2097152 | tf_op jit(solution)/shard_map/all_to_all | solution.py:1107
  368.8 154.3 %reduce-scatter.3.cloned.1.call-start = ((), (), s32[]{:S(2)}) async-start(), calls=%async_computation.11 | async-start | bytes 4587520 | tf_op jit(solution)/shard_map/reduce_scatter | solution.py:1124
  368.9 37.9 %collective-permute-start.38 = (bf16[256,1792]{1,0:T(8,128)(2,1)}, bf16[256,1792]{1,0:T(8,128)(2,1)}, u32[]{:S(2)}, u32[]{:S(2)}) collective-permute-start(bf16[256,1792]{1,0:T(8,128)(2,1)} %get-tuple-element.96), channel_id=1, source_target_pairs={{0,1},{1,0},{2,3},{3,2},{4,5},{5,4},{6,7},{7,6},{8,9},{9,8},{10,11... | collective-permute-start | bytes 2752520 | tf_op jit(solution)/shard_map/ppermute | solution.py:34
  369.0 49.0 %collective-permute-start.37 = (bf16[256,1792]{1,0:T(8,128)(2,1)}, bf16[256,1792]{1,0:T(8,128)(2,1)}, u32[]{:S(2)}, u32[]{:S(2)}) collective-permute-start(bf16[256,1792]{1,0:T(8,128)(2,1)} %get-tuple-element.94), channel_id=1, source_target_pairs={{0,1},{1,0},{2,3},{3,2},{4,5},{5,4},{6,7},{7,6},{8,9},{9,8},{10,11... | collective-permute-start | bytes 2752520 | tf_op jit(solution)/shard_map/ppermute | solution.py:34
  369.4 72.8 %collective-permute-start.48 = (bf16[256,1792]{1,0:T(8,128)(2,1)S(1)}, bf16[256,1792]{1,0:T(8,128)(2,1)S(1)}, u32[]{:S(2)}, u32[]{:S(2)}) collective-permute-start(bf16[256,1792]{1,0:T(8,128)(2,1)S(1)} %get-tuple-element.105.refs_0_), channel_id=1, source_target_pairs={{0,1},{1,0},{2,3},{3,2},{4,5},{5,4},{6,7},{7,6},{8,9},{9,8},{10,11... | collective-permute-start | bytes 2752520 | tf_op jit(solution)/shard_map/ppermute | solution.py:34
  369.5 44.1 %collective-permute-start.49 = (bf16[256,1792]{1,0:T(8,128)(2,1)S(1)}, bf16[256,1792]{1,0:T(8,128)(2,1)}, u32[]{:S(2)}, u32[]{:S(2)}) collective-permute-start(bf16[256,1792]{1,0:T(8,128)(2,1)S(1)} %get-tuple-element.105.refs_0_), channel_id=1, source_target_pairs={{0,2},{2,0},{1,3},{3,1},{4,6},{6,4},{5,7},{7,5},{8,10},{10,8},{9,1... | collective-permute-start | bytes 2752520 | tf_op jit(solution)/shard_map/ppermute | solution.py:34
  369.9 45.7 %collective-permute-start.51 = (bf16[256,1792]{1,0:T(8,128)(2,1)S(1)}, bf16[256,1792]{1,0:T(8,128)(2,1)}, u32[]{:S(2)}, u32[]{:S(2)}) collective-permute-start(bf16[256,1792]{1,0:T(8,128)(2,1)S(1)} %get-tuple-element.105.refs_0_), channel_id=1, source_target_pairs={{0,4},{4,0},{1,5},{5,1},{2,6},{6,2},{3,7},{7,3},{8,12},{12,8},{9,1... | collective-permute-start | bytes 2752520 | tf_op jit(solution)/shard_map/ppermute | solution.py:34
  413.6 22.9 %collective-permute-start.45 = (bf16[128,1792]{1,0:T(8,128)(2,1)}, bf16[128,1792]{1,0:T(8,128)(2,1)}, u32[]{:S(2)}, u32[]{:S(2)}) collective-permute-start(bf16[128,1792]{1,0:T(8,128)(2,1)} %get-tuple-element.130), channel_id=1, source_target_pairs={{0,2},{2,0},{1,3},{3,1},{4,6},{6,4},{5,7},{7,5},{8,10},{10,8},{9,1... | collective-permute-start | bytes 1376264 | tf_op jit(solution)/shard_map/ppermute | solution.py:34
  417.9 18.0 %collective-permute-start.53 = (bf16[128,1792]{1,0:T(8,128)(2,1)}, bf16[128,1792]{1,0:T(8,128)(2,1)S(1)}, u32[]{:S(2)}, u32[]{:S(2)}) collective-permute-start(bf16[128,1792]{1,0:T(8,128)(2,1)} %get-tuple-element.106), channel_id=1, source_target_pairs={{0,2},{2,0},{1,3},{3,1},{4,6},{6,4},{5,7},{7,5},{8,10},{10,8},{9,1... | collective-permute-start | bytes 1376264 | tf_op jit(solution)/shard_map/ppermute | solution.py:34
  439.6 24.0 %collective-permute-start.46 = (bf16[256,1792]{1,0:T(8,128)(2,1)}, bf16[256,1792]{1,0:T(8,128)(2,1)}, u32[]{:S(2)}, u32[]{:S(2)}) collective-permute-start(bf16[256,1792]{1,0:T(8,128)(2,1)} %pad_maximum_fusion.3.refs_12_), channel_id=1, source_target_pairs={{0,4},{4,0},{1,5},{5,1},{2,6},{6,2},{3,7},{7,3},{8,12},{12,8},{9,1... | collective-permute-start | bytes 2752520 | tf_op jit(solution)/shard_map/ppermute | solution.py:34
  442.2 22.3 %collective-permute-start.43 = (bf16[256,1792]{1,0:T(8,128)(2,1)}, bf16[256,1792]{1,0:T(8,128)(2,1)}, u32[]{:S(2)}, u32[]{:S(2)}) collective-permute-start(bf16[256,1792]{1,0:T(8,128)(2,1)} %pad_maximum_fusion.2.refs_11_), channel_id=1, source_target_pairs={{0,2},{2,0},{1,3},{3,1},{4,6},{6,4},{5,7},{7,5},{8,10},{10,8},{9,1... | collective-permute-start | bytes 2752520 | tf_op jit(solution)/shard_map/ppermute | solution.py:34
  463.5 23.6 %collective-permute-start.36 = (bf16[256,1792]{1,0:T(8,128)(2,1)S(1)}, bf16[256,1792]{1,0:T(8,128)(2,1)S(1)}, u32[]{:S(2)}, u32[]{:S(2)}) collective-permute-start(bf16[256,1792]{1,0:T(8,128)(2,1)S(1)} %copy-done.62), channel_id=1, source_target_pairs={{0,1},{1,0},{2,3},{3,2},{4,5},{5,4},{6,7},{7,6},{8,9},{9,8},{10,11... | collective-permute-start | bytes 2752520 | tf_op jit(solution)/shard_map/ppermute | solution.py:34
  463.6 33.8 %collective-permute-start.56 = (bf16[256,1792]{1,0:T(8,128)(2,1)}, bf16[256,1792]{1,0:T(8,128)(2,1)}, u32[]{:S(2)}, u32[]{:S(2)}) collective-permute-start(bf16[256,1792]{1,0:T(8,128)(2,1)} %get-tuple-element.110), channel_id=1, source_target_pairs={{0,1},{1,0},{2,3},{3,2},{4,5},{5,4},{6,7},{7,6},{8,9},{9,8},{10,11... | collective-permute-start | bytes 2752520 | tf_op jit(solution)/shard_map/ppermute | solution.py:34
  480.9 23.5 %collective-permute-start.60 = (bf16[256,1792]{1,0:T(8,128)(2,1)}, bf16[256,1792]{1,0:T(8,128)(2,1)S(1)}, u32[]{:S(2)}, u32[]{:S(2)}) collective-permute-start(bf16[256,1792]{1,0:T(8,128)(2,1)} %pad_maximum_fusion.4), channel_id=1, source_target_pairs={{0,2},{2,0},{1,3},{3,1},{4,6},{6,4},{5,7},{7,5},{8,10},{10,8},{9,1... | collective-permute-start | bytes 2752520 | tf_op jit(solution)/shard_map/ppermute | solution.py:34
  485.6 29.7 %collective-permute-start.63 = (bf16[256,1792]{1,0:T(8,128)(2,1)}, bf16[256,1792]{1,0:T(8,128)(2,1)}, u32[]{:S(2)}, u32[]{:S(2)}) collective-permute-start(bf16[256,1792]{1,0:T(8,128)(2,1)} %pad_maximum_fusion.5), channel_id=1, source_target_pairs={{0,4},{4,0},{1,5},{5,1},{2,6},{6,2},{3,7},{7,3},{8,12},{12,8},{9,1... | collective-permute-start | bytes 2752520 | tf_op jit(solution)/shard_map/ppermute | solution.py:34
  492.0 27.1 %all-to-all-start.4 = ((bf16[8,5,56,256]{3,2,1,0:T(8,128)(2,1)}), bf16[8,5,56,256]{3,2,1,0:T(8,128)(2,1)S(1)}, u32[]{:S(2)}, u32[]{:S(2)}) async-start(bf16[8,5,56,256]{3,2,1,0:T(8,128)(2,1)} %bitcast.51), calls=%async_computation.6 | async-start | bytes 2293760 | tf_op jit(solution)/shard_map/all_to_all | solution.py:1128
  528.0 26.9 %all-to-all-start.5 = ((bf16[8,3,56,256]{3,2,1,0:T(8,128)(2,1)}), bf16[8,3,56,256]{3,2,1,0:T(8,128)(2,1)S(1)}, u32[]{:S(2)}, u32[]{:S(2)}) async-start(bf16[8,3,56,256]{3,2,1,0:T(8,128)(2,1)} %get-tuple-element.119), calls=%async_computation.7 | async-start | bytes 1376256 | tf_op jit(solution)/shard_map/all_to_all | solution.py:1139
  533.6 20.6 %collective-permute-start.64 = (bf16[448,256]{1,0:T(8,128)(2,1)S(1)}, bf16[448,256]{1,0:T(8,128)(2,1)S(1)}, u32[]{:S(2)}, u32[]{:S(2)}) collective-permute-start(bf16[448,256]{1,0:T(8,128)(2,1)S(1)} %get-tuple-element.124), channel_id=1, source_target_pairs={{0,0},{1,4},{2,8},{3,12},{4,16},{5,20},{6,24},{7,28},{8,1},{9,5},{... | collective-permute-start | bytes 688136 | tf_op jit(solution)/shard_map/ppermute | solution.py:1144
  (95 other events, 911.6 us)
Sparse Core Ops, SparseCore 0:
  10.2 48.1 all-gather.3
  62.1 70.7 all-gather.5
  134.4 88.4 all-gather.7
  323.4 124.0 reduce-scatter.4
  450.7 68.9 reduce-scatter.2
